TPU v7x, 512 devices: a whole 4x4x16 slice. The times are simulated.
512 devices in a mesh: ctx: 16 (over z), ch: 32 (over y, x, core).
Axes of the slice: x: 4, y: 4, z: 16, core: 2. Of those that a mesh axis runs over, the one named last changes fastest.
Arguments:
- resid_in: bfloat16 [2048, 4096], P('ctx', 'ch'), may hold values from -800 to 800
- query_in: bfloat16 [2048, 4096], P('ctx', 'ch'), may hold values from -6 to 6
- key_in: bfloat16 [2048, 4096], P('ctx', 'ch'), may hold values from -6 to 6
- value_in: bfloat16 [2048, 4096], P('ctx', 'ch'), may hold values from -6 to 6
- filt: float32 [4096, 2048], P(('ch', 'ctx')), may hold values from -4 to 4
- gain: float32 [4096], P('ch'), may hold values from 0.5 to 1.5
- w_gate: bfloat16 [4096, 11008], P('ctx', 'ch'), may hold values from -0.09375 to 0.09375
- w_up: bfloat16 [4096, 11008], P('ctx', 'ch'), may hold values from -0.09375 to 0.09375
- g_hid: bfloat16 [2048, 11008], P('ctx', 'ch'), may hold values from -6 to 6
- g_res: bfloat16 [2048, 4096], P('ctx', 'ch'), may hold values from -1.5 to 1.5
Outputs:
- dx: bfloat16 [2048, 4096], P('ctx', 'ch')
- dq: bfloat16 [2048, 4096], P('ctx', 'ch')
- dk: bfloat16 [2048, 4096], P('ctx', 'ch')
- dv: bfloat16 [2048, 4096], P('ctx', 'ch')
- dfilt: float32 [4096, 2048], P(('ch', 'ctx'))
- dgain: float32 [4096], P('ch')
- dw_gate: float32 [4096, 11008], P('ctx', 'ch')
- dw_up: float32 [4096, 11008], P('ctx', 'ch')
- amax: float32 [], replicated
All inputs are finite; a program needn't handle non-finite values.
Results may differ from a plain program's by a relative error of at most 0.025.
Values may be sent and summed in bfloat16 or wider, within the bound.
No kernel may reach another device: no remote copies, remote signals or barrier semaphores. Data moves between devices by JAX's collectives and lax.ppermute only.
A program may use at most 64 MiB of HBM per device.

v0:
```python
import math

import jax
import jax.numpy as jnp
from jax import lax
from jax.sharding import PartitionSpec as P

epsilon = 1e-06
highest = lax.Precision.HIGHEST


def split_sizes(total):
    size_p = math.gcd(total, 2 ** (total.bit_length() // 2))
    return (size_p, total // size_p)


def dft_tables(size_p, size_q):
    total = size_p * size_q
    rows_p = jnp.arange(size_p, dtype=jnp.int32)
    rows_q = jnp.arange(size_q, dtype=jnp.int32)
    angle_p = (rows_p[:, None] * rows_p[None, :] % size_p).astype(jnp.float32) * (
        2.0 * math.pi / size_p
    )
    angle_q = (rows_q[:, None] * rows_q[None, :] % size_q).astype(jnp.float32) * (
        2.0 * math.pi / size_q
    )
    angle_t = (rows_p[:, None] * rows_q[None, :] % total).astype(jnp.float32) * (
        2.0 * math.pi / total
    )
    return (
        jnp.cos(angle_p),
        jnp.sin(angle_p),
        jnp.cos(angle_q),
        jnp.sin(angle_q),
        jnp.cos(angle_t),
        jnp.sin(angle_t),
    )


def left_mult(table, block):
    return jnp.einsum("kp,cpq->ckq", table, block, precision=highest)


def right_mult(block, table):
    return jnp.einsum("ckq,qm->ckm", block, table, precision=highest)


def forward_dft(signal, tables):
    cos_p, sin_p, cos_q, sin_q, cos_t, sin_t = tables
    chans = signal.shape[0]
    block = signal.reshape(chans, cos_p.shape[0], cos_q.shape[0])
    first_re = left_mult(cos_p, block)
    first_im = -left_mult(sin_p, block)
    turn_re = first_re * cos_t + first_im * sin_t
    turn_im = first_im * cos_t - first_re * sin_t
    out_re = right_mult(turn_re, cos_q) + right_mult(turn_im, sin_q)
    out_im = right_mult(turn_im, cos_q) - right_mult(turn_re, sin_q)
    return (out_re, out_im)


def inverse_dft(spec_re, spec_im, tables):
    cos_p, sin_p, cos_q, sin_q, cos_t, sin_t = tables
    chans = spec_re.shape[0]
    total = cos_p.shape[0] * cos_q.shape[0]
    mid_re = right_mult(spec_re, cos_q) - right_mult(spec_im, sin_q)
    mid_im = right_mult(spec_re, sin_q) + right_mult(spec_im, cos_q)
    turn_re = mid_re * cos_t - mid_im * sin_t
    turn_im = mid_re * sin_t + mid_im * cos_t
    signal = left_mult(cos_p, turn_re) - left_mult(sin_p, turn_im)
    return signal.reshape(chans, total) / total


def spectral_product(left_re, left_im, right_re, right_im, conjugate):
    if conjugate:
        return (left_re * right_re + left_im * right_im, left_im * right_re - left_re * right_im)
    return (left_re * right_re - left_im * right_im, left_re * right_im + left_im * right_re)


def padded(signal, length):
    return jnp.concatenate([signal, jnp.zeros((signal.shape[0], length), jnp.float32)], axis=1)


def on_device(resid_in, query_in, key_in, value_in, filt, gain, w_gate, w_up, g_hid, g_res):
    tokens, chans = resid_in.shape
    length = tokens * lax.axis_size("ctx")
    width = chans * lax.axis_size("ch")
    size_p, size_q = split_sizes(2 * length)
    tables = dft_tables(size_p, size_q)
    query_f = query_in.astype(jnp.float32)
    keys_f = key_in.astype(jnp.float32)
    values_f = value_in.astype(jnp.float32)
    mixed = (keys_f * values_f).astype(jnp.bfloat16)
    spread = lax.all_to_all(mixed.T, "ctx", split_axis=0, concat_axis=1, tiled=True)
    src_re, src_im = forward_dft(padded(spread.astype(jnp.float32), length), tables)
    filt_re, filt_im = forward_dft(padded(filt, length), tables)
    conv_re, conv_im = spectral_product(src_re, src_im, filt_re, filt_im, False)
    conv_full = inverse_dft(conv_re, conv_im, tables)[:, :length].astype(jnp.bfloat16)
    conv_f = lax.all_to_all(conv_full, "ctx", split_axis=1, concat_axis=0, tiled=True).T.astype(
        jnp.float32
    )
    resid = resid_in.astype(jnp.float32) + query_f * conv_f
    scaled_res = resid * gain[None, :]
    sq_local = jnp.sum(resid * resid, axis=1)
    total_sq = lax.psum(sq_local, "ch")
    inv_rms = lax.rsqrt(total_sq / width + epsilon)
    normed = scaled_res * inv_rms[:, None]
    amax = lax.pmax(jnp.max(jnp.abs(normed)), ("ctx", "ch"))
    acts = normed.astype(jnp.bfloat16)
    acts_full = lax.all_gather(acts, "ch", axis=1, tiled=True)
    row_acts = lax.all_to_all(acts_full, "ctx", split_axis=1, concat_axis=0, tiled=True)
    contract = (((1,), (1,)), ((), ()))
    lead = (((0,), (0,)), ((), ()))
    gate_rows, up_rows = (
        lax.all_gather(w_gate, "ctx", axis=0, tiled=True),
        lax.all_gather(w_up, "ctx", axis=0, tiled=True),
    )
    gate = jnp.dot(acts_full, gate_rows, preferred_element_type=jnp.float32)
    up = jnp.dot(acts_full, up_rows, preferred_element_type=jnp.float32)
    sigma = jax.nn.sigmoid(gate)
    hid_grad = g_hid.astype(jnp.float32)
    d_gate = (hid_grad * up * sigma * (1.0 + gate * (1.0 - sigma))).astype(jnp.bfloat16)
    d_up = (hid_grad * gate * sigma).astype(jnp.bfloat16)
    term = lax.dot_general(gate_rows, d_gate, contract, preferred_element_type=jnp.float32)
    term = term + lax.dot_general(up_rows, d_up, contract, preferred_element_type=jnp.float32)
    rounded = lax.optimization_barrier(term.astype(jnp.bfloat16))
    d_norm = (
        lax.psum_scatter(
            rounded.astype(jnp.float32).astype(jnp.bfloat16), "ch", scatter_dimension=0, tiled=True
        )
        .astype(jnp.float32)
        .T
    )
    first = lax.dot_general(
        row_acts,
        lax.all_gather(d_gate, "ctx", axis=0, tiled=True),
        lead,
        preferred_element_type=jnp.float32,
    )
    second = lax.dot_general(
        row_acts,
        lax.all_gather(d_up, "ctx", axis=0, tiled=True),
        lead,
        preferred_element_type=jnp.float32,
    )
    scaled_grad = gain[None, :] * d_norm
    inner = lax.psum(jnp.sum(scaled_grad * resid, axis=1), "ch")
    gain_grad = lax.psum(jnp.sum(d_norm * resid * inv_rms[:, None], axis=0), "ctx")
    d_resid = (
        g_res.astype(jnp.float32)
        + scaled_grad * inv_rms[:, None]
        - resid * (inv_rms**3 * inner / width)[:, None]
    )
    d_conv = (d_resid * query_f).astype(jnp.bfloat16)
    d_query = (d_resid * conv_f).astype(jnp.bfloat16)
    back_spread = lax.all_to_all(d_conv.T, "ctx", split_axis=0, concat_axis=1, tiled=True)
    grad_re, grad_im = forward_dft(padded(back_spread.astype(jnp.float32), length), tables)
    srcg_re, srcg_im = spectral_product(grad_re, grad_im, filt_re, filt_im, True)
    src_grad = inverse_dft(srcg_re, srcg_im, tables)[:, :length].astype(jnp.bfloat16)
    fltg_re, fltg_im = spectral_product(grad_re, grad_im, src_re, src_im, True)
    filt_grad = inverse_dft(fltg_re, fltg_im, tables)[:, :length]
    src_tok = lax.all_to_all(src_grad, "ctx", split_axis=1, concat_axis=0, tiled=True).T.astype(
        jnp.float32
    )
    d_keys = (src_tok * values_f).astype(jnp.bfloat16)
    d_values = (src_tok * keys_f).astype(jnp.bfloat16)
    return (
        d_resid.astype(jnp.bfloat16),
        d_query,
        d_keys,
        d_values,
        filt_grad,
        gain_grad,
        first,
        second,
        amax,
    )


def solution(mesh):
    return jax.shard_map(
        on_device,
        mesh=mesh,
        in_specs=(
            P("ctx", "ch"),
            P("ctx", "ch"),
            P("ctx", "ch"),
            P("ctx", "ch"),
            P(("ch", "ctx"), None),
            P("ch"),
            P("ctx", "ch"),
            P("ctx", "ch"),
            P("ctx", "ch"),
            P("ctx", "ch"),
        ),
        out_specs=(
            P("ctx", "ch"),
            P("ctx", "ch"),
            P("ctx", "ch"),
            P("ctx", "ch"),
            P(("ch", "ctx"), None),
            P("ch"),
            P("ctx", "ch"),
            P("ctx", "ch"),
            P(),
        ),
        check_vma=False,
    )
```

profile of v0, /device:TPU:1, one launch (start us, length us, event | category | flops | bytes accessed | tf_op | source)
XLA Modules:
  0.0 734.3 jit_solution(6751559115110520331)
XLA Ops:
  9.6 15.7 %all-to-all-start = ((bf16[16,8,128]{2,1,0:T(8,128)(2,1)}), bf16[16,8,128]{2,1,0:T(8,128)(2,1)S(1)}, u32[]{:S(2)}, u32[]{:S(2)}) async-start(bf16[16,8,128]{2,1,0:T(8,128)(2,1)} %fusion.75), calls=%async_computation | async-start | bytes 65536 | tf_op jit(solution)/shard_map/all_to_all | solution.py:93
  30.7 6.1 all-to-all-done
  39.9 1.4 multiply_add_fusion.3
  43.3 1.0 convolution_subtract_fusion.6
  44.4 1.0 convolution_add_fusion.4
  47.3 5.4 all-to-all-start.1
  53.1 11.2 %all-to-all-done.1 = bf16[8,16,128]{2,0,1:T(8,128)(2,1)S(1)} async-done(((bf16[8,16,128]{2,0,1:T(8,128)(2,1)}), bf16[8,16,128]{2,0,1:T(8,128)(2,1)S(1)}, u32[]{:S(2)}, u32[]{:S(2)}) %all-to-all-start.1) | async-done | bytes 32800 | tf_op jit(solution)/shard_map/all_to_all | solution.py:98
  64.3 65.1 %psum.21 = f32[128]{0:T(128)S(1)} all-reduce(f32[128]{0:T(128)S(1)} %get-tuple-element.32), channel_id=1, replica_groups=mesh['ctx'=16,'ch'=32] {'ch'}, use_global_device_ids=true, to_apply=%region_1.2 | all-reduce | flops 128 | bytes 1024 | tf_op jit(solution)/shard_map/psum | solution.py:104
  131.7 46.4 %all-gather.6.cloned.1.call-done = bf16[128,4096]{0,1:T(8,128)(2,1)} async-done(((bf16[128,128]{0,1:T(8,128)(2,1)}), bf16[128,4096]{0,1:T(8,128)(2,1)}) %all-gather.6.cloned.1.call-update) | async-done | bytes 1048592 | tf_op jit(solution)/shard_map/all_gather | solution.py:109
  178.1 76.3 %all-gather.10.cloned.1.call-done = bf16[4096,344]{0,1:T(8,128)(2,1)} async-done(((bf16[256,344]{0,1:T(8,128)(2,1)}), bf16[4096,344]{0,1:T(8,128)(2,1)}) %all-gather.10.cloned.1.call-update) | async-done | bytes 2818064 | tf_op jit(solution)/shard_map/all_gather | solution.py:114
  254.4 3.7 fusion.38
  258.1 78.1 %all-gather.8.cloned.1.call-done = bf16[4096,344]{0,1:T(8,128)(2,1)} async-done(((bf16[256,344]{0,1:T(8,128)(2,1)}), bf16[4096,344]{0,1:T(8,128)(2,1)}) %all-gather.8.cloned.1.call-update) | async-done | bytes 2818064 | tf_op jit(solution)/shard_map/all_gather | solution.py:115
  336.2 2.7 fusion.13
  338.9 2.6 fusion.314
  341.5 2.7 fusion.1
  344.2 1.3 copy.167
  345.7 103.4 %reduce-scatter.4.cloned.1.call-done = bf16[128,128]{1,0:T(8,128)(2,1)} async-done(((bf16[4096,128]{1,0:T(8,128)(2,1)}), bf16[128,128]{1,0:T(8,128)(2,1)}) %reduce-scatter.4.cloned.1.call-update) | async-done | bytes 32784 | tf_op jit(solution)/shard_map/reduce_scatter | solution.py:127
  449.1 1.5 fusion.63
  450.6 64.3 %psum.22 = f32[128]{0:T(128)S(1)} all-reduce(f32[128]{0:T(128)S(1)} %get-tuple-element.28), channel_id=1, replica_groups=mesh['ctx'=16,'ch'=32] {'ch'}, use_global_device_ids=true, to_apply=%region_4.5 | all-reduce | flops 128 | bytes 1024 | tf_op jit(solution)/shard_map/psum | solution.py:146
  514.9 1.5 fusion.76
  516.4 12.0 %all-to-all-start.2 = ((bf16[16,8,128]{2,1,0:T(8,128)(2,1)}), bf16[16,8,128]{2,1,0:T(8,128)(2,1)S(1)}, u32[]{:S(2)}, u32[]{:S(2)}) async-start(bf16[16,8,128]{2,1,0:T(8,128)(2,1)} %get-tuple-element.30), calls=%async_computation.2 | async-start | bytes 65536 | tf_op jit(solution)/shard_map/all_to_all | solution.py:155
  529.0 11.0 %all-to-all-done.2 = bf16[16,8,128]{2,1,0:T(8,128)(2,1)S(1)} async-done(((bf16[16,8,128]{2,1,0:T(8,128)(2,1)}), bf16[16,8,128]{2,1,0:T(8,128)(2,1)S(1)}, u32[]{:S(2)}, u32[]{:S(2)}) %all-to-all-start.2) | async-done | bytes 32800 | tf_op jit(solution)/shard_map/all_to_all | solution.py:155
  545.8 1.0 convolution_subtract_fusion.3
  549.8 3.5 all-to-all-start.3
  553.3 1.3 copy.132
  554.6 10.4 %all-to-all-done.3 = bf16[8,16,128]{2,0,1:T(8,128)(2,1)S(1)} async-done(((bf16[8,16,128]{2,0,1:T(8,128)(2,1)}), bf16[8,16,128]{2,0,1:T(8,128)(2,1)S(1)}, u32[]{:S(2)}, u32[]{:S(2)}) %all-to-all-start.3) | async-done | bytes 32800 | tf_op jit(solution)/shard_map/all_to_all | solution.py:161
  565.0 3.7 all-to-all-start.4
  569.3 123.0 %pmax.7 = f32[]{:T(128)} all-reduce(f32[]{:T(128)} %get-tuple-element.29), channel_id=1, replica_groups=mesh['ctx'=16,'ch'=32] {'ctx','ch'}, use_global_device_ids=true, to_apply=%region_8.9 | all-reduce | flops 1 | bytes 8 | tf_op jit(solution)/shard_map/pmax | solution.py:107
  693.7 21.0 %psum.23 = f32[128]{0:T(128)} all-reduce(f32[128]{0:T(128)S(1)} %get-tuple-element.27), channel_id=1, replica_groups=mesh['ctx'=16,'ch'=32] {'ctx'}, use_global_device_ids=true, to_apply=%region_6.7 | all-reduce | flops 128 | bytes 1024 | tf_op jit(solution)/shard_map/psum | solution.py:147
  716.7 1.0 convolution_subtract_fusion.1
  722.2 2.6 fusion.315
  724.8 2.6 fusion.316
  (123 shorter events, 35.1 us)
Async XLA Ops:
  8.0 17.4 %copy-start.8 = (bf16[128,128]{0,1:T(8,128)(2,1)}, bf16[128,128]{0,1:T(8,128)(2,1)S(1)}, u32[]{:S(2)}) copy-start(bf16[128,128]{0,1:T(8,128)(2,1)S(1)} %copy.92) | copy-start | bytes 98308
  8.9 16.6 %copy-start.10 = (bf16[128,128]{0,1:T(8,128)(2,1)}, bf16[128,128]{0,1:T(8,128)(2,1)S(1)}, u32[]{:S(2)}) copy-start(bf16[128,128]{0,1:T(8,128)(2,1)S(1)} %copy.93) | copy-start | bytes 98308
  9.6 27.2 %all-to-all-start = ((bf16[16,8,128]{2,1,0:T(8,128)(2,1)}), bf16[16,8,128]{2,1,0:T(8,128)(2,1)S(1)}, u32[]{:S(2)}, u32[]{:S(2)}) async-start(bf16[16,8,128]{2,1,0:T(8,128)(2,1)} %fusion.75), calls=%async_computation | async-start | bytes 65536 | tf_op jit(solution)/shard_map/all_to_all | solution.py:93
  30.7 10.5 %copy-start = (f32[8,64,64]{2,1,0:T(8,128)}, f32[8,64,64]{2,1,0:T(8,128)S(1)}, u32[]{:S(2)}) copy-start(f32[8,64,64]{2,1,0:T(8,128)S(1)} %convolution_add_fusion.5) | copy-start | bytes 393220
  39.9 6.0 copy-start.2
  41.3 11.5 %copy-start.16 = (bf16[128,128]{1,0:T(8,128)(2,1)S(1)}, bf16[128,128]{1,0:T(8,128)(2,1)}, u32[]{:S(2)}) copy-start(bf16[128,128]{1,0:T(8,128)(2,1)} %param.11) | copy-start | bytes 98308
  41.3 11.7 %copy-start.17 = (bf16[128,128]{1,0:T(8,128)(2,1)S(1)}, bf16[128,128]{1,0:T(8,128)(2,1)}, u32[]{:S(2)}) copy-start(bf16[128,128]{1,0:T(8,128)(2,1)} %param.10) | copy-start | bytes 98308
  41.3 88.1 %copy-start.19 = (f32[128]{0:T(128)S(1)}, f32[128]{0:T(128)}, u32[]{:S(2)}) copy-start(f32[128]{0:T(128)} %param.15) | copy-start | bytes 1540
  41.3 213.1 %copy-start.20 = (bf16[128,344]{0,1:T(8,128)(2,1)S(1)}, bf16[128,344]{0,1:T(8,128)(2,1)}, u32[]{:S(2)}) copy-start(bf16[128,344]{0,1:T(8,128)(2,1)} %param.18) | copy-start | bytes 264196
  47.3 16.9 %all-to-all-start.1 = ((bf16[8,16,128]{2,0,1:T(8,128)(2,1)}), bf16[8,16,128]{2,0,1:T(8,128)(2,1)S(1)}, u32[]{:S(2)}, u32[]{:S(2)}) async-start(bf16[8,16,128]{2,0,1:T(8,128)(2,1)} %slice_bitcast_fusion.1), calls=%async_computation.1 | async-start | bytes 65536 | tf_op jit(solution)/shard_map/all_to_all | solution.py:98
  52.8 125.3 %all-gather.6.cloned.1.call-start = ((), (), s32[]{:S(2)}) async-start(), calls=%async_computation.6 | async-start | bytes 1081344 | tf_op jit(solution)/shard_map/all_gather | solution.py:109
  52.9 78.8 %copy-start.14 = (bf16[128,128]{0,1:T(8,128)(2,1)}, bf16[128,128]{0,1:T(8,128)(2,1)S(1)}, u32[]{:S(2)}) copy-start(bf16[128,128]{0,1:T(8,128)(2,1)S(1)} %copy.91) | copy-start | bytes 98308
  64.2 67.5 %copy-start.12 = (bf16[8,16,128]{2,0,1:T(8,128)(2,1)}, bf16[8,16,128]{2,0,1:T(8,128)(2,1)S(1)}, u32[]{:S(2)}) copy-start(bf16[8,16,128]{2,0,1:T(8,128)(2,1)S(1)} %all-to-all-done.1) | copy-start | bytes 98308
  130.2 124.2 %all-gather.10.cloned.1.call-start = ((), (), s32[]{:S(2)}) async-start(), calls=%async_computation.8 | async-start | bytes 2994176 | tf_op jit(solution)/shard_map/all_gather | solution.py:114
  130.9 205.3 %all-gather.8.cloned.1.call-start = ((), (), s32[]{:S(2)}) async-start(), calls=%async_computation.7 | async-start | bytes 2994176 | tf_op jit(solution)/shard_map/all_gather | solution.py:115
  131.6 317.4 %reduce-scatter.4.cloned.1.call-start = ((), (), s32[]{:S(2)}) async-start(), calls=%async_computation.11 | async-start | bytes 1081344 | tf_op jit(solution)/shard_map/reduce_scatter | solution.py:127
  178.1 158.1 %copy-start.5 = (bf16[128,4096]{0,1:T(8,128)(2,1)S(1)}, bf16[128,4096]{0,1:T(8,128)(2,1)}, u32[]{:S(2)}) copy-start(bf16[128,4096]{0,1:T(8,128)(2,1)} %all-gather.6.cloned.1.call-done) | copy-start | bytes 3145732
  338.9 2.6 copy-start.7
  344.2 1.4 copy-start.18
  344.2 170.7 %copy-start.15 = (bf16[128,128]{0,1:T(8,128)(2,1)S(1)}, bf16[128,128]{0,1:T(8,128)(2,1)}, u32[]{:S(2)}) copy-start(bf16[128,128]{0,1:T(8,128)(2,1)} %copy-done.14) | copy-start | bytes 98308
  345.5 197.5 %copy-start.1 = (f32[8,64,64]{2,1,0:T(8,128)S(1)}, f32[8,64,64]{2,1,0:T(8,128)}, u32[]{:S(2)}) copy-start(f32[8,64,64]{2,1,0:T(8,128)} %copy-done) | copy-start | bytes 393220
  345.5 197.5 %copy-start.3 = (f32[8,64,64]{2,1,0:T(8,128)S(1)}, f32[8,64,64]{2,1,0:T(8,128)}, u32[]{:S(2)}) copy-start(f32[8,64,64]{2,1,0:T(8,128)} %copy-done.2) | copy-start | bytes 393220
  345.5 197.5 %copy-start.4 = (f32[8,64,64]{2,1,0:T(8,128)S(1)}, f32[8,64,64]{2,1,0:T(8,128)}, u32[]{:S(2)}) copy-start(f32[8,64,64]{2,1,0:T(8,128)} %get-tuple-element.46) | copy-start | bytes 393220
  516.4 23.6 %all-to-all-start.2 = ((bf16[16,8,128]{2,1,0:T(8,128)(2,1)}), bf16[16,8,128]{2,1,0:T(8,128)(2,1)S(1)}, u32[]{:S(2)}, u32[]{:S(2)}) async-start(bf16[16,8,128]{2,1,0:T(8,128)(2,1)} %get-tuple-element.30), calls=%async_computation.2 | async-start | bytes 65536 | tf_op jit(solution)/shard_map/all_to_all | solution.py:155
  528.4 193.8 %all-gather.12.cloned.1.call-start = ((), (), s32[]{:S(2)}) async-start(), calls=%async_computation.9 | async-start | bytes 1497088 | tf_op jit(solution)/shard_map/all_gather | solution.py:135
  543.7 9.6 %copy-start.6 = (bf16[128,4096]{0,1:T(8,128)(2,1)S(1)}, bf16[128,4096]{0,1:T(8,128)(2,1)}, u32[]{:S(2)}) copy-start(bf16[128,4096]{0,1:T(8,128)(2,1)} %all-gather.6.cloned.1.call-done) | copy-start | bytes 3145732
  548.3 143.9 %copy-start.13 = (bf16[8,16,128]{2,0,1:T(8,128)(2,1)S(1)}, bf16[8,16,128]{2,0,1:T(8,128)(2,1)}, u32[]{:S(2)}) copy-start(bf16[8,16,128]{2,0,1:T(8,128)(2,1)} %copy-done.12) | copy-start | bytes 98308
  549.8 15.2 %all-to-all-start.3 = ((bf16[8,16,128]{2,0,1:T(8,128)(2,1)}), bf16[8,16,128]{2,0,1:T(8,128)(2,1)S(1)}, u32[]{:S(2)}, u32[]{:S(2)}) async-start(bf16[8,16,128]{2,0,1:T(8,128)(2,1)} %slice_bitcast_fusion), calls=%async_computation.3 | async-start | bytes 65536 | tf_op jit(solution)/shard_map/all_to_all | solution.py:161
  565.0 157.2 %all-to-all-start.4 = ((bf16[128,16,256]{2,0,1:T(8,128)(2,1)}), bf16[128,16,256]{2,0,1:T(8,128)(2,1)S(1)}, u32[]{:S(2)}, u32[]{:S(2)}) async-start(bf16[128,16,256]{2,0,1:T(8,128)(2,1)} %copy.132), calls=%async_computation.4 | async-start | bytes 2097152 | tf_op jit(solution)/shard_map/all_to_all | solution.py:110
  568.7 156.1 %all-gather.14.cloned.1.call-start = ((), (), s32[]{:S(2)}) async-start(), calls=%async_computation.10 | async-start | bytes 1497088 | tf_op jit(solution)/shard_map/all_gather | solution.py:141
  714.7 6.0 copy-start.9
  714.7 6.0 copy-start.11
Sparse Core Ops, SparseCore 0:
  130.3 47.7 all-gather.5
  180.1 74.2 all-gather.9
  256.4 79.7 all-gather.7
  345.7 103.3 reduce-scatter.3
  531.1 96.8 all-gather.11
  630.1 66.3 all-gather.13
where the time goes:
time: 741 us; the launch traced here: 734 us
  waiting for transfers between devices  345 us (47%)
  blocking collectives  273 us (37%)
  matrix products  43.8 us (6%)
  starting transfers between devices  40.8 us (6%)
  between operations  14.7 us (2%)
  local copies, waits for them, and re-layouts  11.9 us (2%)
    pmax x1, blocking collectives, on_device(): amax = lax.pmax(jnp.max(jnp.abs(normed)), ('ctx', 'ch'))  123 us
    reduce_scatter x1, waiting for transfers between devices, on_device(): lax.psum_scatter(rounded.astype(jnp.float32).astype(jnp.bfloat16), 'ch',...  103 us
    all_gather x1, waiting for transfers between devices, on_device(): lax.all_gather(w_up, 'ctx', axis=0, tiled=True)  78.1 us
    all_gather x1, waiting for transfers between devices, on_device(): lax.all_gather(w_gate, 'ctx', axis=0, tiled=True)  76.3 us
    psum x1, blocking collectives, on_device(): total_sq = lax.psum(sq_local, 'ch')  65.1 us
    psum x1, blocking collectives, on_device(): inner = lax.psum(jnp.sum(scaled_grad * resid, axis=1), 'ch')  64.3 us
    all_gather x1, waiting for transfers between devices, on_device(): acts_full = lax.all_gather(acts, 'ch', axis=1, tiled=True)  46.4 us
    dot_general x24, matrix products, right_mult(): return jnp.einsum('ckq,qm->ckm', block, table, precision=highest)  21 us
  transfers between devices with their start and end apart: 11, of which 8 were waited for; matrix products, arithmetic and copies ran while one was open for 4% of the time, Pallas kernels for 0%

commit v1 on v0

--- a/solution.py
+++ b/solution.py
@@ -80,98 +80,145 @@
     return jnp.concatenate([signal, jnp.zeros((signal.shape[0], length), jnp.float32)], axis=1)
 
 
+def gather_ch(block):
+    copies = lax.axis_size("ch")
+    spread = jnp.broadcast_to(block[None], (copies,) + block.shape)
+    return lax.all_to_all(spread, "ch", split_axis=0, concat_axis=0, tiled=True)
+
+
+def split_rows(row):
+    high = lax.reduce_precision(row, 8, 7)
+    rest = row - high
+    mid = lax.reduce_precision(rest, 8, 7)
+    low = rest - mid
+    return jnp.stack([high, mid, low]).astype(jnp.bfloat16)
+
+
+def join_rows(rows):
+    rows = rows.astype(jnp.float32)
+    return rows[..., 0, :] + rows[..., 1, :] + rows[..., 2, :]
+
+
 def on_device(resid_in, query_in, key_in, value_in, filt, gain, w_gate, w_up, g_hid, g_res):
     tokens, chans = resid_in.shape
-    length = tokens * lax.axis_size("ctx")
-    width = chans * lax.axis_size("ch")
+    n_ctx = lax.axis_size("ctx")
+    n_ch = lax.axis_size("ch")
+    length = tokens * n_ctx
+    width = chans * n_ch
+    rows, hidden = w_gate.shape
+    lanes = -(-hidden // 128) * 128
+    my_ch = lax.axis_index("ch")
     size_p, size_q = split_sizes(2 * length)
     tables = dft_tables(size_p, size_q)
-    query_f = query_in.astype(jnp.float32)
-    keys_f = key_in.astype(jnp.float32)
-    values_f = value_in.astype(jnp.float32)
+
+    def widen(block):
+        return jnp.pad(block, ((0, 0), (0, lanes - hidden)))
+
+    w_all = lax.all_gather(
+        jnp.concatenate([widen(w_gate), widen(w_up)], axis=1), "ctx", axis=0, tiled=True
+    )
+    query_f = query_in.T.astype(jnp.float32)
+    keys_f = key_in.T.astype(jnp.float32)
+    values_f = value_in.T.astype(jnp.float32)
     mixed = (keys_f * values_f).astype(jnp.bfloat16)
-    spread = lax.all_to_all(mixed.T, "ctx", split_axis=0, concat_axis=1, tiled=True)
+    spread = lax.all_to_all(mixed, "ctx", split_axis=0, concat_axis=1, tiled=True)
     src_re, src_im = forward_dft(padded(spread.astype(jnp.float32), length), tables)
     filt_re, filt_im = forward_dft(padded(filt, length), tables)
     conv_re, conv_im = spectral_product(src_re, src_im, filt_re, filt_im, False)
     conv_full = inverse_dft(conv_re, conv_im, tables)[:, :length].astype(jnp.bfloat16)
-    conv_f = lax.all_to_all(conv_full, "ctx", split_axis=1, concat_axis=0, tiled=True).T.astype(
+    conv_f = lax.all_to_all(conv_full, "ctx", split_axis=1, concat_axis=0, tiled=True).astype(
         jnp.float32
     )
-    resid = resid_in.astype(jnp.float32) + query_f * conv_f
-    scaled_res = resid * gain[None, :]
-    sq_local = jnp.sum(resid * resid, axis=1)
-    total_sq = lax.psum(sq_local, "ch")
-    inv_rms = lax.rsqrt(total_sq / width + epsilon)
-    normed = scaled_res * inv_rms[:, None]
-    amax = lax.pmax(jnp.max(jnp.abs(normed)), ("ctx", "ch"))
-    acts = normed.astype(jnp.bfloat16)
-    acts_full = lax.all_gather(acts, "ch", axis=1, tiled=True)
-    row_acts = lax.all_to_all(acts_full, "ctx", split_axis=1, concat_axis=0, tiled=True)
-    contract = (((1,), (1,)), ((), ()))
-    lead = (((0,), (0,)), ((), ()))
-    gate_rows, up_rows = (
-        lax.all_gather(w_gate, "ctx", axis=0, tiled=True),
-        lax.all_gather(w_up, "ctx", axis=0, tiled=True),
-    )
-    gate = jnp.dot(acts_full, gate_rows, preferred_element_type=jnp.float32)
-    up = jnp.dot(acts_full, up_rows, preferred_element_type=jnp.float32)
+    resid = resid_in.T.astype(jnp.float32) + query_f * conv_f
+    scaled_res = resid * gain[:, None]
+    payload = jnp.concatenate(
+        [
+            scaled_res.astype(jnp.bfloat16),
+            split_rows(jnp.sum(resid * resid, axis=0)),
+            jnp.zeros((5, tokens), jnp.bfloat16),
+        ]
+    )
+    met = gather_ch(payload)
+    acts = met[:, :chans].reshape(width, tokens)
+    inv_rms = lax.rsqrt(jnp.sum(join_rows(met[:, chans : chans + 3]), axis=0) / width + epsilon)
+    inv_col = inv_rms[:, None]
+    amax = jnp.max(jnp.abs(scaled_res * inv_rms[None, :]))
+
+    piece = lax.dynamic_slice_in_dim(acts.reshape(n_ctx, rows, tokens), my_ch * (rows // n_ch), rows // n_ch, 1)
+    piece = lax.all_to_all(piece, "ctx", split_axis=0, concat_axis=0, tiled=True)
+    piece = piece.transpose(1, 0, 2).reshape(rows // n_ch, length)
+    row_acts = gather_ch(piece).reshape(rows, length)
+
+    both = lax.dot_general(
+        acts, w_all, (((0,), (0,)), ((), ())), preferred_element_type=jnp.float32
+    )
+    both = both * inv_col
+    gate = both[:, :lanes]
+    up = both[:, lanes:]
     sigma = jax.nn.sigmoid(gate)
-    hid_grad = g_hid.astype(jnp.float32)
-    d_gate = (hid_grad * up * sigma * (1.0 + gate * (1.0 - sigma))).astype(jnp.bfloat16)
-    d_up = (hid_grad * gate * sigma).astype(jnp.bfloat16)
-    term = lax.dot_general(gate_rows, d_gate, contract, preferred_element_type=jnp.float32)
-    term = term + lax.dot_general(up_rows, d_up, contract, preferred_element_type=jnp.float32)
-    rounded = lax.optimization_barrier(term.astype(jnp.bfloat16))
-    d_norm = (
-        lax.psum_scatter(
-            rounded.astype(jnp.float32).astype(jnp.bfloat16), "ch", scatter_dimension=0, tiled=True
-        )
-        .astype(jnp.float32)
-        .T
-    )
-    first = lax.dot_general(
-        row_acts,
-        lax.all_gather(d_gate, "ctx", axis=0, tiled=True),
-        lead,
-        preferred_element_type=jnp.float32,
-    )
-    second = lax.dot_general(
-        row_acts,
-        lax.all_gather(d_up, "ctx", axis=0, tiled=True),
-        lead,
-        preferred_element_type=jnp.float32,
-    )
-    scaled_grad = gain[None, :] * d_norm
-    inner = lax.psum(jnp.sum(scaled_grad * resid, axis=1), "ch")
-    gain_grad = lax.psum(jnp.sum(d_norm * resid * inv_rms[:, None], axis=0), "ctx")
+    hid_grad = widen(g_hid).astype(jnp.float32)
+    d_gate = hid_grad * up * sigma * (1.0 + gate * (1.0 - sigma))
+    d_up = hid_grad * gate * sigma
+    d_both = jnp.concatenate([d_gate, d_up], axis=1)
+    inner_part = jnp.sum(d_both * both, axis=1)
+    d_hid = d_both.astype(jnp.bfloat16)
+    d_all = lax.all_gather((d_both * inv_col).astype(jnp.bfloat16), "ctx", axis=0, tiled=True)
+    term = lax.dot_general(
+        w_all, d_hid, (((1,), (1,)), ((), ())), preferred_element_type=jnp.float32
+    )
+    term = term.astype(jnp.bfloat16).reshape(n_ch, chans, tokens)
+    extra = jnp.concatenate(
+        [
+            split_rows(inner_part),
+            split_rows(jnp.full((tokens,), amax, jnp.float32)),
+            jnp.zeros((2, tokens), jnp.bfloat16),
+        ]
+    )
+    sent = jnp.concatenate([term, jnp.broadcast_to(extra[None], (n_ch, 8, tokens))], axis=1)
+    back = lax.all_to_all(sent, "ch", split_axis=0, concat_axis=0, tiled=True)
+    d_norm = jnp.sum(back[:, :chans].astype(jnp.float32), axis=0)
+    inner = jnp.sum(join_rows(back[:, chans : chans + 3]), axis=0)
+    amax = jnp.max(join_rows(back[:, chans + 3 : chans + 6]), axis=0)
+
+    scaled_grad = gain[:, None] * d_norm
+    gain_part = jnp.sum(d_norm * resid * inv_rms[None, :], axis=1)
     d_resid = (
-        g_res.astype(jnp.float32)
-        + scaled_grad * inv_rms[:, None]
-        - resid * (inv_rms**3 * inner / width)[:, None]
+        g_res.T.astype(jnp.float32)
+        + scaled_grad * inv_rms[None, :]
+        - resid * (inv_rms * inv_rms * inner / width)[None, :]
     )
     d_conv = (d_resid * query_f).astype(jnp.bfloat16)
     d_query = (d_resid * conv_f).astype(jnp.bfloat16)
-    back_spread = lax.all_to_all(d_conv.T, "ctx", split_axis=0, concat_axis=1, tiled=True)
+    own = chans // n_ctx
+    extra = jnp.concatenate([split_rows(gain_part), split_rows(amax), jnp.zeros((2, chans), jnp.bfloat16)])
+    sent = jnp.concatenate(
+        [d_conv.reshape(n_ctx, own, tokens), jnp.broadcast_to(extra[None], (n_ctx, 8, chans))], axis=1
+    )
+    back = lax.all_to_all(sent, "ctx", split_axis=0, concat_axis=0, tiled=True)
+    gain_grad = jnp.sum(join_rows(back[:, own : own + 3]), axis=0)
+    amax = jnp.max(join_rows(back[:, own + 3 : own + 6]))
+    back_spread = back[:, :own].transpose(1, 0, 2).reshape(own, length)
     grad_re, grad_im = forward_dft(padded(back_spread.astype(jnp.float32), length), tables)
     srcg_re, srcg_im = spectral_product(grad_re, grad_im, filt_re, filt_im, True)
     src_grad = inverse_dft(srcg_re, srcg_im, tables)[:, :length].astype(jnp.bfloat16)
     fltg_re, fltg_im = spectral_product(grad_re, grad_im, src_re, src_im, True)
     filt_grad = inverse_dft(fltg_re, fltg_im, tables)[:, :length]
-    src_tok = lax.all_to_all(src_grad, "ctx", split_axis=1, concat_axis=0, tiled=True).T.astype(
+    src_tok = lax.all_to_all(src_grad, "ctx", split_axis=1, concat_axis=0, tiled=True).astype(
         jnp.float32
     )
     d_keys = (src_tok * values_f).astype(jnp.bfloat16)
     d_values = (src_tok * keys_f).astype(jnp.bfloat16)
+    first = jnp.dot(row_acts, d_all[:, :lanes], preferred_element_type=jnp.float32)
+    second = jnp.dot(row_acts, d_all[:, lanes:], preferred_element_type=jnp.float32)
     return (
-        d_resid.astype(jnp.bfloat16),
-        d_query,
-        d_keys,
-        d_values,
+        d_resid.astype(jnp.bfloat16).T,
+        d_query.T,
+        d_keys.T,
+        d_values.T,
         filt_grad,
         gain_grad,
-        first,
-        second,
+        first[:, :hidden],
+        second[:, :hidden],
         amax,
     )
 

time: 741 us -> 264 us (0.36)
  blocking collectives: 273 us -> 0 us
  waiting for transfers between devices: 345 us -> 102 us
  starting transfers between devices: 40.8 us -> 78.7 us
    all_gather x5 -> x2, waiting for transfers between devices: 201 us -> 17.9 us  [the longest x1 17.9 us: on_device(): lax.all_gather(jnp.concatenate([widen(w_gate), widen(w_up)], axis=1), 'ct...]
    psum x3 -> x0, blocking collectives: 150 us -> none  [the longest x1 65.1 us: on_device(): total_sq = lax.psum(sq_local, 'ch')]
    pmax x1 -> x0, blocking collectives: 123 us -> none  [on_device(): amax = lax.pmax(jnp.max(jnp.abs(normed)), ('ctx', 'ch'))]
    reduce_scatter x1 -> x0, waiting for transfers between devices: 103 us -> none  [on_device(): lax.psum_scatter(rounded.astype(jnp.float32).astype(jnp.bfloat16), 'ch',...]
    all_to_all x3 -> x6, waiting for transfers between devices: 17 us -> 62.2 us  [the longest x2 29.4 us: gather_ch(): return lax.all_to_all(spread, 'ch', split_axis=0, concat_axis=0, tiled=True)]
    all_to_all x3 -> x6, starting transfers between devices: 31.4 us -> 62.2 us  [the longest x1 18.8 us: on_device(): back = lax.all_to_all(sent, 'ch', split_axis=0, concat_axis=0, tiled=True)]
    all_to_all x1, starting transfers between devices: 3.5 us -> 11.2 us  [on_device(): lax.all_to_all(src_grad, 'ctx', split_axis=1, concat_axis=0, tiled=True)]
    dot_general x6 -> x4, matrix products: 16.9 us -> 14.2 us  [the longest x1 5.08 us: on_device(): lax.dot_general(acts, w_all, (((0,), (0,)), ((), ())), preferred_element_...]
  transfers between devices with their start and end apart: 11 -> 10, of which waited for: 8 -> 8; matrix products, arithmetic and copies ran while one was open for 4% -> 16% of each run, Pallas kernels for 0% -> 0%
where the time goes in v1:
time: 264 us; the launch traced here: 263 us
  waiting for transfers between devices  102 us (39%)
  starting transfers between devices  78.7 us (30%)
  matrix products  41.2 us (16%)
  between operations  19.6 us (7%)
  local copies, waits for them, and re-layouts  13.1 us (5%)
  other arithmetic  7.82 us (3%)
    all_to_all x2, waiting for transfers between devices, gather_ch(): return lax.all_to_all(spread, 'ch', split_axis=0, concat_axis=0, tiled=True)  29.4 us
    dot_general x24, matrix products, right_mult(): return jnp.einsum('ckq,qm->ckm', block, table, precision=highest)  21 us
    all_to_all x1, starting transfers between devices, on_device(): back = lax.all_to_all(sent, 'ch', split_axis=0, concat_axis=0, tiled=True)  18.8 us
    all_gather x1, waiting for transfers between devices, on_device(): lax.all_gather(jnp.concatenate([widen(w_gate), widen(w_up)], axis=1), 'ct...  17.9 us
    all_to_all x2, starting transfers between devices, gather_ch(): return lax.all_to_all(spread, 'ch', split_axis=0, concat_axis=0, tiled=True)  17.5 us
    all_to_all x1, waiting for transfers between devices, on_device(): back = lax.all_to_all(sent, 'ch', split_axis=0, concat_axis=0, tiled=True)  17.3 us
    all_to_all x1, starting transfers between devices, on_device(): lax.all_to_all(mixed, 'ctx', split_axis=0, concat_axis=1, tiled=True)  15.7 us
    all_to_all x1, waiting for transfers between devices, on_device(): lax.all_to_all(conv_full, 'ctx', split_axis=1, concat_axis=0, tiled=True)  11.3 us
  transfers between devices with their start and end apart: 10, of which 8 were waited for; matrix products, arithmetic and copies ran while one was open for 16% of the time, Pallas kernels for 0%

profile of v1, /device:TPU:1, one launch (start us, length us, event | category | flops | bytes accessed | tf_op | source)
XLA Modules:
  0.0 262.5 jit_solution(7780356039277695844)
XLA Ops:
  7.2 1.8 fusion.19
  11.4 15.7 %all-to-all-start = ((bf16[16,8,128]{2,1,0:T(8,128)(2,1)}), bf16[16,8,128]{2,1,0:T(8,128)(2,1)S(1)}, u32[]{:S(2)}, u32[]{:S(2)}) async-start(bf16[16,8,128]{2,1,0:T(8,128)(2,1)} %fusion.76), calls=%async_computation | async-start | bytes 65536 | tf_op jit(solution)/shard_map/all_to_all | solution.py:124
  32.6 6.2 %all-to-all-done = bf16[16,8,128]{2,1,0:T(8,128)(2,1)S(1)} async-done(((bf16[16,8,128]{2,1,0:T(8,128)(2,1)}), bf16[16,8,128]{2,1,0:T(8,128)(2,1)S(1)}, u32[]{:S(2)}, u32[]{:S(2)}) %all-to-all-start) | async-done | bytes 32800 | tf_op jit(solution)/shard_map/all_to_all | solution.py:124
  41.8 1.4 multiply_add_fusion.3
  44.2 1.0 fusion.114
  46.3 1.0 convolution_subtract_fusion.6
  49.3 5.3 %all-to-all-start.1 = ((bf16[8,16,128]{2,0,1:T(8,128)(2,1)}), bf16[8,16,128]{2,0,1:T(8,128)(2,1)S(1)}, u32[]{:S(2)}, u32[]{:S(2)}) async-start(bf16[8,16,128]{2,0,1:T(8,128)(2,1)} %slice_bitcast_fusion.2), calls=%async_computation.1 | async-start | bytes 65536 | tf_op jit(solution)/shard_map/all_to_all | solution.py:129
  54.8 11.3 %all-to-all-done.1 = bf16[8,16,128]{2,0,1:T(8,128)(2,1)S(1)} async-done(((bf16[8,16,128]{2,0,1:T(8,128)(2,1)}), bf16[8,16,128]{2,0,1:T(8,128)(2,1)S(1)}, u32[]{:S(2)}, u32[]{:S(2)}) %all-to-all-start.1) | async-done | bytes 32800 | tf_op jit(solution)/shard_map/all_to_all | solution.py:129
  66.3 1.1 broadcast_in_dim.13
  67.4 9.8 %all-to-all-start.2 = ((bf16[32,136,128]{2,1,0:T(8,128)(2,1)}), bf16[32,136,128]{2,1,0:T(8,128)(2,1)S(1)}, u32[]{:S(2)}, u32[]{:S(2)}) async-start(bf16[32,136,128]{2,1,0:T(8,128)(2,1)} %broadcast_in_dim.13), calls=%async_computation.2 | async-start | bytes 2228224 | tf_op jit(solution)/shard_map/all_to_all | solution.py:86
  78.0 16.7 %all-to-all-done.2 = bf16[32,136,128]{2,1,0:T(8,128)(2,1)S(1)} async-done(((bf16[32,136,128]{2,1,0:T(8,128)(2,1)}), bf16[32,136,128]{2,1,0:T(8,128)(2,1)S(1)}, u32[]{:S(2)}, u32[]{:S(2)}) %all-to-all-start.2) | async-done | bytes 1114144 | tf_op jit(solution)/shard_map/all_to_all | solution.py:86
  100.5 17.9 %all-gather.3.cloned.1.call-done = bf16[4096,768]{0,1:T(8,128)(2,1)} async-done(((bf16[256,768]{0,1:T(8,128)(2,1)}), bf16[4096,768]{0,1:T(8,128)(2,1)}) %all-gather.3.cloned.1.call-update) | async-done | bytes 6291472 | tf_op jit(solution)/shard_map/all_gather | solution.py:117
  118.4 5.1 %convolution_multiply_fusion = f32[128,768]{1,0:T(8,128)S(1)} fusion(bf16[4096,128]{1,0:T(8,128)(2,1)S(1)} %bitcast.267, bf16[4096,768]{0,1:T(8,128)(2,1)} %all-gather.3.cloned.1.call-done, f32[128]{0:T(128)S(1)} %add_rsqrt_fusion), kind=kOutput, calls=%fused_computation.6 | convolution fusion | flops 805404672 | bytes 7733760 | tf_op jit(solution)/shard_map/dot_general | solution.py:152
  124.5 4.7 %convolution_convert_fusion = bf16[4096,128]{1,0:T(8,128)(2,1)S(1)} fusion(bf16[4096,768]{0,1:T(8,128)(2,1)} %all-gather.3.cloned.1.call-done, f32[128,384]{1,0:T(8,128)S(1)} %get-tuple-element.58, f32[128,384]{1,0:T(8,128)S(1)} %get-tuple-element.57), kind=kOutput, calls=%fused_computation | convolution fusion | flops 806223872 | bytes 7733248 | tf_op jit(solution)/shard_map/dot_general | solution.py:166
  129.2 1.1 pad_maximum_fusion
  130.3 18.8 %all-to-all-start.3 = ((bf16[32,136,128]{2,1,0:T(8,128)(2,1)}), bf16[32,136,128]{2,1,0:T(8,128)(2,1)S(1)}, u32[]{:S(2)}, u32[]{:S(2)}) async-start(bf16[32,136,128]{2,1,0:T(8,128)(2,1)} %pad_maximum_fusion), calls=%async_computation.3 | async-start | bytes 2228224 | tf_op jit(solution)/shard_map/all_to_all | solution.py:178
  149.2 17.3 %all-to-all-done.3 = bf16[32,136,128]{2,1,0:T(8,128)(2,1)S(1)} async-done(((bf16[32,136,128]{2,1,0:T(8,128)(2,1)}), bf16[32,136,128]{2,1,0:T(8,128)(2,1)S(1)}, u32[]{:S(2)}, u32[]{:S(2)}) %all-to-all-start.3) | async-done | bytes 1114144 | tf_op jit(solution)/shard_map/all_to_all | solution.py:178
  167.6 6.5 %all-to-all-start.4 = ((bf16[16,16,128]{2,1,0:T(8,128)(2,1)}), bf16[16,16,128]{2,1,0:T(8,128)(2,1)S(1)}, u32[]{:S(2)}, u32[]{:S(2)}) async-start(bf16[16,16,128]{2,1,0:T(8,128)(2,1)} %pad_maximum_fusion.2), calls=%async_computation.4 | async-start | bytes 131072 | tf_op jit(solution)/shard_map/all_to_all | solution.py:197
  176.4 9.4 %all-to-all-done.4 = bf16[16,16,128]{2,1,0:T(8,128)(2,1)S(1)} async-done(((bf16[16,16,128]{2,1,0:T(8,128)(2,1)}), bf16[16,16,128]{2,1,0:T(8,128)(2,1)S(1)}, u32[]{:S(2)}, u32[]{:S(2)}) %all-to-all-start.4) | async-done | bytes 65568 | tf_op jit(solution)/shard_map/all_to_all | solution.py:197
  185.7 3.7 %all-to-all-start.6 = ((bf16[16,8,128]{2,1,0:T(8,128)(2,1)}), bf16[16,8,128]{2,1,0:T(8,128)(2,1)S(1)}, u32[]{:S(2)}, u32[]{:S(2)}) async-start(bf16[16,8,128]{2,1,0:T(8,128)(2,1)} %constant_dynamic-slice_fusion), calls=%async_computation.6 | async-start | bytes 65536 | tf_op jit(solution)/shard_map/all_to_all | solution.py:148
  194.3 1.0 fusion.107
  195.3 1.0 convolution_add_fusion.1
  196.3 1.0 convolution_subtract_fusion.3
  199.7 1.0 fusion.103
  200.7 1.0 convolution_add_fusion
  202.3 11.2 %all-to-all-start.5 = ((bf16[8,16,128]{2,0,1:T(8,128)(2,1)}), bf16[8,16,128]{2,0,1:T(8,128)(2,1)S(1)}, u32[]{:S(2)}, u32[]{:S(2)}) async-start(bf16[8,16,128]{2,0,1:T(8,128)(2,1)} %slice_bitcast_fusion), calls=%async_computation.5 | async-start | bytes 65536 | tf_op jit(solution)/shard_map/all_to_all | solution.py:206
  214.5 10.6 %all-to-all-done.5 = bf16[8,16,128]{2,0,1:T(8,128)(2,1)S(1)} async-done(((bf16[8,16,128]{2,0,1:T(8,128)(2,1)}), bf16[8,16,128]{2,0,1:T(8,128)(2,1)S(1)}, u32[]{:S(2)}, u32[]{:S(2)}) %all-to-all-start.5) | async-done | bytes 32800 | tf_op jit(solution)/shard_map/all_to_all | solution.py:206
  225.1 1.1 broadcast_in_dim.17
  226.2 7.6 %all-to-all-start.7 = ((bf16[32,8,2048]{2,1,0:T(8,128)(2,1)}), bf16[32,8,2048]{2,1,0:T(8,128)(2,1)S(1)}, u32[]{:S(2)}, u32[]{:S(2)}) async-start(bf16[32,8,2048]{2,1,0:T(8,128)(2,1)} %broadcast_in_dim.17), calls=%async_computation.7 | async-start | bytes 2097152 | tf_op jit(solution)/shard_map/all_to_all | solution.py:86
  238.5 12.7 %all-to-all-done.7 = bf16[32,8,2048]{2,1,0:T(8,128)(2,1)S(1)} async-done(((bf16[32,8,2048]{2,1,0:T(8,128)(2,1)}), bf16[32,8,2048]{2,1,0:T(8,128)(2,1)S(1)}, u32[]{:S(2)}, u32[]{:S(2)}) %all-to-all-start.7) | async-done | bytes 1048608 | tf_op jit(solution)/shard_map/all_to_all | solution.py:86
  251.2 3.0 %fusion = f32[256,344]{0,1:T(8,128)} fusion(bf16[2048,768]{1,0:T(8,128)(2,1)} %all-gather.5.cloned.1.call-done, bf16[32,8,2048]{2,1,0:T(8,128)(2,1)S(1)} %all-to-all-done.7), kind=kOutput, calls=%fused_computation.2 | convolution fusion | flops 360710144 | bytes 2973696 | tf_op jit(solution)/shard_map/dot_general | solution.py:212
  254.2 1.5 fusion.2
  (124 shorter events, 34.4 us)
Async XLA Ops:
  7.2 111.2 %all-gather.3.cloned.1.call-start = ((), (), s32[]{:S(2)}) async-start(), calls=%async_computation.8 | async-start | bytes 6684672 | tf_op jit(solution)/shard_map/all_gather | solution.py:117
  10.8 16.4 %copy-start.2 = (bf16[128,128]{0,1:T(8,128)(2,1)}, bf16[128,128]{0,1:T(8,128)(2,1)S(1)}, u32[]{:S(2)}) copy-start(bf16[128,128]{0,1:T(8,128)(2,1)S(1)} %copy.197) | copy-start | bytes 98308
  11.4 27.3 %all-to-all-start = ((bf16[16,8,128]{2,1,0:T(8,128)(2,1)}), bf16[16,8,128]{2,1,0:T(8,128)(2,1)S(1)}, u32[]{:S(2)}, u32[]{:S(2)}) async-start(bf16[16,8,128]{2,1,0:T(8,128)(2,1)} %fusion.76), calls=%async_computation | async-start | bytes 65536 | tf_op jit(solution)/shard_map/all_to_all | solution.py:124
  45.2 9.3 %copy-start.5 = (bf16[128,128]{1,0:T(8,128)(2,1)S(1)}, bf16[128,128]{1,0:T(8,128)(2,1)}, u32[]{:S(2)}) copy-start(bf16[128,128]{1,0:T(8,128)(2,1)} %param.10) | copy-start | bytes 98308
  45.3 9.4 %copy-start.6 = (bf16[128,128]{1,0:T(8,128)(2,1)S(1)}, bf16[128,128]{1,0:T(8,128)(2,1)}, u32[]{:S(2)}) copy-start(bf16[128,128]{1,0:T(8,128)(2,1)} %param.11) | copy-start | bytes 98308
  45.3 20.9 %copy-start.8 = (f32[128]{0:T(128)S(1)}, f32[128]{0:T(128)}, u32[]{:S(2)}) copy-start(f32[128]{0:T(128)} %param.15) | copy-start | bytes 1540
  48.3 28.9 %copy-start.4 = (bf16[128,344]{0,1:T(8,128)(2,1)S(1)}, bf16[128,344]{0,1:T(8,128)(2,1)}, u32[]{:S(2)}) copy-start(bf16[128,344]{0,1:T(8,128)(2,1)} %param.18) | copy-start | bytes 264196
  49.3 16.8 %all-to-all-start.1 = ((bf16[8,16,128]{2,0,1:T(8,128)(2,1)}), bf16[8,16,128]{2,0,1:T(8,128)(2,1)S(1)}, u32[]{:S(2)}, u32[]{:S(2)}) async-start(bf16[8,16,128]{2,0,1:T(8,128)(2,1)} %slice_bitcast_fusion.2), calls=%async_computation.1 | async-start | bytes 65536 | tf_op jit(solution)/shard_map/all_to_all | solution.py:129
  67.4 27.2 %all-to-all-start.2 = ((bf16[32,136,128]{2,1,0:T(8,128)(2,1)}), bf16[32,136,128]{2,1,0:T(8,128)(2,1)S(1)}, u32[]{:S(2)}, u32[]{:S(2)}) async-start(bf16[32,136,128]{2,1,0:T(8,128)(2,1)} %broadcast_in_dim.13), calls=%async_computation.2 | async-start | bytes 2228224 | tf_op jit(solution)/shard_map/all_to_all | solution.py:86
  94.8 28.8 %copy-start.9 = (f32[128]{0:T(128)}, f32[128]{0:T(128)S(1)}, u32[]{:S(2)}) copy-start(f32[128]{0:T(128)S(1)} %reduce_sum.71) | copy-start | bytes 1540
  118.4 5.1 %copy-start.1 = (bf16[128,344]{1,0:T(8,128)(2,1)S(1)}, bf16[128,344]{1,0:T(8,128)(2,1)}, u32[]{:S(2)}) copy-start(bf16[128,344]{1,0:T(8,128)(2,1)} %copy.193) | copy-start | bytes 264196
  129.2 19.9 %copy-start.7 = (bf16[128,128]{1,0:T(8,128)(2,1)S(1)}, bf16[128,128]{1,0:T(8,128)(2,1)}, u32[]{:S(2)}) copy-start(bf16[128,128]{1,0:T(8,128)(2,1)} %param.19) | copy-start | bytes 98308
  129.2 37.4 %copy-start.10 = (f32[128]{0:T(128)S(1)}, f32[128]{0:T(128)}, u32[]{:S(2)}) copy-start(f32[128]{0:T(128)} %copy-done.9) | copy-start | bytes 1540
  130.3 36.2 %all-to-all-start.3 = ((bf16[32,136,128]{2,1,0:T(8,128)(2,1)}), bf16[32,136,128]{2,1,0:T(8,128)(2,1)S(1)}, u32[]{:S(2)}, u32[]{:S(2)}) async-start(bf16[32,136,128]{2,1,0:T(8,128)(2,1)} %pad_maximum_fusion), calls=%async_computation.3 | async-start | bytes 2228224 | tf_op jit(solution)/shard_map/all_to_all | solution.py:178
  167.6 18.1 %all-to-all-start.4 = ((bf16[16,16,128]{2,1,0:T(8,128)(2,1)}), bf16[16,16,128]{2,1,0:T(8,128)(2,1)S(1)}, u32[]{:S(2)}, u32[]{:S(2)}) async-start(bf16[16,16,128]{2,1,0:T(8,128)(2,1)} %pad_maximum_fusion.2), calls=%async_computation.4 | async-start | bytes 131072 | tf_op jit(solution)/shard_map/all_to_all | solution.py:197
  174.1 77.1 %all-gather.5.cloned.1.call-start = ((), (), s32[]{:S(2)}) async-start(), calls=%async_computation.9 | async-start | bytes 3342336 | tf_op jit(solution)/shard_map/all_gather | solution.py:165
  174.9 17.6 %copy-start = (f32[8,64,64]{2,1,0:T(8,128)S(1)}, f32[8,64,64]{2,1,0:T(8,128)}, u32[]{:S(2)}) copy-start(f32[8,64,64]{2,1,0:T(8,128)} %get-tuple-element.82) | copy-start | bytes 393220
  185.7 16.6 %all-to-all-start.6 = ((bf16[16,8,128]{2,1,0:T(8,128)(2,1)}), bf16[16,8,128]{2,1,0:T(8,128)(2,1)S(1)}, u32[]{:S(2)}, u32[]{:S(2)}) async-start(bf16[16,8,128]{2,1,0:T(8,128)(2,1)} %constant_dynamic-slice_fusion), calls=%async_computation.6 | async-start | bytes 65536 | tf_op jit(solution)/shard_map/all_to_all | solution.py:148
  202.3 22.8 %all-to-all-start.5 = ((bf16[8,16,128]{2,0,1:T(8,128)(2,1)}), bf16[8,16,128]{2,0,1:T(8,128)(2,1)S(1)}, u32[]{:S(2)}, u32[]{:S(2)}) async-start(bf16[8,16,128]{2,0,1:T(8,128)(2,1)} %slice_bitcast_fusion), calls=%async_computation.5 | async-start | bytes 65536 | tf_op jit(solution)/shard_map/all_to_all | solution.py:206
  226.2 24.9 %all-to-all-start.7 = ((bf16[32,8,2048]{2,1,0:T(8,128)(2,1)}), bf16[32,8,2048]{2,1,0:T(8,128)(2,1)S(1)}, u32[]{:S(2)}, u32[]{:S(2)}) async-start(bf16[32,8,2048]{2,1,0:T(8,128)(2,1)} %broadcast_in_dim.17), calls=%async_computation.7 | async-start | bytes 2097152 | tf_op jit(solution)/shard_map/all_to_all | solution.py:86
  233.9 3.1 %copy-start.3 = (bf16[128,128]{0,1:T(8,128)(2,1)S(1)}, bf16[128,128]{0,1:T(8,128)(2,1)}, u32[]{:S(2)}) copy-start(bf16[128,128]{0,1:T(8,128)(2,1)} %copy-done.2) | copy-start | bytes 98308
  251.2 3.0 %copy-start.11 = (bf16[2048,768]{1,0:T(8,128)(2,1)S(1)}, bf16[2048,768]{1,0:T(8,128)(2,1)}, u32[]{:S(2)}) copy-start(bf16[2048,768]{1,0:T(8,128)(2,1)} %all-gather.5.cloned.1.call-done) | copy-start | bytes 9437188
Sparse Core Ops, SparseCore 0:
  10.0 108.3 all-gather.2
  177.6 66.7 all-gather.4

commit v2 on v0

v2 whole, which is shorter than its diff:
```python
import functools
import math

import jax
import jax.numpy as jnp
import numpy as np
from jax import lax
from jax.experimental import pallas as pl
from jax.experimental.pallas import tpu as pltpu
from jax.sharding import PartitionSpec as P

epsilon = 1e-06
f32 = jnp.float32
bf16 = jnp.bfloat16
VMEM = pl.BlockSpec(memory_space=pltpu.VMEM)
HBM = pl.BlockSpec(memory_space=pltpu.HBM)
EXTRA = 16


def call(body, outs, n_in, flops=1e8, in_specs=None, out_specs=None, scratch=(), limit=8, hbm=(), vmem=()):
    return pl.pallas_call(
        body,
        out_shape=tuple(
            pltpu.HBM(s, d) if k in hbm else pltpu.VMEM(s, d) if k in vmem else jax.ShapeDtypeStruct(s, d)
            for k, (s, d) in enumerate(outs)
        ),
        in_specs=in_specs or [VMEM] * n_in,
        out_specs=tuple(out_specs or [VMEM] * len(outs)),
        scratch_shapes=list(scratch),
        compiler_params=pltpu.CompilerParams(vmem_limit_bytes=limit * 2**20),
        cost_estimate=pl.CostEstimate(flops=int(flops), bytes_accessed=2**20, transcendentals=0),
    )


def split_table(table):
    high = table.astype(np.float32).astype(jnp.bfloat16)
    low = (table - high.astype(np.float64)).astype(np.float32).astype(jnp.bfloat16)
    return np.asarray(high), np.asarray(low)


@functools.cache
def dft_tables(blocks, chans, lanes):
    turns = 2 * blocks
    half = blocks + 1
    total = turns * lanes
    freq = np.arange(half)
    eye = np.eye(chans)
    angle = 2.0 * np.pi * (np.outer(freq, np.arange(blocks)) % turns) / turns
    first = np.concatenate([np.kron(np.cos(angle), eye), np.kron(-np.sin(angle), eye)])
    weight = np.where((freq == 0) | (freq == blocks), 1.0, 2.0)[:, None] / total
    last = np.concatenate(
        [np.kron(weight * np.cos(angle), eye), np.kron(-weight * np.sin(angle), eye)]
    ).T
    angle = 2.0 * np.pi * (np.outer(np.arange(lanes), np.arange(lanes)) % lanes) / lanes
    inner = np.concatenate([np.cos(angle), np.sin(angle)], axis=1)
    angle = 2.0 * np.pi * np.repeat(np.outer(freq, np.arange(lanes)), chans, axis=0) / total
    twiddle = np.stack([np.cos(angle), np.sin(angle)]).astype(np.float32)
    last = np.pad(last, ((0, 0), (0, -last.shape[1] % lanes)))
    wide = [np.concatenate(np.split(t, t.shape[1] // lanes, axis=1)) for t in (last, inner)]
    return (*split_table(first), *split_table(wide[0]), *split_table(wide[1]), twiddle)


def read_tables(refs):
    tables = []
    for ref in refs:
        table = ref[...]
        if 2 <= len(tables) < 6:
            lanes = table.shape[1]
            table = jnp.concatenate(
                [table[k : k + lanes] for k in range(0, table.shape[0], lanes)], axis=1
            )
        tables.append(table)
    return tables


def pair(value):
    high = value.astype(bf16)
    return high, (value - high.astype(f32)).astype(bf16)


def dot(left, right):
    return jnp.dot(left, right, preferred_element_type=f32)


def turn_lanes(parts, inner_hi, inner_lo, lanes, sign):
    rows = parts.shape[0] // 2
    high, low = pair(parts)
    both = dot(high, inner_hi) + (dot(high, inner_lo) + dot(low, inner_hi))
    by_cos, by_sin = both[:, :lanes], both[:, lanes:]
    real = by_cos[:rows] - sign * by_sin[rows:]
    imag = by_cos[rows:] + sign * by_sin[:rows]
    return real, imag


def to_spectrum(signal, tables, exact):
    first_hi, first_lo, _, _, inner_hi, inner_lo, twiddle = tables
    lanes = signal.shape[1]
    if exact:
        signal = signal.astype(bf16)
        out = dot(first_hi, signal) + dot(first_lo, signal)
    else:
        high, low = pair(signal)
        out = dot(first_hi, high) + (dot(first_hi, low) + dot(first_lo, high))
    rows = out.shape[0] // 2
    real, imag = out[:rows], out[rows:]
    cos, sin = twiddle[0], twiddle[1]
    turned = jnp.concatenate([real * cos + imag * sin, imag * cos - real * sin])
    return turn_lanes(turned, inner_hi, inner_lo, lanes, -1.0)


def from_spectrum(real, imag, tables):
    _, _, last_hi, last_lo, inner_hi, inner_lo, twiddle = tables
    lanes = real.shape[1]
    real, imag = turn_lanes(jnp.concatenate([real, imag]), inner_hi, inner_lo, lanes, 1.0)
    cos, sin = twiddle[0], twiddle[1]
    both = jnp.concatenate([real * cos - imag * sin, real * sin + imag * cos])
    rest = jnp.zeros((last_hi.shape[1] - both.shape[0], lanes), f32)
    high, low = pair(jnp.concatenate([both, rest]))
    return dot(last_hi, high) + (dot(last_hi, low) + dot(last_lo, high))


def split_rows(row):
    high = row.astype(bf16).astype(f32)
    rest = row - high
    mid = rest.astype(bf16).astype(f32)
    low = rest - mid
    return [high, mid, low]


def start_kernel(key_ref, value_ref, resid_ref, query_ref, gate_ref, up_ref, sent_ref, w_ref):
    w_ref[0] = gate_ref[...]
    w_ref[1] = up_ref[...]
    n_ctx = sent_ref.shape[0]
    own = key_ref.shape[1] // n_ctx
    mixed = (key_ref[...].astype(f32) * value_ref[...].astype(f32)).astype(bf16)
    parts = [mixed.astype(f32).T, resid_ref[...].astype(f32).T, query_ref[...].astype(f32).T]
    for peer in range(n_ctx):
        rows = slice(peer * own, (peer + 1) * own)
        sent_ref[peer] = jnp.concatenate([part[rows] for part in parts]).astype(bf16)


def filter_kernel(filt_ref, *refs):
    n_kept = (len(refs) - 2) // 2
    kept, (re_ref, im_ref), copies = refs[:n_kept], refs[n_kept : n_kept + 2], refs[n_kept + 2 :]
    for source, copy in zip(kept, copies):
        copy[...] = source[...]
    tables = read_tables(kept[:7])
    lanes = kept[0].shape[1]
    blocks = filt_ref.shape[1] // lanes
    signal = jnp.concatenate([filt_ref[:, a * lanes : (a + 1) * lanes] for a in range(blocks)])
    re_ref[...], im_ref[...] = to_spectrum(signal, tables, False)


def conv_kernel(met_ref, gain_ref, fre_ref, fim_ref, *refs):
    tables = read_tables(refs[:7])
    conv_ref, sre_ref, sim_ref, piece_ref = refs[7:]
    n_ctx = met_ref.shape[0]
    own = conv_ref.shape[0] // n_ctx
    blocks = [met_ref[k].astype(f32) for k in range(n_ctx)]
    source, resid, query = (
        jnp.concatenate([block[p * own : (p + 1) * own] for block in blocks]) for p in range(3)
    )
    real, imag = to_spectrum(source, tables, True)
    sre_ref[...], sim_ref[...] = real, imag
    fre, fim = fre_ref[...], fim_ref[...]
    conv = from_spectrum(real * fre - imag * fim, real * fim + imag * fre, tables).astype(bf16)
    conv_ref[...] = conv
    piece_ref[...] = ((resid + query * conv.astype(f32)) * gain_ref[...]).astype(bf16)


def resid_kernel(conv_ref, resid_ref, query_ref, gain_ref, piece_ref, sent_ref, r_ref):
    chans, tokens = conv_ref.shape
    resid = resid_ref[...].astype(f32).T + query_ref[...].astype(f32).T * conv_ref[...].astype(f32)
    r_ref[...] = resid
    scaled = (resid * gain_ref[...]).astype(bf16)
    square = jnp.sum(resid * resid, axis=0, keepdims=True)
    extra = jnp.concatenate(split_rows(square) + [jnp.zeros((EXTRA - 3, tokens), f32)]).astype(bf16)
    piece = piece_ref[...]
    for peer in range(sent_ref.shape[0]):
        sent_ref[peer, :chans] = scaled
        sent_ref[peer, chans : chans + EXTRA] = extra
        sent_ref[peer, chans + EXTRA :] = piece


def load_weights(w_ref, w_vmem, sems):
    copies = [
        pltpu.make_async_copy(w_ref.at[i], w_vmem.at[i], sems.at[i]) for i in range(w_ref.shape[0])
    ]
    for copy in copies:
        copy.start()
    return copies


def hidden_kernel(
    met_ref, w_ref, grad_ref, r_ref, gain_ref, d_ref, hid_ref, inv_ref, extra_ref, w_vmem, sems
):
    copies = load_weights(w_ref, w_vmem, sems)
    n_ch, _, tokens = met_ref.shape
    chans = r_ref.shape[0]
    per = w_ref.shape[3] // chans
    total = jnp.zeros((8, tokens), f32)
    for peer in range(n_ch):
        total = total + met_ref[peer, chans : chans + EXTRA].astype(f32)[:8]
    inv = lax.rsqrt((total[0:1] + total[1:2] + total[2:3]) / (n_ch * chans) + epsilon)
    inv_ref[...] = inv
    amax = jnp.max(jnp.abs((r_ref[...] * gain_ref[...]) * inv), axis=0, keepdims=True)
    amax = jnp.max(amax, axis=1, keepdims=True)
    gate, up = None, None
    for i, copy in enumerate(copies):
        copy.wait()
        acts = jnp.concatenate([met_ref[i * per + k, :chans] for k in range(per)])
        part = dot(w_vmem[i, 0], acts)
        gate = part if gate is None else gate + part
        part = dot(w_vmem[i, 1], acts)
        up = part if up is None else up + part
    gate, up = gate * inv, up * inv
    sigma = 1.0 / (1.0 + jnp.exp(-gate))
    hid = grad_ref[...].astype(f32)
    d_gate = hid * up * sigma * (1.0 + gate * (1.0 - sigma))
    d_up = hid * gate * sigma
    d_ref[0] = (d_gate * inv).astype(bf16)
    d_ref[1] = (d_up * inv).astype(bf16)
    hid_ref[0] = d_gate.astype(bf16)
    hid_ref[1] = d_up.astype(bf16)
    inner = jnp.sum(d_gate * gate + d_up * up, axis=0, keepdims=True)
    extra_ref[...] = jnp.concatenate(
        split_rows(inner)
        + split_rows(jnp.broadcast_to(amax, (1, tokens)))
        + [jnp.zeros((EXTRA - 6, tokens), f32)]
    ).astype(bf16)


def back_kernel(w_ref, hid_ref, extra_ref, sent_ref, w_vmem, sent_vmem, sems, sent_sems):
    arrivals = load_weights(w_ref, w_vmem, sems)
    n_ch, padded, chans = sent_ref.shape
    tokens = padded - EXTRA
    per = w_ref.shape[3] // chans
    extra = extra_ref[...]
    parts = sent_sems.shape[0]
    share = n_ch // parts
    copies = []
    for i, arrival in enumerate(arrivals):
        arrival.wait()
        term = 0.0
        for half in range(2):
            term = term + lax.dot_general(
                hid_ref[half],
                w_vmem[i, half],
                (((0,), (0,)), ((), ())),
                preferred_element_type=f32,
            )
        term = term.astype(bf16)
        for k in range(per):
            sent_vmem[i * per + k, :tokens] = term[:, k * chans : (k + 1) * chans]
            sent_vmem[i * per + k, tokens:] = extra
        done = (i + 1) * per
        if done % share == 0:
            copy = pltpu.make_async_copy(
                sent_vmem.at[done - share : done],
                sent_ref.at[done - share : done],
                sent_sems.at[done // share - 1],
            )
            copy.start()
            copies.append(copy)
    for copy in copies:
        copy.wait()


def norm_kernel(
    back_ref, r_ref, conv_ref, query_ref, gres_ref, gain_ref, inv_ref, dx_ref, dq_ref, sent_ref
):
    n_ch = back_ref.shape[0]
    chans, tokens = r_ref.shape
    n_ctx = sent_ref.shape[0]
    own = chans // n_ctx
    total = back_ref[0, :tokens].astype(f32)
    extra = back_ref[0, tokens : tokens + EXTRA].astype(f32)[:8]
    inner, peak = extra[0:1] + extra[1:2] + extra[2:3], extra[3:4] + extra[4:5] + extra[5:6]
    for peer in range(1, n_ch):
        total = total + back_ref[peer, :tokens].astype(f32)
        extra = back_ref[peer, tokens : tokens + EXTRA].astype(f32)[:8]
        inner = inner + (extra[0:1] + extra[1:2] + extra[2:3])
        peak = jnp.maximum(peak, extra[3:4] + extra[4:5] + extra[5:6])
    d_norm = total.T
    resid = r_ref[...]
    inv = inv_ref[...]
    gain = gain_ref[...]
    d_resid = (
        gres_ref[...].astype(f32).T
        + (gain * d_norm) * inv
        - resid * (inv * inv * inner / (n_ch * chans))
    )
    dx_ref[...] = d_resid.T.astype(bf16)
    dq_ref[...] = (d_resid * conv_ref[...].astype(f32)).T.astype(bf16)
    d_conv = (d_resid * query_ref[...].astype(f32).T).astype(bf16).astype(f32)
    product = (d_norm * resid * inv).T
    gain_part = jnp.sum(product, axis=0, keepdims=True)
    extra = split_rows(gain_part) + split_rows(peak) + [jnp.zeros((2, chans), f32)]
    for peer in range(n_ctx):
        rows = slice(peer * own, (peer + 1) * own)
        sent_ref[peer] = jnp.concatenate([d_conv[rows]] + extra).astype(bf16)


def rows_kernel(back_ref, out_ref):
    n_ch = back_ref.shape[0]
    lanes = back_ref.shape[2]
    start = back_ref.shape[1] - lanes
    blocks = out_ref.shape[1] // lanes
    own = lanes // blocks
    pair_of = EXTRA // own
    for first in range(0, n_ch, pair_of):
        parts = []
        for peer in range(first, first + pair_of):
            block = back_ref[peer, start:].astype(f32)
            parts.append(
                jnp.concatenate([block[a * own : (a + 1) * own] for a in range(blocks)], axis=1)
            )
        out_ref[first * own : (first + pair_of) * own] = jnp.concatenate(parts).astype(bf16)


def grad_kernel(back_ref, fre_ref, fim_ref, *refs):
    tables = read_tables(refs[:7])
    ds_ref, gre_ref, gim_ref, dgain_ref, amax_ref = refs[7:]
    n_ctx = back_ref.shape[0]
    own = ds_ref.shape[0] // n_ctx
    blocks = [back_ref[k].astype(f32) for k in range(n_ctx)]
    real, imag = to_spectrum(jnp.concatenate([b[:own] for b in blocks]), tables, True)
    gre_ref[...], gim_ref[...] = real, imag
    fre, fim = fre_ref[...], fim_ref[...]
    back = from_spectrum(real * fre + imag * fim, imag * fre - real * fim, tables)
    ds_ref[...] = back.astype(bf16)
    gain, peak = None, None
    for block in blocks:
        extra = block[own:]
        g = extra[0:1] + extra[1:2] + extra[2:3]
        p = extra[3:4] + extra[4:5] + extra[5:6]
        gain = g if gain is None else gain + g
        peak = p if peak is None else jnp.maximum(peak, p)
    dgain_ref[...] = gain
    amax_ref[...] = jnp.max(peak, axis=1, keepdims=True)


def filter_grad_kernel(gre_ref, gim_ref, sre_ref, sim_ref, *refs):
    tables = read_tables(refs[:7])
    out_ref = refs[7]
    own = out_ref.shape[0]
    real, imag, sre, sim = gre_ref[...], gim_ref[...], sre_ref[...], sim_ref[...]
    grad = from_spectrum(real * sre + imag * sim, imag * sre - real * sim, tables)
    lanes = grad.shape[1]
    for a in range(out_ref.shape[1] // lanes):
        out_ref[:, a * lanes : (a + 1) * lanes] = grad[a * own : (a + 1) * own]


def products_kernel(ds_ref, key_ref, value_ref, dk_ref, dv_ref):
    grad = ds_ref[...].astype(f32).T
    dk_ref[...] = (grad * value_ref[...].astype(f32)).astype(bf16)
    dv_ref[...] = (grad * key_ref[...].astype(f32)).astype(bf16)


def weight_kernel(d_ref, rows_ref, first_ref, second_ref, d_vmem, sems):
    n_ctx, _, _, tokens = d_ref.shape
    copies = load_weights(d_ref, d_vmem, sems)
    acc = [0.0, 0.0]
    for i in range(n_ctx):
        copies[i].wait()
        for half in range(2):
            acc[half] = acc[half] + lax.dot_general(
                d_vmem[i, half],
                rows_ref[:, i * tokens : (i + 1) * tokens],
                (((1,), (1,)), ((), ())),
                preferred_element_type=f32,
            )
    first_ref[...] = acc[0]
    second_ref[...] = acc[1]


def on_device(resid_in, query_in, key_in, value_in, filt, gain, w_gate, w_up, g_hid, g_res):
    tokens, chans = resid_in.shape
    n_ctx = lax.axis_size("ctx")
    n_ch = lax.axis_size("ch")
    length = tokens * n_ctx
    rows, hidden = w_gate.shape
    own = chans // n_ctx
    tables = dft_tables(n_ctx, own, tokens)
    spec_rows = tables[6].shape[1]

    def in_hbm(array):
        return pltpu.with_memory_space_constraint(array, pltpu.HBM)

    tables = [in_hbm(jnp.asarray(table)) for table in tables]
    key_in, value_in, resid_in, query_in, g_res, filt = (
        in_hbm(array) for array in (key_in, value_in, resid_in, query_in, g_res, filt)
    )
    spectrum = ((spec_rows, tokens), f32)
    square = ((chans, tokens), bf16)
    gain_col = gain[:, None]
    gain_own = jnp.tile(
        lax.dynamic_slice_in_dim(gain_col, lax.axis_index("ctx") * own, own, 0), (n_ctx, 1)
    )
    groups = 4

    weights_vmem = pltpu.VMEM((n_ctx, 2, hidden, rows), bf16)
    weights_sems = pltpu.SemaphoreType.DMA((n_ctx,))
    places = []
    for i in range(n_ctx):
        for j in range(n_ch):
            block = i * n_ch + j
            held_by = (block % n_ctx) * n_ch + block // n_ctx
            places.append((held_by, block))

    sent, w_both = call(
        start_kernel,
        [((n_ctx, 3 * own, tokens), bf16), ((2, hidden, rows), bf16)],
        6,
        hbm=(0, 1),
    )(key_in, value_in, resid_in, query_in, in_hbm(w_gate.T), in_hbm(w_up.T))
    w_all = in_hbm(lax.all_gather(w_both, "ctx", axis=0, tiled=False))
    met = lax.all_to_all(sent, "ctx", 0, 0, tiled=True)
    kept = [*tables, key_in, value_in, resid_in, query_in, g_res]
    fre, fim, *kept = call(
        filter_kernel,
        [spectrum] * 2 + [(array.shape, array.dtype) for array in kept],
        len(kept) + 1,
        vmem=range(len(kept) + 2),
    )(filt, *kept)
    tables = kept[:7]
    key_in, value_in, resid_in, query_in, g_res = kept[7:]
    conv, sre, sim, piece = call(conv_kernel, [square, spectrum, spectrum, square], 11, vmem=(1, 2))(
        met, gain_own, fre, fim, *tables
    )
    piece = lax.ppermute(piece, ("ctx", "ch"), places)
    conv = lax.all_to_all(conv.reshape(n_ctx, own, tokens), "ctx", 0, 0, tiled=True).reshape(
        chans, tokens
    )
    sent, resid = call(
        resid_kernel,
        [((n_ch, 2 * chans + EXTRA, tokens), bf16), ((chans, tokens), f32)],
        5,
    )(conv, resid_in, query_in, gain_col, piece)
    met = lax.all_to_all(sent, "ch", 0, 0, tiled=True)
    (row_acts,) = call(rows_kernel, [((rows, length), bf16)], 1)(met)
    d_scaled, d_hid, inv, extra = call(
        hidden_kernel,
        [
            ((2, hidden, tokens), bf16),
            ((2, hidden, tokens), bf16),
            ((1, tokens), f32),
            ((EXTRA, tokens), bf16),
        ],
        5,
        in_specs=[VMEM, HBM, VMEM, VMEM, VMEM],
        scratch=[weights_vmem, weights_sems],
        flops=1e9,
        limit=16,
    )(met, w_all, in_hbm(g_hid.T), resid, gain_col)
    d_all = in_hbm(lax.all_gather(d_scaled, "ctx", axis=0, tiled=False))
    sent_shape = (n_ch, tokens + EXTRA, chans)
    (sent,) = call(
        back_kernel,
        [(sent_shape, bf16)],
        3,
        in_specs=[HBM, VMEM, VMEM],
        out_specs=[HBM],
        scratch=[
            weights_vmem,
            pltpu.VMEM(sent_shape, bf16),
            weights_sems,
            pltpu.SemaphoreType.DMA((groups,)),
        ],
        flops=1e9,
        limit=16,
    )(w_all, d_hid, extra)
    back = lax.all_to_all(sent, "ch", 0, 0, tiled=True)
    dx, dq, sent = call(
        norm_kernel,
        [((tokens, chans), bf16), ((tokens, chans), bf16), ((n_ctx, 2 * own, tokens), bf16)],
        7,
    )(back, resid, conv, query_in, g_res, gain_col, inv)
    back = lax.all_to_all(sent, "ctx", 0, 0, tiled=True)
    ds, gre, gim, dgain, amax = call(
        grad_kernel,
        [square, spectrum, spectrum, ((1, chans), f32), ((1, 1), f32)],
        10,
        vmem=(1, 2),
    )(back, fre, fim, *tables)
    ds = lax.all_to_all(ds.reshape(n_ctx, own, tokens), "ctx", 0, 0, tiled=True)
    (dfilt,) = call(filter_grad_kernel, [(filt.shape, f32)], 11)(gre, gim, sre, sim, *tables)
    dk, dv = call(products_kernel, [((tokens, chans), bf16)] * 2, 3)(
        ds.reshape(chans, tokens), key_in, value_in
    )
    first, second = call(
        weight_kernel,
        [((hidden, rows), f32)] * 2,
        2,
        in_specs=[HBM, VMEM],
        scratch=[pltpu.VMEM((n_ctx, 2, hidden, tokens), bf16), pltpu.SemaphoreType.DMA((n_ctx,))],
        flops=1e9,
        limit=16,
    )(d_all, row_acts)
    return (dx, dq, dk, dv, dfilt, dgain[0], first.T, second.T, amax[0, 0])


def solution(mesh):
    return jax.shard_map(
        on_device,
        mesh=mesh,
        in_specs=(
            P("ctx", "ch"),
            P("ctx", "ch"),
            P("ctx", "ch"),
            P("ctx", "ch"),
            P(("ch", "ctx"), None),
            P("ch"),
            P("ctx", "ch"),
            P("ctx", "ch"),
            P("ctx", "ch"),
            P("ctx", "ch"),
        ),
        out_specs=(
            P("ctx", "ch"),
            P("ctx", "ch"),
            P("ctx", "ch"),
            P("ctx", "ch"),
            P(("ch", "ctx"), None),
            P("ch"),
            P("ctx", "ch"),
            P("ctx", "ch"),
            P(),
        ),
        check_vma=False,
    )
```

time: 741 us -> 196 us (0.26)
  waiting for transfers between devices: 345 us -> 21.7 us
  blocking collectives: 273 us -> 93.2 us
  matrix products: 43.8 us -> 0 us
  Pallas kernels: 0 us -> 26.4 us
  starting transfers between devices: 40.8 us -> 31.4 us
    all_gather x5 -> x2, waiting for transfers between devices: 201 us -> 0.01 us  [the longest x1 0.01 us: on_device(): w_all = in_hbm(lax.all_gather(w_both, 'ctx', axis=0, tiled=False))]
    psum x3 -> x0, blocking collectives: 150 us -> none  [the longest x1 65.1 us: on_device(): total_sq = lax.psum(sq_local, 'ch')]
    pmax x1 -> x0, blocking collectives: 123 us -> none  [on_device(): amax = lax.pmax(jnp.max(jnp.abs(normed)), ('ctx', 'ch'))]
    reduce_scatter x1 -> x0, waiting for transfers between devices: 103 us -> none  [on_device(): lax.psum_scatter(rounded.astype(jnp.float32).astype(jnp.bfloat16), 'ch',...]
    all_to_all x0 -> x3, blocking collectives: none -> 93.2 us  [the longest x1 43.6 us: on_device(): met = lax.all_to_all(sent, 'ch', 0, 0, tiled=True)]
    dot_general x42 -> x0, matrix products: 43.8 us -> none  [the longest x24 21 us: right_mult(): return jnp.einsum('ckq,qm->ckm', block, table, precision=highest)]
    pallas_call x0 -> x12, Pallas kernels: none -> 26.4 us  [the longest x1 6.32 us: on_device(): call(back_kernel, [(sent_shape, bf16)], 3, in_specs=[HBM, VMEM, VMEM], ou...]
    all_to_all x5 -> x3, waiting for transfers between devices: 38.6 us -> 19.9 us  [the longest x1 9.04 us: on_device(): met = lax.all_to_all(sent, 'ctx', 0, 0, tiled=True)]
  transfers between devices with their start and end apart: 11 -> 6, of which waited for: 8 -> 4; matrix products, arithmetic and copies ran while one was open for 4% -> 0% of each run, Pallas kernels for 0% -> 8%
where the time goes in v2:
time: 196 us; the launch traced here: 195 us
  blocking collectives  93.2 us (48%)
  starting transfers between devices  31.4 us (16%)
  Pallas kernels  26.4 us (13%)
  waiting for transfers between devices  21.7 us (11%)
  between operations  14.3 us (7%)
  local copies, waits for them, and re-layouts  7.73 us (4%)
    all_to_all x1, blocking collectives, on_device(): met = lax.all_to_all(sent, 'ch', 0, 0, tiled=True)  43.6 us
    all_to_all x1, blocking collectives, on_device(): back = lax.all_to_all(sent, 'ch', 0, 0, tiled=True)  30.9 us
    all_to_all x1, blocking collectives, on_device(): back = lax.all_to_all(sent, 'ctx', 0, 0, tiled=True)  18.8 us
    all_to_all x1, starting transfers between devices, on_device(): met = lax.all_to_all(sent, 'ctx', 0, 0, tiled=True)  15.8 us
    all_to_all x1, waiting for transfers between devices, on_device(): met = lax.all_to_all(sent, 'ctx', 0, 0, tiled=True)  9.04 us
    all_to_all x1, waiting for transfers between devices, on_device(): ds = lax.all_to_all(ds.reshape(n_ctx, own, tokens), 'ctx', 0, 0, tiled=True)  7.5 us
    unnamed x46, local copies, waits for them, and re-layouts  6.81 us
    pallas_call x1, Pallas kernels, on_device(): call(back_kernel, [(sent_shape, bf16)], 3, in_specs=[HBM, VMEM, VMEM], ou...  6.32 us
  transfers between devices with their start and end apart: 6, of which 4 were waited for; matrix products, arithmetic and copies ran while one was open for 0% of the time, Pallas kernels for 8%

profile of v2, /device:TPU:1, one launch (start us, length us, event | category | flops | bytes accessed | tf_op | source)
XLA Modules:
  0.0 194.8 jit_solution(151440179294308911)
XLA Ops:
  7.2 1.9 shard_map.232
  9.1 15.8 %all-to-all-start = ((bf16[16,24,128]{2,1,0:T(8,128)(2,1)}), bf16[16,24,128]{2,1,0:T(8,128)(2,1)S(1)}, u32[]{:S(2)}, u32[]{:S(2)}) async-start(bf16[16,24,128]{2,1,0:T(8,128)(2,1)} %get-tuple-element.48), calls=%async_computation | async-start | bytes 196608 | tf_op jit(solution)/shard_map/all_to_all | solution.py:418
  24.9 0.7 dynamic-slice.3
  25.7 1.9 shard_map.233
  27.7 9.0 %all-to-all-done.met_ref = bf16[16,24,128]{2,1,0:T(8,128)(2,1)S(1)} async-done(((bf16[16,24,128]{2,1,0:T(8,128)(2,1)}), bf16[16,24,128]{2,1,0:T(8,128)(2,1)S(1)}, u32[]{:S(2)}, u32[]{:S(2)}) %all-to-all-start) | async-done | bytes 98336 | tf_op jit(solution)/shard_map/all_to_all | solution.py:418
  36.8 1.8 shard_map.234
  38.6 0.6 copy-done.10
  39.2 0.6 copy-done.12
  39.8 4.7 %all-to-all-start.1 = ((bf16[16,8,128]{2,1,0:T(8,128)(2,1)}), bf16[16,8,128]{2,1,0:T(8,128)(2,1)S(1)}, u32[]{:S(2)}, u32[]{:S(2)}) async-start(bf16[16,8,128]{2,1,0:T(8,128)(2,1)} %bitcast.3), calls=%async_computation.1 | async-start | bytes 65536 | tf_op jit(solution)/shard_map/all_to_all | solution.py:432
  44.6 6.3 %collective-permute-start = (bf16[128,128]{1,0:T(8,128)(2,1)S(1)}, bf16[128,128]{1,0:T(8,128)(2,1)S(1)}, u32[]{:S(2)}, u32[]{:S(2)}) collective-permute-start(bf16[128,128]{1,0:T(8,128)(2,1)S(1)} %get-tuple-element.61), channel_id=1, source_target_pairs={{0,0},{32,1},{64,2},{96,3},{128,4},{160,5},{192,6},{224,7},{256,8}... | collective-permute-start | bytes 98312 | tf_op jit(solution)/shard_map/ppermute | solution.py:431
  51.0 1.7 collective-permute-done.piece_ref
  52.7 3.4 %all-to-all-done.1 = bf16[16,8,128]{2,1,0:T(8,128)(2,1)S(1)} async-done(((bf16[16,8,128]{2,1,0:T(8,128)(2,1)}), bf16[16,8,128]{2,1,0:T(8,128)(2,1)S(1)}, u32[]{:S(2)}, u32[]{:S(2)}) %all-to-all-start.1) | async-done | bytes 32800 | tf_op jit(solution)/shard_map/all_to_all | solution.py:432
  56.1 0.2 shard_map.235
  56.3 43.6 %all_to_all.30.met_ref.back_ref = bf16[32,272,128]{2,1,0:T(8,128)(2,1)S(1)} all-to-all(bf16[32,272,128]{2,1,0:T(8,128)(2,1)S(1)} %get-tuple-element.62), channel_id=1, replica_groups=mesh['ctx'=16,'ch'=32] {'ch'}, dimensions={0} | all-to-all | bytes 4456448 | tf_op jit(solution)/shard_map/all_to_all | solution.py:440
  99.9 5.1 %shard_map.236 = (bf16[2,344,128]{2,1,0:T(8,128)(2,1)}, bf16[2,344,128]{2,1,0:T(8,128)(2,1)S(1)}, f32[1,128]{1,0:T(1,128)S(1)}, bf16[16,128]{1,0:T(8,128)(2,1)S(1)}) custom-call(bf16[32,272,128]{2,1,0:T(8,128)(2,1)S(1)} %all_to_all.30.met_ref.back_ref, bf16[16,2,344,256]{3,2,1,0:T(8,128)(2,1)} %bitcast.17, bf16[344,128]{1,0:T(8,128)(2,1)} %bitcast.22, ...), custom_call_target="tpu_custom_call" | custom-call | flops 1000000000 | bytes 1048576 | tf_op jit(solution)/shard_map/pallas_call | solution.py:442
  105.1 6.3 %shard_map.237 = bf16[32,144,128]{2,1,0:T(8,128)(2,1)S(1)} custom-call(bf16[16,2,344,256]{3,2,1,0:T(8,128)(2,1)} %bitcast.18, bf16[2,344,128]{2,1,0:T(8,128)(2,1)S(1)} %get-tuple-element.64.hid_ref, bf16[16,128]{1,0:T(8,128)(2,1)S(1)} %get-tuple-element.65.extra_ref), custom_call_target="tpu_custom_call" | custom-call | flops 1000000000 | bytes 1048576 | tf_op jit(solution)/shard_map/pallas_call | solution.py:458
  111.4 30.9 %all_to_all.31.back_ref = bf16[32,144,128]{2,1,0:T(8,128)(2,1)S(1)} all-to-all(bf16[32,144,128]{2,1,0:T(8,128)(2,1)S(1)} %shard_map.237), channel_id=1, replica_groups=mesh['ctx'=16,'ch'=32] {'ch'}, dimensions={0} | all-to-all | bytes 2359296 | tf_op jit(solution)/shard_map/all_to_all | solution.py:473
  142.3 1.0 shard_map.238
  143.2 18.8 %all_to_all.32.back_ref = bf16[16,16,128]{2,1,0:T(8,128)(2,1)S(1)} all-to-all(bf16[16,16,128]{2,1,0:T(8,128)(2,1)S(1)} %get-tuple-element.70), channel_id=1, replica_groups=mesh['ctx'=16,'ch'=32] {'ctx'}, dimensions={0} | all-to-all | bytes 131072 | tf_op jit(solution)/shard_map/all_to_all | solution.py:479
  162.0 1.8 shard_map.239
  163.8 0.6 copy-done.14
  164.5 0.6 copy-done.16
  165.1 4.6 %all-to-all-start.5 = ((bf16[16,8,128]{2,1,0:T(8,128)(2,1)}), bf16[16,8,128]{2,1,0:T(8,128)(2,1)S(1)}, u32[]{:S(2)}, u32[]{:S(2)}) async-start(bf16[16,8,128]{2,1,0:T(8,128)(2,1)} %bitcast.7), calls=%async_computation.5 | async-start | bytes 65536 | tf_op jit(solution)/shard_map/all_to_all | solution.py:486
  169.8 0.7 copy-done.1
  170.8 0.9 copy-done.11
  171.7 0.9 copy-done.13
  172.6 1.2 shard_map.241
  173.8 7.5 %all-to-all-done.5 = bf16[16,8,128]{2,1,0:T(8,128)(2,1)S(1)} async-done(((bf16[16,8,128]{2,1,0:T(8,128)(2,1)}), bf16[16,8,128]{2,1,0:T(8,128)(2,1)S(1)}, u32[]{:S(2)}, u32[]{:S(2)}) %all-to-all-start.5) | async-done | bytes 32800 | tf_op jit(solution)/shard_map/all_to_all | solution.py:486
  181.3 0.8 copy-done.19
  182.1 0.8 copy-done.21
  182.8 0.7 shard_map.240
  183.6 4.3 %shard_map.243 = (f32[344,256]{1,0:T(8,128)}, f32[344,256]{1,0:T(8,128)}) custom-call(bf16[16,2,344,128]{3,2,1,0:T(8,128)(2,1)} %bitcast.19, bf16[256,2048]{1,0:T(8,128)(2,1)S(1)} %shard_map.242.rows_ref), custom_call_target="tpu_custom_call" | custom-call | flops 1000000000 | bytes 1048576 | tf_op jit(solution)/shard_map/pallas_call | solution.py:491
  (47 shorter events, 0.7 us)
Async XLA Ops:
  7.2 43.7 %copy-start.22 = (f32[128]{0:T(128)S(1)}, f32[128]{0:T(128)}, u32[]{:S(2)}) copy-start(f32[128]{0:T(128)} %param.22) | copy-start | bytes 1540
  7.2 92.7 %all-gather.5.cloned.1.call-start = ((), (), s32[]{:S(2)}) async-start(), calls=%async_computation.6 | async-start | bytes 5988352 | tf_op jit(solution)/shard_map/all_gather | solution.py:417
  9.1 27.6 %all-to-all-start = ((bf16[16,24,128]{2,1,0:T(8,128)(2,1)}), bf16[16,24,128]{2,1,0:T(8,128)(2,1)S(1)}, u32[]{:S(2)}, u32[]{:S(2)}) async-start(bf16[16,24,128]{2,1,0:T(8,128)(2,1)} %get-tuple-element.48), calls=%async_computation | async-start | bytes 196608 | tf_op jit(solution)/shard_map/all_to_all | solution.py:418
  27.6 72.3 %copy-start.18 = (bf16[128,128]{1,0:T(8,128)(2,1)}, bf16[128,128]{1,0:T(8,128)(2,1)S(1)}, u32[]{:S(2)}) copy-start(bf16[128,128]{1,0:T(8,128)(2,1)S(1)} %get-tuple-element.72.key_ref) | copy-start | bytes 98308
  27.7 72.2 %copy-start.20 = (bf16[128,128]{1,0:T(8,128)(2,1)}, bf16[128,128]{1,0:T(8,128)(2,1)S(1)}, u32[]{:S(2)}) copy-start(bf16[128,128]{1,0:T(8,128)(2,1)S(1)} %get-tuple-element.73.value_ref) | copy-start | bytes 98308
  27.7 134.3 %copy-start = (bf16[384,128]{1,0:T(8,128)(2,1)}, bf16[384,128]{1,0:T(8,128)(2,1)S(1)}, u32[]{:S(2)}) copy-start(bf16[384,128]{1,0:T(8,128)(2,1)S(1)} %get-tuple-element.54.refs_3_) | copy-start | bytes 294916
  27.7 134.3 %copy-start.2 = (bf16[272,128]{1,0:T(8,128)(2,1)}, bf16[272,128]{1,0:T(8,128)(2,1)S(1)}, u32[]{:S(2)}) copy-start(bf16[272,128]{1,0:T(8,128)(2,1)S(1)} %get-tuple-element.51.refs_0_) | copy-start | bytes 208900
  27.7 134.3 %copy-start.4 = (bf16[272,128]{1,0:T(8,128)(2,1)}, bf16[272,128]{1,0:T(8,128)(2,1)S(1)}, u32[]{:S(2)}) copy-start(bf16[272,128]{1,0:T(8,128)(2,1)S(1)} %get-tuple-element.52.refs_1_) | copy-start | bytes 208900
  27.7 134.3 %copy-start.6 = (bf16[256,128]{1,0:T(8,128)(2,1)}, bf16[256,128]{1,0:T(8,128)(2,1)S(1)}, u32[]{:S(2)}) copy-start(bf16[256,128]{1,0:T(8,128)(2,1)S(1)} %get-tuple-element.55.refs_4_) | copy-start | bytes 196612
  27.7 134.3 %copy-start.8 = (bf16[256,128]{1,0:T(8,128)(2,1)}, bf16[256,128]{1,0:T(8,128)(2,1)S(1)}, u32[]{:S(2)}) copy-start(bf16[256,128]{1,0:T(8,128)(2,1)S(1)} %get-tuple-element.56.refs_5_) | copy-start | bytes 196612
  38.6 0.6 copy-start.10
  39.2 0.6 copy-start.12
  39.8 16.3 %all-to-all-start.1 = ((bf16[16,8,128]{2,1,0:T(8,128)(2,1)}), bf16[16,8,128]{2,1,0:T(8,128)(2,1)S(1)}, u32[]{:S(2)}, u32[]{:S(2)}) async-start(bf16[16,8,128]{2,1,0:T(8,128)(2,1)} %bitcast.3), calls=%async_computation.1 | async-start | bytes 65536 | tf_op jit(solution)/shard_map/all_to_all | solution.py:432
  44.5 139.0 %all-gather.7.cloned.1.call-start = ((), (), s32[]{:S(2)}) async-start(), calls=%async_computation.7 | async-start | bytes 2994176 | tf_op jit(solution)/shard_map/all_gather | solution.py:456
  44.6 8.1 %collective-permute-start = (bf16[128,128]{1,0:T(8,128)(2,1)S(1)}, bf16[128,128]{1,0:T(8,128)(2,1)S(1)}, u32[]{:S(2)}, u32[]{:S(2)}) collective-permute-start(bf16[128,128]{1,0:T(8,128)(2,1)S(1)} %get-tuple-element.61), channel_id=1, source_target_pairs={{0,0},{32,1},{64,2},{96,3},{128,4},{160,5},{192,6},{224,7},{256,8}... | collective-permute-start | bytes 98312 | tf_op jit(solution)/shard_map/ppermute | solution.py:431
  163.8 0.6 copy-start.14
  164.5 0.6 copy-start.16
  165.1 16.2 %all-to-all-start.5 = ((bf16[16,8,128]{2,1,0:T(8,128)(2,1)}), bf16[16,8,128]{2,1,0:T(8,128)(2,1)S(1)}, u32[]{:S(2)}, u32[]{:S(2)}) async-start(bf16[16,8,128]{2,1,0:T(8,128)(2,1)} %bitcast.7), calls=%async_computation.5 | async-start | bytes 65536 | tf_op jit(solution)/shard_map/all_to_all | solution.py:486
  169.7 0.9 copy-start.1
  169.7 0.9 copy-start.3
  169.7 1.0 copy-start.5
  169.7 0.9 copy-start.7
  169.7 1.0 copy-start.9
  169.7 1.0 copy-start.15
  169.8 1.1 copy-start.17
  170.8 0.9 copy-start.11
  171.7 0.9 copy-start.13
  181.3 0.8 copy-start.19
  182.1 0.8 copy-start.21
Sparse Core Ops, SparseCore 0:
  10.7 88.9 all-gather.4
  105.2 69.7 all-gather.6

commit v3 on v2

--- a/solution.py
+++ b/solution.py
@@ -127,59 +127,53 @@
     return [high, mid, low]
 
 
-def start_kernel(key_ref, value_ref, resid_ref, query_ref, gate_ref, up_ref, sent_ref, w_ref):
+def start_kernel(key_ref, value_ref, gate_ref, up_ref, mixed_ref, w_ref):
     w_ref[0] = gate_ref[...]
     w_ref[1] = up_ref[...]
-    n_ctx = sent_ref.shape[0]
-    own = key_ref.shape[1] // n_ctx
     mixed = (key_ref[...].astype(f32) * value_ref[...].astype(f32)).astype(bf16)
-    parts = [mixed.astype(f32).T, resid_ref[...].astype(f32).T, query_ref[...].astype(f32).T]
-    for peer in range(n_ctx):
-        rows = slice(peer * own, (peer + 1) * own)
-        sent_ref[peer] = jnp.concatenate([part[rows] for part in parts]).astype(bf16)
+    mixed_ref[...] = mixed.astype(f32).T.astype(bf16)
+
+
+def reload_kernel(mark_ref, *refs):
+    half = len(refs) // 2
+    for source, copy in zip(refs[:half], refs[half:]):
+        copy[...] = source[...]
 
 
 def filter_kernel(filt_ref, *refs):
-    n_kept = (len(refs) - 2) // 2
-    kept, (re_ref, im_ref), copies = refs[:n_kept], refs[n_kept : n_kept + 2], refs[n_kept + 2 :]
+    n_kept = (len(refs) - 4) // 2
+    kept, spectra, copies = refs[:n_kept], refs[n_kept : n_kept + 4], refs[n_kept + 4 :]
     for source, copy in zip(kept, copies):
         copy[...] = source[...]
     tables = read_tables(kept[:7])
     lanes = kept[0].shape[1]
     blocks = filt_ref.shape[1] // lanes
     signal = jnp.concatenate([filt_ref[:, a * lanes : (a + 1) * lanes] for a in range(blocks)])
-    re_ref[...], im_ref[...] = to_spectrum(signal, tables, False)
-
-
-def conv_kernel(met_ref, gain_ref, fre_ref, fim_ref, *refs):
+    real, imag = to_spectrum(signal, tables, False)
+    for k in range(2):
+        spectra[2 * k][...], spectra[2 * k + 1][...] = real, imag
+
+
+def conv_kernel(src_ref, fre_ref, fim_ref, *refs):
     tables = read_tables(refs[:7])
-    conv_ref, sre_ref, sim_ref, piece_ref = refs[7:]
-    n_ctx = met_ref.shape[0]
-    own = conv_ref.shape[0] // n_ctx
-    blocks = [met_ref[k].astype(f32) for k in range(n_ctx)]
-    source, resid, query = (
-        jnp.concatenate([block[p * own : (p + 1) * own] for block in blocks]) for p in range(3)
-    )
-    real, imag = to_spectrum(source, tables, True)
+    conv_ref, sre_ref, sim_ref = refs[7:]
+    real, imag = to_spectrum(src_ref[...], tables, True)
     sre_ref[...], sim_ref[...] = real, imag
     fre, fim = fre_ref[...], fim_ref[...]
-    conv = from_spectrum(real * fre - imag * fim, real * fim + imag * fre, tables).astype(bf16)
-    conv_ref[...] = conv
-    piece_ref[...] = ((resid + query * conv.astype(f32)) * gain_ref[...]).astype(bf16)
-
-
-def resid_kernel(conv_ref, resid_ref, query_ref, gain_ref, piece_ref, sent_ref, r_ref):
+    conv = from_spectrum(real * fre - imag * fim, real * fim + imag * fre, tables)
+    conv_ref[...] = conv.astype(bf16)
+
+
+def resid_kernel(conv_ref, resid_ref, query_ref, gain_ref, sent_ref, r_ref):
     chans, tokens = conv_ref.shape
     resid = resid_ref[...].astype(f32).T + query_ref[...].astype(f32).T * conv_ref[...].astype(f32)
     r_ref[...] = resid
     scaled = (resid * gain_ref[...]).astype(bf16)
     square = jnp.sum(resid * resid, axis=0, keepdims=True)
     extra = jnp.concatenate(split_rows(square) + [jnp.zeros((EXTRA - 3, tokens), f32)]).astype(bf16)
-    piece = piece_ref[...]
     for peer in range(sent_ref.shape[0]):
         sent_ref[peer, :chans] = scaled
-        sent_ref[peer, chans : chans + EXTRA] = extra
-        sent_ref[peer, chans + EXTRA :] = piece
+        sent_ref[peer, chans:] = extra
 
 
 def load_weights(w_ref, w_vmem, sems):
@@ -192,9 +186,11 @@
 
 
 def hidden_kernel(
-    met_ref, w_ref, grad_ref, r_ref, gain_ref, d_ref, hid_ref, inv_ref, extra_ref, w_vmem, sems
+    met_ref, w_ref, grad_ref, r_ref, gain_ref, d_ref, hid_ref, inv_ref, extra_ref, w_vmem, grad_vmem, sems, grad_sem
 ):
     copies = load_weights(w_ref, w_vmem, sems)
+    grad_copy = pltpu.make_async_copy(grad_ref, grad_vmem, grad_sem)
+    grad_copy.start()
     n_ch, _, tokens = met_ref.shape
     chans = r_ref.shape[0]
     per = w_ref.shape[3] // chans
@@ -215,13 +211,15 @@
         up = part if up is None else up + part
     gate, up = gate * inv, up * inv
     sigma = 1.0 / (1.0 + jnp.exp(-gate))
-    hid = grad_ref[...].astype(f32)
+    grad_copy.wait()
+    hid = grad_vmem[...].astype(f32)
     d_gate = hid * up * sigma * (1.0 + gate * (1.0 - sigma))
     d_up = hid * gate * sigma
     d_ref[0] = (d_gate * inv).astype(bf16)
     d_ref[1] = (d_up * inv).astype(bf16)
-    hid_ref[0] = d_gate.astype(bf16)
-    hid_ref[1] = d_up.astype(bf16)
+    rest = jnp.zeros((hid_ref.shape[2] - d_gate.shape[0], tokens), f32)
+    for half, part in enumerate((d_gate, d_up)):
+        hid_ref[half] = jnp.concatenate([part, rest]).T.astype(bf16)
     inner = jnp.sum(d_gate * gate + d_up * up, axis=0, keepdims=True)
     extra_ref[...] = jnp.concatenate(
         split_rows(inner)
@@ -230,53 +228,64 @@
     ).astype(bf16)
 
 
-def back_kernel(w_ref, hid_ref, extra_ref, sent_ref, w_vmem, sent_vmem, sems, sent_sems):
+def back_kernel(w_ref, hid_ref, extra_ref, sent_ref, w_vmem, sems):
     arrivals = load_weights(w_ref, w_vmem, sems)
-    n_ch, padded, chans = sent_ref.shape
-    tokens = padded - EXTRA
-    per = w_ref.shape[3] // chans
-    extra = extra_ref[...]
-    parts = sent_sems.shape[0]
-    share = n_ch // parts
-    copies = []
-    for i, arrival in enumerate(arrivals):
-        arrival.wait()
-        term = 0.0
-        for half in range(2):
-            term = term + lax.dot_general(
-                hid_ref[half],
-                w_vmem[i, half],
-                (((0,), (0,)), ((), ())),
-                preferred_element_type=f32,
-            )
-        term = term.astype(bf16)
+    tokens = hid_ref.shape[1]
+    cores, _, chans = sent_ref.shape
+    n_ctx, _, hidden, rows = w_ref.shape
+    per = rows // chans
+    terms = n_ctx * per // cores * tokens
+    for core in range(cores):
+        sent_ref[core, terms:] = extra_ref[...]
+    d_gate, d_up = (hid_ref[half][:, :hidden] for half in range(2))
+    step = 4
+    for i in range(n_ctx):
+        if i % step == 0:
+            for arrival in arrivals[i : i + step]:
+                arrival.wait()
+        term = (dot(d_gate, w_vmem[i, 0]) + dot(d_up, w_vmem[i, 1])).astype(bf16)
         for k in range(per):
-            sent_vmem[i * per + k, :tokens] = term[:, k * chans : (k + 1) * chans]
-            sent_vmem[i * per + k, tokens:] = extra
-        done = (i + 1) * per
-        if done % share == 0:
-            copy = pltpu.make_async_copy(
-                sent_vmem.at[done - share : done],
-                sent_ref.at[done - share : done],
-                sent_sems.at[done // share - 1],
-            )
-            copy.start()
-            copies.append(copy)
-    for copy in copies:
-        copy.wait()
+            pair_at, core = divmod(i * per + k, cores)
+            sent_ref[core, pair_at * tokens : (pair_at + 1) * tokens] = term[
+                :, k * chans : (k + 1) * chans
+            ]
+
+
+def add_kernel(tokens, met_ref, piece_ref, sent_ref):
+    cores, _, chans = met_ref.shape
+    pairs = sent_ref.shape[0]
+    terms = pairs * tokens
+    piece = piece_ref[...]
+    inner, peak = None, None
+    for core in range(cores):
+        extra = met_ref[core, terms : terms + EXTRA].astype(f32)[:8]
+        part = extra[0:1] + extra[1:2] + extra[2:3]
+        top = extra[3:4] + extra[4:5] + extra[5:6]
+        inner = part if inner is None else inner + part
+        peak = top if peak is None else jnp.maximum(peak, top)
+    extra = jnp.concatenate(
+        split_rows(inner) + split_rows(peak) + [jnp.zeros((EXTRA - 6, chans), f32)]
+    ).astype(bf16)
+    for q in range(pairs):
+        total = met_ref[0, q * tokens : (q + 1) * tokens].astype(f32)
+        for core in range(1, cores):
+            total = total + met_ref[core, q * tokens : (q + 1) * tokens].astype(f32)
+        sent_ref[q, :tokens] = total.astype(bf16)
+        sent_ref[q, tokens : tokens + EXTRA] = extra
+        sent_ref[q, tokens + EXTRA :] = piece
 
 
 def norm_kernel(
-    back_ref, r_ref, conv_ref, query_ref, gres_ref, gain_ref, inv_ref, dx_ref, dq_ref, sent_ref
+    width, back_ref, r_ref, conv_ref, query_ref, gres_ref, gain_ref, inv_ref, dx_ref, dq_ref, sent_ref, mark_ref
 ):
-    n_ch = back_ref.shape[0]
+    peers = back_ref.shape[0]
     chans, tokens = r_ref.shape
     n_ctx = sent_ref.shape[0]
     own = chans // n_ctx
     total = back_ref[0, :tokens].astype(f32)
     extra = back_ref[0, tokens : tokens + EXTRA].astype(f32)[:8]
     inner, peak = extra[0:1] + extra[1:2] + extra[2:3], extra[3:4] + extra[4:5] + extra[5:6]
-    for peer in range(1, n_ch):
+    for peer in range(1, peers):
         total = total + back_ref[peer, :tokens].astype(f32)
         extra = back_ref[peer, tokens : tokens + EXTRA].astype(f32)[:8]
         inner = inner + (extra[0:1] + extra[1:2] + extra[2:3])
@@ -288,34 +297,32 @@
     d_resid = (
         gres_ref[...].astype(f32).T
         + (gain * d_norm) * inv
-        - resid * (inv * inv * inner / (n_ch * chans))
+        - resid * (inv * inv * inner / width)
     )
     dx_ref[...] = d_resid.T.astype(bf16)
     dq_ref[...] = (d_resid * conv_ref[...].astype(f32)).T.astype(bf16)
     d_conv = (d_resid * query_ref[...].astype(f32).T).astype(bf16).astype(f32)
     product = (d_norm * resid * inv).T
     gain_part = jnp.sum(product, axis=0, keepdims=True)
+    mark_ref[...] = gain_part
     extra = split_rows(gain_part) + split_rows(peak) + [jnp.zeros((2, chans), f32)]
     for peer in range(n_ctx):
         rows = slice(peer * own, (peer + 1) * own)
         sent_ref[peer] = jnp.concatenate([d_conv[rows]] + extra).astype(bf16)
 
 
-def rows_kernel(back_ref, out_ref):
-    n_ch = back_ref.shape[0]
-    lanes = back_ref.shape[2]
-    start = back_ref.shape[1] - lanes
-    blocks = out_ref.shape[1] // lanes
+def rows_kernel(own_ref, other_ref, out_ref):
+    peers, _, lanes = own_ref.shape
+    blocks = out_ref.shape[0] // lanes
     own = lanes // blocks
-    pair_of = EXTRA // own
-    for first in range(0, n_ch, pair_of):
-        parts = []
-        for peer in range(first, first + pair_of):
-            block = back_ref[peer, start:].astype(f32)
-            parts.append(
-                jnp.concatenate([block[a * own : (a + 1) * own] for a in range(blocks)], axis=1)
-            )
-        out_ref[first * own : (first + pair_of) * own] = jnp.concatenate(parts).astype(bf16)
+    first = lax.axis_index("ch") % 2 == 0
+    pieces = []
+    for peer in range(peers):
+        mine, theirs = own_ref[peer].astype(f32), other_ref[peer].astype(f32)
+        pieces += [jnp.where(first, mine, theirs), jnp.where(first, theirs, mine)]
+    for a in range(blocks):
+        part = jnp.concatenate([piece[a * own : (a + 1) * own] for piece in pieces])
+        out_ref[a * lanes : (a + 1) * lanes] = part.T.astype(bf16)
 
 
 def grad_kernel(back_ref, fre_ref, fim_ref, *refs):
@@ -342,10 +349,11 @@
 
 def filter_grad_kernel(gre_ref, gim_ref, sre_ref, sim_ref, *refs):
     tables = read_tables(refs[:7])
-    out_ref = refs[7]
+    out_ref, mark_ref = refs[7:]
     own = out_ref.shape[0]
     real, imag, sre, sim = gre_ref[...], gim_ref[...], sre_ref[...], sim_ref[...]
     grad = from_spectrum(real * sre + imag * sim, imag * sre - real * sim, tables)
+    mark_ref[...] = grad[:1]
     lanes = grad.shape[1]
     for a in range(out_ref.shape[1] // lanes):
         out_ref[:, a * lanes : (a + 1) * lanes] = grad[a * own : (a + 1) * own]
@@ -357,21 +365,19 @@
     dv_ref[...] = (grad * key_ref[...].astype(f32)).astype(bf16)
 
 
-def weight_kernel(d_ref, rows_ref, first_ref, second_ref, d_vmem, sems):
+def weight_kernel(d_ref, rows_ref, first_ref, second_ref, d_vmem, out_vmem, sems, out_sems):
     n_ctx, _, _, tokens = d_ref.shape
-    copies = load_weights(d_ref, d_vmem, sems)
-    acc = [0.0, 0.0]
-    for i in range(n_ctx):
-        copies[i].wait()
-        for half in range(2):
-            acc[half] = acc[half] + lax.dot_general(
-                d_vmem[i, half],
-                rows_ref[:, i * tokens : (i + 1) * tokens],
-                (((1,), (1,)), ((), ())),
-                preferred_element_type=f32,
-            )
-    first_ref[...] = acc[0]
-    second_ref[...] = acc[1]
+    for copy in load_weights(d_ref, d_vmem, sems):
+        copy.wait()
+    stores = []
+    for half, out_ref in enumerate((first_ref, second_ref)):
+        part = jnp.concatenate([d_vmem[i, half] for i in range(n_ctx)], axis=1)
+        out_vmem[half] = dot(part, rows_ref[...])
+        store = pltpu.make_async_copy(out_vmem.at[half], out_ref, out_sems.at[half])
+        store.start()
+        stores.append(store)
+    for store in stores:
+        store.wait()
 
 
 def on_device(resid_in, query_in, key_in, value_in, filt, gain, w_gate, w_up, g_hid, g_res):
@@ -388,103 +394,125 @@
         return pltpu.with_memory_space_constraint(array, pltpu.HBM)
 
     tables = [in_hbm(jnp.asarray(table)) for table in tables]
-    key_in, value_in, resid_in, query_in, g_res, filt = (
-        in_hbm(array) for array in (key_in, value_in, resid_in, query_in, g_res, filt)
+    query_near = query_in
+    key_in, value_in, resid_in, query_in, filt = (
+        in_hbm(array) for array in (key_in, value_in, resid_in, query_in, filt)
     )
     spectrum = ((spec_rows, tokens), f32)
     square = ((chans, tokens), bf16)
     gain_col = gain[:, None]
-    gain_own = jnp.tile(
-        lax.dynamic_slice_in_dim(gain_col, lax.axis_index("ctx") * own, own, 0), (n_ctx, 1)
-    )
-    groups = 4
-
-    weights_vmem = pltpu.VMEM((n_ctx, 2, hidden, rows), bf16)
-    weights_sems = pltpu.SemaphoreType.DMA((n_ctx,))
-    places = []
-    for i in range(n_ctx):
-        for j in range(n_ch):
-            block = i * n_ch + j
-            held_by = (block % n_ctx) * n_ch + block // n_ctx
-            places.append((held_by, block))
-
-    sent, w_both = call(
-        start_kernel,
-        [((n_ctx, 3 * own, tokens), bf16), ((2, hidden, rows), bf16)],
-        6,
-        hbm=(0, 1),
-    )(key_in, value_in, resid_in, query_in, in_hbm(w_gate.T), in_hbm(w_up.T))
+
+    mixed, w_both = call(start_kernel, [square, ((2, hidden, rows), bf16)], 4, hbm=(0, 1))(
+        key_in, value_in, in_hbm(w_gate.T), in_hbm(w_up.T)
+    )
     w_all = in_hbm(lax.all_gather(w_both, "ctx", axis=0, tiled=False))
-    met = lax.all_to_all(sent, "ctx", 0, 0, tiled=True)
-    kept = [*tables, key_in, value_in, resid_in, query_in, g_res]
-    fre, fim, *kept = call(
+    spread = lax.all_to_all(mixed.reshape(n_ctx, own, tokens), "ctx", 0, 0, tiled=True)
+    kept = [*tables, resid_in, query_in]
+    fre, fim, fre_far, fim_far, *kept = call(
         filter_kernel,
-        [spectrum] * 2 + [(array.shape, array.dtype) for array in kept],
+        [spectrum] * 4 + [(array.shape, array.dtype) for array in kept],
         len(kept) + 1,
-        vmem=range(len(kept) + 2),
+        vmem=(0, 1, *range(4, 4 + len(kept))),
+        hbm=(2, 3),
     )(filt, *kept)
-    tables = kept[:7]
-    key_in, value_in, resid_in, query_in, g_res = kept[7:]
-    conv, sre, sim, piece = call(conv_kernel, [square, spectrum, spectrum, square], 11, vmem=(1, 2))(
-        met, gain_own, fre, fim, *tables
-    )
-    piece = lax.ppermute(piece, ("ctx", "ch"), places)
+    conv, sre, sim = call(conv_kernel, [square, spectrum, spectrum], 10, hbm=(1, 2))(
+        spread.reshape(chans, tokens), fre, fim, *kept[:7]
+    )
     conv = lax.all_to_all(conv.reshape(n_ctx, own, tokens), "ctx", 0, 0, tiled=True).reshape(
         chans, tokens
     )
     sent, resid = call(
         resid_kernel,
-        [((n_ch, 2 * chans + EXTRA, tokens), bf16), ((chans, tokens), f32)],
-        5,
-    )(conv, resid_in, query_in, gain_col, piece)
+        [((n_ch, chans + EXTRA, tokens), bf16), ((chans, tokens), f32)],
+        4,
+    )(conv, *kept[7:], gain_col)
     met = lax.all_to_all(sent, "ch", 0, 0, tiled=True)
-    (row_acts,) = call(rows_kernel, [((rows, length), bf16)], 1)(met)
+    share = rows // n_ch
+    per = chans // share
+    my_ch = lax.axis_index("ch")
+    piece = lax.dynamic_slice(
+        met.reshape(n_ctx, n_ch // n_ctx, chans + EXTRA, tokens),
+        (0, my_ch // per, my_ch % per * share, 0),
+        (n_ctx, 1, share, tokens),
+    ).reshape(n_ctx, share, tokens)
+    piece = lax.all_to_all(piece, "ctx", 0, 0, tiled=True).reshape(n_ctx * share, tokens)
+    met, piece = lax.optimization_barrier((met, piece))
+    weights = (n_ctx, 2, hidden, rows)
     d_scaled, d_hid, inv, extra = call(
         hidden_kernel,
         [
             ((2, hidden, tokens), bf16),
-            ((2, hidden, tokens), bf16),
+            ((2, tokens, -(-hidden // 128) * 128), bf16),
             ((1, tokens), f32),
             ((EXTRA, tokens), bf16),
         ],
         5,
-        in_specs=[VMEM, HBM, VMEM, VMEM, VMEM],
-        scratch=[weights_vmem, weights_sems],
+        in_specs=[VMEM, HBM, HBM, VMEM, VMEM],
+        scratch=[
+            pltpu.VMEM(weights, bf16),
+            pltpu.VMEM((hidden, tokens), bf16),
+            pltpu.SemaphoreType.DMA((n_ctx,)),
+            pltpu.SemaphoreType.DMA(()),
+        ],
         flops=1e9,
-        limit=16,
+        limit=20,
+        hbm=(0,),
     )(met, w_all, in_hbm(g_hid.T), resid, gain_col)
     d_all = in_hbm(lax.all_gather(d_scaled, "ctx", axis=0, tiled=False))
-    sent_shape = (n_ch, tokens + EXTRA, chans)
+    cores = 2
+    pairs = n_ch // cores
+    piece_rows = n_ctx * share
     (sent,) = call(
         back_kernel,
-        [(sent_shape, bf16)],
+        [((cores, pairs * tokens + EXTRA, chans), bf16)],
         3,
         in_specs=[HBM, VMEM, VMEM],
-        out_specs=[HBM],
-        scratch=[
-            weights_vmem,
-            pltpu.VMEM(sent_shape, bf16),
-            weights_sems,
-            pltpu.SemaphoreType.DMA((groups,)),
+        scratch=[pltpu.VMEM(weights, bf16), pltpu.SemaphoreType.DMA((n_ctx,))],
+        flops=1e9,
+        limit=20,
+    )(w_all, d_hid, extra)
+    chip = [[q * cores + core for core in range(cores)] for q in range(pairs)]
+    plane = [[q * cores + core for q in range(pairs)] for core in range(cores)]
+    met = lax.all_to_all(sent, "ch", 0, 0, tiled=True, axis_index_groups=chip)
+    (sent,) = call(
+        functools.partial(add_kernel, tokens),
+        [((pairs, tokens + EXTRA + piece_rows, chans), bf16)],
+        2,
+        limit=16,
+    )(met, piece)
+    back = lax.all_to_all(sent, "ch", 0, 0, tiled=True, axis_index_groups=plane)
+    dx, dq, sent, mark = call(
+        functools.partial(norm_kernel, chans * n_ch),
+        [
+            ((tokens, chans), bf16),
+            ((tokens, chans), bf16),
+            ((n_ctx, 2 * own, tokens), bf16),
+            ((1, chans), f32),
         ],
-        flops=1e9,
-        limit=16,
-    )(w_all, d_hid, extra)
-    back = lax.all_to_all(sent, "ch", 0, 0, tiled=True)
-    dx, dq, sent = call(
-        norm_kernel,
-        [((tokens, chans), bf16), ((tokens, chans), bf16), ((n_ctx, 2 * own, tokens), bf16)],
         7,
-    )(back, resid, conv, query_in, g_res, gain_col, inv)
+    )(back, resid, conv, query_near, g_res, gain_col, inv)
+    kept = [fre_far, fim_far, *tables]
+    kept = call(
+        reload_kernel,
+        [(array.shape, array.dtype) for array in kept],
+        len(kept) + 1,
+        vmem=range(len(kept)),
+    )(mark, *(in_hbm(array) for array in kept))
+    mine = back[:, tokens + EXTRA :]
     back = lax.all_to_all(sent, "ctx", 0, 0, tiled=True)
     ds, gre, gim, dgain, amax = call(
         grad_kernel,
         [square, spectrum, spectrum, ((1, chans), f32), ((1, 1), f32)],
         10,
-        vmem=(1, 2),
-    )(back, fre, fim, *tables)
+        hbm=(1, 2),
+    )(back, *kept)
     ds = lax.all_to_all(ds.reshape(n_ctx, own, tokens), "ctx", 0, 0, tiled=True)
-    (dfilt,) = call(filter_grad_kernel, [(filt.shape, f32)], 11)(gre, gim, sre, sim, *tables)
+    dfilt, mark = call(filter_grad_kernel, [(filt.shape, f32), ((1, tokens), f32)], 11)(
+        *(in_hbm(array) for array in (gre, gim, sre, sim)), *tables
+    )
+    mine, mark = lax.optimization_barrier((mine, mark))
+    theirs = lax.ppermute(mine, "ch", [(j, j + 1 - 2 * (j % 2)) for j in range(n_ch)])
+    (row_acts,) = call(rows_kernel, [((length, rows), bf16)], 2)(mine, theirs)
     dk, dv = call(products_kernel, [((tokens, chans), bf16)] * 2, 3)(
         ds.reshape(chans, tokens), key_in, value_in
     )
@@ -493,7 +521,14 @@
         [((hidden, rows), f32)] * 2,
         2,
         in_specs=[HBM, VMEM],
-        scratch=[pltpu.VMEM((n_ctx, 2, hidden, tokens), bf16), pltpu.SemaphoreType.DMA((n_ctx,))],
+        out_specs=[HBM, HBM],
+        scratch=[
+            pltpu.VMEM((n_ctx, 2, hidden, tokens), bf16),
+            pltpu.VMEM((2, hidden, rows), f32),
+            pltpu.SemaphoreType.DMA((n_ctx,)),
+            pltpu.SemaphoreType.DMA((2,)),
+        ],
+        hbm=(0, 1),
         flops=1e9,
         limit=16,
     )(d_all, row_acts)

time: 196 us -> 193 us (0.985)
  blocking collectives: 93.2 us -> 46.9 us
  waiting for transfers between devices: 21.7 us -> 58.6 us
  starting transfers between devices: 31.4 us -> 44.6 us
  local copies, waits for them, and re-layouts: 7.73 us -> 0.18 us
    all_to_all x3, blocking collectives: 93.2 us -> 46.9 us  [the longest x1 23.6 us: on_device(): back = lax.all_to_all(sent, 'ch', 0, 0, tiled=True, axis_index_groups=plane)]
    all_to_all x1 -> x3, waiting for transfers between devices: 9.04 us -> 37.9 us  [the longest x1 17.6 us: on_device(): met = lax.all_to_all(sent, 'ch', 0, 0, tiled=True)]
    all_to_all x1 -> x3, starting transfers between devices: 15.8 us -> 33.3 us  [the longest x1 15.8 us: on_device(): lax.all_to_all(mixed.reshape(n_ctx, own, tokens), 'ctx', 0, 0, tiled=True)]
    all_to_all x1, waiting for transfers between devices: 3.4 us -> 11.4 us  [on_device(): lax.all_to_all(conv.reshape(n_ctx, own, tokens), 'ctx', 0, 0, tiled=True)]
    unnamed x46 -> x6, local copies, waits for them, and re-layouts: 6.81 us -> 0.02 us
    ppermute x1, starting transfers between devices: 6.25 us -> 3.71 us  [on_device(): lax.ppermute(mine, 'ch', [(j, j + 1 - 2 * (j % 2)) for j in range(n_ch)])]
    pallas_call x9 -> x11, Pallas kernels: 19.5 us -> 20.1 us  [the longest x1 4.33 us: on_device(): call(hidden_kernel, [((2, hidden, tokens), bf16), ((2, tokens, -(-hidden...]
  transfers between devices with their start and end apart: 6 -> 8, of which waited for: 4 -> 5; matrix products, arithmetic and copies ran while one was open for 0% -> 0% of each run, Pallas kernels for 8% -> 9%
where the time goes in v3:
time: 193 us; the launch traced here: 192 us
  waiting for transfers between devices  58.6 us (30%)
  blocking collectives  46.9 us (24%)
  starting transfers between devices  44.6 us (23%)
  Pallas kernels  27.2 us (14%)
  between operations  14.2 us (7%)
    all_to_all x1, blocking collectives, on_device(): back = lax.all_to_all(sent, 'ch', 0, 0, tiled=True, axis_index_groups=plane)  23.6 us
    all_to_all x1, waiting for transfers between devices, on_device(): met = lax.all_to_all(sent, 'ch', 0, 0, tiled=True)  17.6 us
    all_to_all x1, starting transfers between devices, on_device(): lax.all_to_all(mixed.reshape(n_ctx, own, tokens), 'ctx', 0, 0, tiled=True)  15.8 us
    all_to_all x1, blocking collectives, on_device(): lax.all_to_all(piece, 'ctx', 0, 0, tiled=True)  14 us
    all_to_all x1, waiting for transfers between devices, on_device(): lax.all_to_all(conv.reshape(n_ctx, own, tokens), 'ctx', 0, 0, tiled=True)  11.4 us
    all_to_all x1, waiting for transfers between devices, on_device(): back = lax.all_to_all(sent, 'ctx', 0, 0, tiled=True)  11.4 us
    all_to_all x1, starting transfers between devices, on_device(): met = lax.all_to_all(sent, 'ch', 0, 0, tiled=True)  10.6 us
    all_to_all x1, blocking collectives, on_device(): met = lax.all_to_all(sent, 'ch', 0, 0, tiled=True, axis_index_groups=chip)  9.36 us
  transfers between devices with their start and end apart: 8, of which 5 were waited for; matrix products, arithmetic and copies ran while one was open for 0% of the time, Pallas kernels for 9%

profile of v3, /device:TPU:1, one launch (start us, length us, event | category | flops | bytes accessed | tf_op | source)
XLA Modules:
  0.0 191.7 jit_solution(13528735825532630502)
XLA Ops:
  7.2 0.0 all-gather.5.cloned.1.call-start
  7.2 1.8 shard_map.232
  9.1 15.8 %all-to-all-start = ((bf16[16,8,128]{2,1,0:T(8,128)(2,1)}), bf16[16,8,128]{2,1,0:T(8,128)(2,1)S(1)}, u32[]{:S(2)}, u32[]{:S(2)}) async-start(bf16[16,8,128]{2,1,0:T(8,128)(2,1)} %bitcast.32), calls=%async_computation | async-start | bytes 65536 | tf_op jit(solution)/shard_map/all_to_all | solution.py:409
  24.8 2.5 %shard_map.233 = (f32[136,128]{1,0:T(8,128)S(1)}, f32[136,128]{1,0:T(8,128)S(1)}, f32[136,128]{1,0:T(8,128)}, f32[136,128]{1,0:T(8,128)}, bf16[272,128]{1,0:T(8,...) custom-call(f32[8,2048]{1,0:T(8,128)} %filt_ref.1, ...), custom_call_target="tpu_custom_call" | custom-call | flops 100000000 | bytes 1048576 | tf_op jit(solution)/shard_map/pallas_call | solution.py:411
  27.4 8.9 %all-to-all-done = bf16[16,8,128]{2,1,0:T(8,128)(2,1)S(1)} async-done(((bf16[16,8,128]{2,1,0:T(8,128)(2,1)}), bf16[16,8,128]{2,1,0:T(8,128)(2,1)S(1)}, u32[]{:S(2)}, u32[]{:S(2)}) %all-to-all-start) | async-done | bytes 32800 | tf_op jit(solution)/shard_map/all_to_all | solution.py:409
  36.3 1.8 shard_map.234
  38.1 3.5 %all-to-all-start.1 = ((bf16[16,8,128]{2,1,0:T(8,128)(2,1)}), bf16[16,8,128]{2,1,0:T(8,128)(2,1)S(1)}, u32[]{:S(2)}, u32[]{:S(2)}) async-start(bf16[16,8,128]{2,1,0:T(8,128)(2,1)} %bitcast.5), calls=%async_computation.1 | async-start | bytes 65536 | tf_op jit(solution)/shard_map/all_to_all | solution.py:421
  41.6 0.1 copy.29.gain_ref
  41.7 11.4 %all-to-all-done.1 = bf16[16,8,128]{2,1,0:T(8,128)(2,1)S(1)} async-done(((bf16[16,8,128]{2,1,0:T(8,128)(2,1)}), bf16[16,8,128]{2,1,0:T(8,128)(2,1)S(1)}, u32[]{:S(2)}, u32[]{:S(2)}) %all-to-all-start.1) | async-done | bytes 32800 | tf_op jit(solution)/shard_map/all_to_all | solution.py:421
  53.2 1.2 shard_map.235
  54.4 10.6 %all-to-all-start.2 = ((bf16[32,144,128]{2,1,0:T(8,128)(2,1)}), bf16[32,144,128]{2,1,0:T(8,128)(2,1)S(1)}, u32[]{:S(2)}, u32[]{:S(2)}) async-start(bf16[32,144,128]{2,1,0:T(8,128)(2,1)} %get-tuple-element.72), calls=%async_computation.2 | async-start | bytes 2359296 | tf_op jit(solution)/shard_map/all_to_all | solution.py:429
  65.0 0.0 all-gather.7.cloned.1.call-start
  65.0 17.6 %all-to-all-done.2.met_ref = bf16[32,144,128]{2,1,0:T(8,128)(2,1)S(1)} async-done(((bf16[32,144,128]{2,1,0:T(8,128)(2,1)}), bf16[32,144,128]{2,1,0:T(8,128)(2,1)S(1)}, u32[]{:S(2)}, u32[]{:S(2)}) %all-to-all-start.2) | async-done | bytes 1179680 | tf_op jit(solution)/shard_map/all_to_all | solution.py:429
  82.7 14.0 %all_to_all.40 = bf16[16,8,128]{2,1,0:T(8,128)(2,1)S(1)} all-to-all(bf16[16,8,128]{2,1,0:T(8,128)(2,1)S(1)} %dynamic-slice_bitcast_fusion), channel_id=1, replica_groups=mesh['ctx'=16,'ch'=32] {'ctx'}, dimensions={0} | all-to-all | bytes 65536 | tf_op jit(solution)/shard_map/all_to_all | solution.py:438
  96.6 4.3 %shard_map.236 = (bf16[2,344,128]{2,1,0:T(8,128)(2,1)}, bf16[2,128,384]{2,1,0:T(8,128)(2,1)S(1)}, f32[1,128]{1,0:T(1,128)S(1)}, bf16[16,128]{1,0:T(8,128)(2,1)S(1)}) custom-call(bf16[32,144,128]{2,1,0:T(8,128)(2,1)S(1)} %all-to-all-done.2.met_ref, bf16[16,2,344,256]{3,2,1,0:T(8,128)(2,1)} %bitcast.26, bf16[344,128]{1,0:T(8,128)(2,1)} %bitcast.31, ...), custom_call_target="tpu_custom_call" | custom-call | flops 1000000000 | bytes 1048576 | tf_op jit(solution)/shard_map/pallas_call | solution.py:441
  101.0 3.2 %shard_map.237 = bf16[2,2064,128]{2,1,0:T(8,128)(2,1)S(1)} custom-call(bf16[16,2,344,256]{3,2,1,0:T(8,128)(2,1)} %bitcast.27, bf16[2,128,384]{2,1,0:T(8,128)(2,1)S(1)} %get-tuple-element.75.hid_ref, bf16[16,128]{1,0:T(8,128)(2,1)S(1)} %get-tuple-element.76.extra_ref), custom_call_target="tpu_custom_call" | custom-call | flops 1000000000 | bytes 1048576 | tf_op jit(solution)/shard_map/pallas_call | solution.py:465
  104.2 9.4 %all_to_all.41.met_ref = bf16[2,2064,128]{2,1,0:T(8,128)(2,1)S(1)} all-to-all(bf16[2,2064,128]{2,1,0:T(8,128)(2,1)S(1)} %shard_map.237), channel_id=1, replica_groups={{0,1},{2,3},{4,5},{6,7},{8,9},{10,11},{12,13},{14,15},{16,17},{18,19},{..., dimensions={0} | all-to-all | bytes 2113536 | tf_op jit(solution)/shard_map/all_to_all | solution.py:476
  113.6 0.2 shard_map.238
  113.8 23.6 %all_to_all.42.back_ref = bf16[16,272,128]{2,1,0:T(8,128)(2,1)S(1)} all-to-all(bf16[16,272,128]{2,1,0:T(8,128)(2,1)S(1)} %shard_map.238), channel_id=1, replica_groups={{0,2,4,6,8,10,12,14,16,18,20,22,24,26,28,30},{1,3,5,7,9,11,13,15,17,19,..., dimensions={0} | all-to-all | bytes 2228224 | tf_op jit(solution)/shard_map/all_to_all | solution.py:483
  137.4 3.7 %collective-permute-start = (bf16[16,128,128]{2,1,0:T(8,128)(2,1)S(1)}, bf16[16,128,128]{2,1,0:T(8,128)(2,1)S(1)}, u32[]{:S(2)}, u32[]{:S(2)}) collective-permute-start(bf16[16,128,128]{2,1,0:T(8,128)(2,1)S(1)} %slice.4.own_ref), channel_id=1, source_target_pairs={{0,1},{1,0},{2,3},{3,2},{4,5},{5,4},{6,7},{7,6},{8,9},{9,8},{10,11... | collective-permute-start | bytes 1572872 | tf_op jit(solution)/shard_map/ppermute | solution.py:514
  141.2 0.9 shard_map.239
  142.0 7.0 %all-to-all-start.6 = ((bf16[16,16,128]{2,1,0:T(8,128)(2,1)}), bf16[16,16,128]{2,1,0:T(8,128)(2,1)S(1)}, u32[]{:S(2)}, u32[]{:S(2)}) async-start(bf16[16,16,128]{2,1,0:T(8,128)(2,1)} %get-tuple-element.81), calls=%async_computation.6 | async-start | bytes 131072 | tf_op jit(solution)/shard_map/all_to_all | solution.py:502
  149.0 1.3 shard_map.240
  150.3 11.4 %all-to-all-done.6.back_ref = bf16[16,16,128]{2,1,0:T(8,128)(2,1)S(1)} async-done(((bf16[16,16,128]{2,1,0:T(8,128)(2,1)}), bf16[16,16,128]{2,1,0:T(8,128)(2,1)S(1)}, u32[]{:S(2)}, u32[]{:S(2)}) %all-to-all-start.6) | async-done | bytes 65568 | tf_op jit(solution)/shard_map/all_to_all | solution.py:502
  161.7 1.8 shard_map.241
  163.5 4.0 %all-to-all-start.7 = ((bf16[16,8,128]{2,1,0:T(8,128)(2,1)}), bf16[16,8,128]{2,1,0:T(8,128)(2,1)S(1)}, u32[]{:S(2)}, u32[]{:S(2)}) async-start(bf16[16,8,128]{2,1,0:T(8,128)(2,1)} %bitcast.12), calls=%async_computation.7 | async-start | bytes 65536 | tf_op jit(solution)/shard_map/all_to_all | solution.py:509
  167.5 2.5 %shard_map.243 = (f32[8,2048]{1,0:T(8,128)}, f32[1,128]{1,0:T(1,128)}) custom-call(f32[136,128]{1,0:T(8,128)} %get-tuple-element.97.gre_ref, f32[136,128]{1,0:T(8,128)} %get-tuple-element.98.gim_ref, f32[136,128]{1,0:T(8,128)} %get-tuple-element.99.sre_ref, f32[136,128]{1,0:T(8,128)} %get-tuple-element.100.sim_ref, ...), custom_call_target="tpu_custom_call" | custom-call | flops 100000000 | bytes 1048576 | tf_op jit(solution)/shard_map/pallas_call | solution.py:510
  170.0 9.2 %all-to-all-done.7 = bf16[16,8,128]{2,1,0:T(8,128)(2,1)S(1)} async-done(((bf16[16,8,128]{2,1,0:T(8,128)(2,1)}), bf16[16,8,128]{2,1,0:T(8,128)(2,1)S(1)}, u32[]{:S(2)}, u32[]{:S(2)}) %all-to-all-start.7) | async-done | bytes 32800 | tf_op jit(solution)/shard_map/all_to_all | solution.py:509
  179.2 1.5 shard_map.242
  180.7 0.4 shard_map.244.rows_ref
  181.1 0.0 all-gather.7.cloned.1.call-done
  181.1 3.7 %shard_map.245 = (f32[344,256]{1,0:T(8,128)}, f32[344,256]{1,0:T(8,128)}) custom-call(bf16[16,2,344,128]{3,2,1,0:T(8,128)(2,1)} %bitcast.28, bf16[2048,256]{1,0:T(8,128)(2,1)S(1)} %shard_map.244.rows_ref), custom_call_target="tpu_custom_call" | custom-call | flops 1000000000 | bytes 1048576 | tf_op jit(solution)/shard_map/pallas_call | solution.py:519
  (12 shorter events, 0.1 us)
Async XLA Ops:
  7.2 89.5 %all-gather.5.cloned.1.call-start = ((), (), s32[]{:S(2)}) async-start(), calls=%async_computation.8 | async-start | bytes 5988352 | tf_op jit(solution)/shard_map/all_gather | solution.py:408
  7.2 34.4 %copy-start.2 = (f32[128]{0:T(128)S(1)}, f32[128]{0:T(128)}, u32[]{:S(2)}) copy-start(f32[128]{0:T(128)} %param.22) | copy-start | bytes 1540
  9.1 27.2 %all-to-all-start = ((bf16[16,8,128]{2,1,0:T(8,128)(2,1)}), bf16[16,8,128]{2,1,0:T(8,128)(2,1)S(1)}, u32[]{:S(2)}, u32[]{:S(2)}) async-start(bf16[16,8,128]{2,1,0:T(8,128)(2,1)} %bitcast.32), calls=%async_computation | async-start | bytes 65536 | tf_op jit(solution)/shard_map/all_to_all | solution.py:409
  38.1 15.1 %all-to-all-start.1 = ((bf16[16,8,128]{2,1,0:T(8,128)(2,1)}), bf16[16,8,128]{2,1,0:T(8,128)(2,1)S(1)}, u32[]{:S(2)}, u32[]{:S(2)}) async-start(bf16[16,8,128]{2,1,0:T(8,128)(2,1)} %bitcast.5), calls=%async_computation.1 | async-start | bytes 65536 | tf_op jit(solution)/shard_map/all_to_all | solution.py:421
  54.4 28.3 %all-to-all-start.2 = ((bf16[32,144,128]{2,1,0:T(8,128)(2,1)}), bf16[32,144,128]{2,1,0:T(8,128)(2,1)S(1)}, u32[]{:S(2)}, u32[]{:S(2)}) async-start(bf16[32,144,128]{2,1,0:T(8,128)(2,1)} %get-tuple-element.72), calls=%async_computation.2 | async-start | bytes 2359296 | tf_op jit(solution)/shard_map/all_to_all | solution.py:429
  65.0 116.1 %all-gather.7.cloned.1.call-start = ((), (), s32[]{:S(2)}) async-start(), calls=%async_computation.9 | async-start | bytes 2994176 | tf_op jit(solution)/shard_map/all_gather | solution.py:461
  113.8 27.4 %copy-start = (bf16[128,128]{1,0:T(8,128)(2,1)S(1)}, bf16[128,128]{1,0:T(8,128)(2,1)}, u32[]{:S(2)}) copy-start(bf16[128,128]{1,0:T(8,128)(2,1)} %query_ref.1) | copy-start | bytes 98308
  113.8 27.4 %copy-start.1 = (bf16[128,128]{1,0:T(8,128)(2,1)S(1)}, bf16[128,128]{1,0:T(8,128)(2,1)}, u32[]{:S(2)}) copy-start(bf16[128,128]{1,0:T(8,128)(2,1)} %gres_ref.1) | copy-start | bytes 98308
  137.4 43.3 %collective-permute-start = (bf16[16,128,128]{2,1,0:T(8,128)(2,1)S(1)}, bf16[16,128,128]{2,1,0:T(8,128)(2,1)S(1)}, u32[]{:S(2)}, u32[]{:S(2)}) collective-permute-start(bf16[16,128,128]{2,1,0:T(8,128)(2,1)S(1)} %slice.4.own_ref), channel_id=1, source_target_pairs={{0,1},{1,0},{2,3},{3,2},{4,5},{5,4},{6,7},{7,6},{8,9},{9,8},{10,11... | collective-permute-start | bytes 1572872 | tf_op jit(solution)/shard_map/ppermute | solution.py:514
  142.0 19.6 %all-to-all-start.6 = ((bf16[16,16,128]{2,1,0:T(8,128)(2,1)}), bf16[16,16,128]{2,1,0:T(8,128)(2,1)S(1)}, u32[]{:S(2)}, u32[]{:S(2)}) async-start(bf16[16,16,128]{2,1,0:T(8,128)(2,1)} %get-tuple-element.81), calls=%async_computation.6 | async-start | bytes 131072 | tf_op jit(solution)/shard_map/all_to_all | solution.py:502
  163.5 15.7 %all-to-all-start.7 = ((bf16[16,8,128]{2,1,0:T(8,128)(2,1)}), bf16[16,8,128]{2,1,0:T(8,128)(2,1)S(1)}, u32[]{:S(2)}, u32[]{:S(2)}) async-start(bf16[16,8,128]{2,1,0:T(8,128)(2,1)} %bitcast.12), calls=%async_computation.7 | async-start | bytes 65536 | tf_op jit(solution)/shard_map/all_to_all | solution.py:509
Sparse Core Ops, SparseCore 0:
  10.7 85.5 all-gather.4
  101.1 69.7 all-gather.6

commit v4 on v3

--- a/solution.py
+++ b/solution.py
@@ -17,7 +17,7 @@
 EXTRA = 16
 
 
-def call(body, outs, n_in, flops=1e8, in_specs=None, out_specs=None, scratch=(), limit=8, hbm=(), vmem=()):
+def call(body, outs, n_in, flops=1e3, in_specs=None, out_specs=None, scratch=(), limit=8, hbm=(), vmem=()):
     return pl.pallas_call(
         body,
         out_shape=tuple(
@@ -28,7 +28,7 @@
         out_specs=tuple(out_specs or [VMEM] * len(outs)),
         scratch_shapes=list(scratch),
         compiler_params=pltpu.CompilerParams(vmem_limit_bytes=limit * 2**20),
-        cost_estimate=pl.CostEstimate(flops=int(flops), bytes_accessed=2**20, transcendentals=0),
+        cost_estimate=pl.CostEstimate(flops=int(flops), bytes_accessed=int(flops / 1e3), transcendentals=0),
     )
 
 
@@ -217,9 +217,8 @@
     d_up = hid * gate * sigma
     d_ref[0] = (d_gate * inv).astype(bf16)
     d_ref[1] = (d_up * inv).astype(bf16)
-    rest = jnp.zeros((hid_ref.shape[2] - d_gate.shape[0], tokens), f32)
-    for half, part in enumerate((d_gate, d_up)):
-        hid_ref[half] = jnp.concatenate([part, rest]).T.astype(bf16)
+    hid_ref[0] = d_gate.astype(bf16)
+    hid_ref[1] = d_up.astype(bf16)
     inner = jnp.sum(d_gate * gate + d_up * up, axis=0, keepdims=True)
     extra_ref[...] = jnp.concatenate(
         split_rows(inner)
@@ -230,14 +229,18 @@
 
 def back_kernel(w_ref, hid_ref, extra_ref, sent_ref, w_vmem, sems):
     arrivals = load_weights(w_ref, w_vmem, sems)
-    tokens = hid_ref.shape[1]
+    tokens = hid_ref.shape[2]
     cores, _, chans = sent_ref.shape
     n_ctx, _, hidden, rows = w_ref.shape
     per = rows // chans
     terms = n_ctx * per // cores * tokens
     for core in range(cores):
         sent_ref[core, terms:] = extra_ref[...]
-    d_gate, d_up = (hid_ref[half][:, :hidden] for half in range(2))
+    rest = jnp.zeros((-hidden % 128, tokens), f32)
+    d_gate, d_up = (
+        jnp.concatenate([hid_ref[half].astype(f32), rest]).T.astype(bf16)[:, :hidden]
+        for half in range(2)
+    )
     step = 4
     for i in range(n_ctx):
         if i % step == 0:
@@ -349,11 +352,10 @@
 
 def filter_grad_kernel(gre_ref, gim_ref, sre_ref, sim_ref, *refs):
     tables = read_tables(refs[:7])
-    out_ref, mark_ref = refs[7:]
+    out_ref = refs[7]
     own = out_ref.shape[0]
     real, imag, sre, sim = gre_ref[...], gim_ref[...], sre_ref[...], sim_ref[...]
     grad = from_spectrum(real * sre + imag * sim, imag * sre - real * sim, tables)
-    mark_ref[...] = grad[:1]
     lanes = grad.shape[1]
     for a in range(out_ref.shape[1] // lanes):
         out_ref[:, a * lanes : (a + 1) * lanes] = grad[a * own : (a + 1) * own]
@@ -442,7 +444,7 @@
         hidden_kernel,
         [
             ((2, hidden, tokens), bf16),
-            ((2, tokens, -(-hidden // 128) * 128), bf16),
+            ((2, hidden, tokens), bf16),
             ((1, tokens), f32),
             ((EXTRA, tokens), bf16),
         ],
@@ -491,14 +493,22 @@
         ],
         7,
     )(back, resid, conv, query_near, g_res, gain_col, inv)
-    kept = [fre_far, fim_far, *tables]
-    kept = call(
-        reload_kernel,
-        [(array.shape, array.dtype) for array in kept],
-        len(kept) + 1,
-        vmem=range(len(kept)),
-    )(mark, *(in_hbm(array) for array in kept))
-    mine = back[:, tokens + EXTRA :]
+
+    def reload(mark, arrays):
+        return list(
+            call(
+                reload_kernel,
+                [(array.shape, array.dtype) for array in arrays],
+                len(arrays) + 1,
+                vmem=range(len(arrays)),
+            )(mark, *(in_hbm(array) for array in arrays))
+        )
+
+    mine, mark = lax.optimization_barrier((back[:, tokens + EXTRA :], mark))
+    kept = reload(mark, [fre_far, fim_far, *tables])
+    theirs = lax.ppermute(mine, "ch", [(j, j + 1 - 2 * (j % 2)) for j in range(n_ch)])
+    (row_acts,) = call(rows_kernel, [((length, rows), bf16)], 2)(mine, theirs)
+    kept[0], row_acts = lax.optimization_barrier((kept[0], row_acts))
     back = lax.all_to_all(sent, "ctx", 0, 0, tiled=True)
     ds, gre, gim, dgain, amax = call(
         grad_kernel,
@@ -507,14 +517,12 @@
         hbm=(1, 2),
     )(back, *kept)
     ds = lax.all_to_all(ds.reshape(n_ctx, own, tokens), "ctx", 0, 0, tiled=True)
-    dfilt, mark = call(filter_grad_kernel, [(filt.shape, f32), ((1, tokens), f32)], 11)(
+    (dfilt,) = call(filter_grad_kernel, [(filt.shape, f32)], 11)(
         *(in_hbm(array) for array in (gre, gim, sre, sim)), *tables
     )
-    mine, mark = lax.optimization_barrier((mine, mark))
-    theirs = lax.ppermute(mine, "ch", [(j, j + 1 - 2 * (j % 2)) for j in range(n_ch)])
-    (row_acts,) = call(rows_kernel, [((length, rows), bf16)], 2)(mine, theirs)
+    key_near, value_near = reload(dgain, [key_in, value_in])
     dk, dv = call(products_kernel, [((tokens, chans), bf16)] * 2, 3)(
-        ds.reshape(chans, tokens), key_in, value_in
+        ds.reshape(chans, tokens), key_near, value_near
     )
     first, second = call(
         weight_kernel,

time: 193 us -> 191 us (0.990)
    pallas_call x3 -> x4, Pallas kernels: 8.08 us -> 8.82 us  [the longest x1 4.3 us: on_device(): call(hidden_kernel, [((2, hidden, tokens), bf16), ((2, hidden, tokens), b...]
where the time goes in v4:
time: 191 us
  waiting for transfers between devices  56.8 us (30%)
  blocking collectives  46.9 us (25%)
  starting transfers between devices  44.6 us (23%)
  Pallas kernels  27.1 us (14%)
  between operations  14.2 us (7%)
    all_to_all x1, blocking collectives, on_device(): back = lax.all_to_all(sent, 'ch', 0, 0, tiled=True, axis_index_groups=plane)  23.6 us
    all_to_all x1, waiting for transfers between devices, on_device(): met = lax.all_to_all(sent, 'ch', 0, 0, tiled=True)  17.6 us
    all_to_all x1, starting transfers between devices, on_device(): lax.all_to_all(mixed.reshape(n_ctx, own, tokens), 'ctx', 0, 0, tiled=True)  15.8 us
    all_to_all x1, blocking collectives, on_device(): lax.all_to_all(piece, 'ctx', 0, 0, tiled=True)  14 us
    all_to_all x1, waiting for transfers between devices, on_device(): lax.all_to_all(conv.reshape(n_ctx, own, tokens), 'ctx', 0, 0, tiled=True)  11.4 us
    all_to_all x1, waiting for transfers between devices, on_device(): back = lax.all_to_all(sent, 'ctx', 0, 0, tiled=True)  10.9 us
    all_to_all x1, starting transfers between devices, on_device(): met = lax.all_to_all(sent, 'ch', 0, 0, tiled=True)  10.6 us
    all_to_all x1, blocking collectives, on_device(): met = lax.all_to_all(sent, 'ch', 0, 0, tiled=True, axis_index_groups=chip)  9.39 us
  transfers between devices with their start and end apart: 8, of which 5 were waited for; matrix products, arithmetic and copies ran while one was open for 0% of the time, Pallas kernels for 9%

profile of v4, /device:TPU:1, one launch (start us, length us, event | category | flops | bytes accessed | tf_op | source)
XLA Modules:
  0.0 190.6 jit_solution(832049603094925765)
XLA Ops:
  7.2 1.8 shard_map.232
  9.1 15.8 %all-to-all-start = ((bf16[16,8,128]{2,1,0:T(8,128)(2,1)}), bf16[16,8,128]{2,1,0:T(8,128)(2,1)S(1)}, u32[]{:S(2)}, u32[]{:S(2)}) async-start(bf16[16,8,128]{2,1,0:T(8,128)(2,1)} %bitcast.33), calls=%async_computation | async-start | bytes 65536 | tf_op jit(solution)/shard_map/all_to_all | solution.py:411
  24.8 2.5 %shard_map.233 = (f32[136,128]{1,0:T(8,128)S(1)}, f32[136,128]{1,0:T(8,128)S(1)}, f32[136,128]{1,0:T(8,128)}, f32[136,128]{1,0:T(8,128)}, bf16[272,128]{1,0:T(8,...) custom-call(f32[8,2048]{1,0:T(8,128)} %filt_ref.1, ...), custom_call_target="tpu_custom_call" | custom-call | flops 1000 | bytes 1 | tf_op jit(solution)/shard_map/pallas_call | solution.py:413
  27.4 8.9 %all-to-all-done = bf16[16,8,128]{2,1,0:T(8,128)(2,1)S(1)} async-done(((bf16[16,8,128]{2,1,0:T(8,128)(2,1)}), bf16[16,8,128]{2,1,0:T(8,128)(2,1)S(1)}, u32[]{:S(2)}, u32[]{:S(2)}) %all-to-all-start) | async-done | bytes 32800 | tf_op jit(solution)/shard_map/all_to_all | solution.py:411
  36.3 1.8 shard_map.234
  38.1 3.5 %all-to-all-start.1 = ((bf16[16,8,128]{2,1,0:T(8,128)(2,1)}), bf16[16,8,128]{2,1,0:T(8,128)(2,1)S(1)}, u32[]{:S(2)}, u32[]{:S(2)}) async-start(bf16[16,8,128]{2,1,0:T(8,128)(2,1)} %bitcast.5), calls=%async_computation.1 | async-start | bytes 65536 | tf_op jit(solution)/shard_map/all_to_all | solution.py:423
  41.6 0.1 copy.29.gain_ref
  41.7 11.4 %all-to-all-done.1 = bf16[16,8,128]{2,1,0:T(8,128)(2,1)S(1)} async-done(((bf16[16,8,128]{2,1,0:T(8,128)(2,1)}), bf16[16,8,128]{2,1,0:T(8,128)(2,1)S(1)}, u32[]{:S(2)}, u32[]{:S(2)}) %all-to-all-start.1) | async-done | bytes 32800 | tf_op jit(solution)/shard_map/all_to_all | solution.py:423
  53.2 1.2 shard_map.235
  54.4 10.6 %all-to-all-start.2 = ((bf16[32,144,128]{2,1,0:T(8,128)(2,1)}), bf16[32,144,128]{2,1,0:T(8,128)(2,1)S(1)}, u32[]{:S(2)}, u32[]{:S(2)}) async-start(bf16[32,144,128]{2,1,0:T(8,128)(2,1)} %get-tuple-element.77), calls=%async_computation.2 | async-start | bytes 2359296 | tf_op jit(solution)/shard_map/all_to_all | solution.py:431
  65.0 0.0 all-gather.7.cloned.1.call-start
  65.0 17.6 %all-to-all-done.2.met_ref = bf16[32,144,128]{2,1,0:T(8,128)(2,1)S(1)} async-done(((bf16[32,144,128]{2,1,0:T(8,128)(2,1)}), bf16[32,144,128]{2,1,0:T(8,128)(2,1)S(1)}, u32[]{:S(2)}, u32[]{:S(2)}) %all-to-all-start.2) | async-done | bytes 1179680 | tf_op jit(solution)/shard_map/all_to_all | solution.py:431
  82.7 14.0 %all_to_all.40 = bf16[16,8,128]{2,1,0:T(8,128)(2,1)S(1)} all-to-all(bf16[16,8,128]{2,1,0:T(8,128)(2,1)S(1)} %dynamic-slice_bitcast_fusion), channel_id=1, replica_groups=mesh['ctx'=16,'ch'=32] {'ctx'}, dimensions={0} | all-to-all | bytes 65536 | tf_op jit(solution)/shard_map/all_to_all | solution.py:440
  96.6 4.3 %shard_map.236 = (bf16[2,344,128]{2,1,0:T(8,128)(2,1)}, bf16[2,344,128]{2,1,0:T(8,128)(2,1)S(1)}, f32[1,128]{1,0:T(1,128)S(1)}, bf16[16,128]{1,0:T(8,128)(2,1)S(1)}) custom-call(bf16[32,144,128]{2,1,0:T(8,128)(2,1)S(1)} %all-to-all-done.2.met_ref, bf16[16,2,344,256]{3,2,1,0:T(8,128)(2,1)} %bitcast.27, bf16[344,128]{1,0:T(8,128)(2,1)} %bitcast.32, ...), custom_call_target="tpu_custom_call" | custom-call | flops 1000000000 | bytes 1000000 | tf_op jit(solution)/shard_map/pallas_call | solution.py:443
  101.0 3.2 %shard_map.237 = bf16[2,2064,128]{2,1,0:T(8,128)(2,1)S(1)} custom-call(bf16[16,2,344,256]{3,2,1,0:T(8,128)(2,1)} %bitcast.28, bf16[2,344,128]{2,1,0:T(8,128)(2,1)S(1)} %get-tuple-element.80.hid_ref, bf16[16,128]{1,0:T(8,128)(2,1)S(1)} %get-tuple-element.81.extra_ref), custom_call_target="tpu_custom_call" | custom-call | flops 1000000000 | bytes 1000000 | tf_op jit(solution)/shard_map/pallas_call | solution.py:467
  104.2 9.4 %all_to_all.41.met_ref = bf16[2,2064,128]{2,1,0:T(8,128)(2,1)S(1)} all-to-all(bf16[2,2064,128]{2,1,0:T(8,128)(2,1)S(1)} %shard_map.237), channel_id=1, replica_groups={{0,1},{2,3},{4,5},{6,7},{8,9},{10,11},{12,13},{14,15},{16,17},{18,19},{..., dimensions={0} | all-to-all | bytes 2113536 | tf_op jit(solution)/shard_map/all_to_all | solution.py:478
  113.6 0.2 shard_map.238
  113.8 23.6 %all_to_all.42.back_ref = bf16[16,272,128]{2,1,0:T(8,128)(2,1)S(1)} all-to-all(bf16[16,272,128]{2,1,0:T(8,128)(2,1)S(1)} %shard_map.238), channel_id=1, replica_groups={{0,2,4,6,8,10,12,14,16,18,20,22,24,26,28,30},{1,3,5,7,9,11,13,15,17,19,..., dimensions={0} | all-to-all | bytes 2228224 | tf_op jit(solution)/shard_map/all_to_all | solution.py:485
  137.4 0.9 shard_map.239
  138.3 3.7 %collective-permute-start = (bf16[16,128,128]{2,1,0:T(8,128)(2,1)S(1)}, bf16[16,128,128]{2,1,0:T(8,128)(2,1)S(1)}, u32[]{:S(2)}, u32[]{:S(2)}) collective-permute-start(bf16[16,128,128]{2,1,0:T(8,128)(2,1)S(1)} %slice.4.own_ref), channel_id=1, source_target_pairs={{0,1},{1,0},{2,3},{3,2},{4,5},{5,4},{6,7},{7,6},{8,9},{9,8},{10,11... | collective-permute-start | bytes 1572872 | tf_op jit(solution)/shard_map/ppermute | solution.py:509
  142.0 7.0 %all-to-all-start.6 = ((bf16[16,16,128]{2,1,0:T(8,128)(2,1)}), bf16[16,16,128]{2,1,0:T(8,128)(2,1)S(1)}, u32[]{:S(2)}, u32[]{:S(2)}) async-start(bf16[16,16,128]{2,1,0:T(8,128)(2,1)} %get-tuple-element.86), calls=%async_computation.6 | async-start | bytes 131072 | tf_op jit(solution)/shard_map/all_to_all | solution.py:512
  149.0 1.3 shard_map.240
  150.3 0.4 shard_map.241.rows_ref
  150.7 10.9 %all-to-all-done.6.back_ref = bf16[16,16,128]{2,1,0:T(8,128)(2,1)S(1)} async-done(((bf16[16,16,128]{2,1,0:T(8,128)(2,1)}), bf16[16,16,128]{2,1,0:T(8,128)(2,1)S(1)}, u32[]{:S(2)}, u32[]{:S(2)}) %all-to-all-start.6) | async-done | bytes 65568 | tf_op jit(solution)/shard_map/all_to_all | solution.py:512
  161.6 1.8 shard_map.242
  163.4 4.0 %all-to-all-start.7 = ((bf16[16,8,128]{2,1,0:T(8,128)(2,1)}), bf16[16,8,128]{2,1,0:T(8,128)(2,1)S(1)}, u32[]{:S(2)}, u32[]{:S(2)}) async-start(bf16[16,8,128]{2,1,0:T(8,128)(2,1)} %bitcast.12), calls=%async_computation.7 | async-start | bytes 65536 | tf_op jit(solution)/shard_map/all_to_all | solution.py:519
  167.5 0.6 copy-done.2
  168.1 0.8 shard_map.243
  168.9 2.5 %shard_map.245 = f32[8,2048]{1,0:T(8,128)} custom-call(f32[136,128]{1,0:T(8,128)} %get-tuple-element.108.gre_ref, f32[136,128]{1,0:T(8,128)} %get-tuple-element.109.gim_ref, f32[136,128]{1,0:T(8,128)} %get-tuple-element.110.sre_ref, f32[136,128]{1,0:T(8,128)} %get-tuple-element.111.sim_ref, bf16[272,128]{1,0:T(8,128)(2,1)} %constant.51.clone.refs_0_.refs_2_, ...), custom_call_target="tpu_custom_call" | custom-call | flops 1000 | bytes 1 | tf_op jit(solution)/shard_map/pallas_call | solution.py:520
  171.4 7.9 %all-to-all-done.7 = bf16[16,8,128]{2,1,0:T(8,128)(2,1)S(1)} async-done(((bf16[16,8,128]{2,1,0:T(8,128)(2,1)}), bf16[16,8,128]{2,1,0:T(8,128)(2,1)S(1)}, u32[]{:S(2)}, u32[]{:S(2)}) %all-to-all-start.7) | async-done | bytes 32800 | tf_op jit(solution)/shard_map/all_to_all | solution.py:519
  179.3 0.7 shard_map.244
  180.0 3.7 %shard_map.246 = (f32[344,256]{1,0:T(8,128)}, f32[344,256]{1,0:T(8,128)}) custom-call(bf16[16,2,344,128]{3,2,1,0:T(8,128)(2,1)} %bitcast.29, bf16[2048,256]{1,0:T(8,128)(2,1)S(1)} %shard_map.241.rows_ref), custom_call_target="tpu_custom_call" | custom-call | flops 1000000000 | bytes 1000000 | tf_op jit(solution)/shard_map/pallas_call | solution.py:527
  (15 shorter events, 0.1 us)
Async XLA Ops:
  7.2 89.5 %all-gather.5.cloned.1.call-start = ((), (), s32[]{:S(2)}) async-start(), calls=%async_computation.8 | async-start | bytes 5988352 | tf_op jit(solution)/shard_map/all_gather | solution.py:410
  7.2 34.4 %copy-start.3 = (f32[128]{0:T(128)S(1)}, f32[128]{0:T(128)}, u32[]{:S(2)}) copy-start(f32[128]{0:T(128)} %param.22) | copy-start | bytes 1540
  9.1 27.2 %all-to-all-start = ((bf16[16,8,128]{2,1,0:T(8,128)(2,1)}), bf16[16,8,128]{2,1,0:T(8,128)(2,1)S(1)}, u32[]{:S(2)}, u32[]{:S(2)}) async-start(bf16[16,8,128]{2,1,0:T(8,128)(2,1)} %bitcast.33), calls=%async_computation | async-start | bytes 65536 | tf_op jit(solution)/shard_map/all_to_all | solution.py:411
  38.1 15.1 %all-to-all-start.1 = ((bf16[16,8,128]{2,1,0:T(8,128)(2,1)}), bf16[16,8,128]{2,1,0:T(8,128)(2,1)S(1)}, u32[]{:S(2)}, u32[]{:S(2)}) async-start(bf16[16,8,128]{2,1,0:T(8,128)(2,1)} %bitcast.5), calls=%async_computation.1 | async-start | bytes 65536 | tf_op jit(solution)/shard_map/all_to_all | solution.py:423
  54.4 28.3 %all-to-all-start.2 = ((bf16[32,144,128]{2,1,0:T(8,128)(2,1)}), bf16[32,144,128]{2,1,0:T(8,128)(2,1)S(1)}, u32[]{:S(2)}, u32[]{:S(2)}) async-start(bf16[32,144,128]{2,1,0:T(8,128)(2,1)} %get-tuple-element.77), calls=%async_computation.2 | async-start | bytes 2359296 | tf_op jit(solution)/shard_map/all_to_all | solution.py:431
  65.0 115.0 %all-gather.7.cloned.1.call-start = ((), (), s32[]{:S(2)}) async-start(), calls=%async_computation.9 | async-start | bytes 2994176 | tf_op jit(solution)/shard_map/all_gather | solution.py:463
  113.8 23.6 %copy-start = (bf16[128,128]{1,0:T(8,128)(2,1)S(1)}, bf16[128,128]{1,0:T(8,128)(2,1)}, u32[]{:S(2)}) copy-start(bf16[128,128]{1,0:T(8,128)(2,1)} %query_ref.1) | copy-start | bytes 98308
  113.8 23.6 %copy-start.1 = (bf16[128,128]{1,0:T(8,128)(2,1)S(1)}, bf16[128,128]{1,0:T(8,128)(2,1)}, u32[]{:S(2)}) copy-start(bf16[128,128]{1,0:T(8,128)(2,1)} %gres_ref.1) | copy-start | bytes 98308
  138.3 12.0 %collective-permute-start = (bf16[16,128,128]{2,1,0:T(8,128)(2,1)S(1)}, bf16[16,128,128]{2,1,0:T(8,128)(2,1)S(1)}, u32[]{:S(2)}, u32[]{:S(2)}) collective-permute-start(bf16[16,128,128]{2,1,0:T(8,128)(2,1)S(1)} %slice.4.own_ref), channel_id=1, source_target_pairs={{0,1},{1,0},{2,3},{3,2},{4,5},{5,4},{6,7},{7,6},{8,9},{9,8},{10,11... | collective-permute-start | bytes 1572872 | tf_op jit(solution)/shard_map/ppermute | solution.py:509
  142.0 19.6 %all-to-all-start.6 = ((bf16[16,16,128]{2,1,0:T(8,128)(2,1)}), bf16[16,16,128]{2,1,0:T(8,128)(2,1)S(1)}, u32[]{:S(2)}, u32[]{:S(2)}) async-start(bf16[16,16,128]{2,1,0:T(8,128)(2,1)} %get-tuple-element.86), calls=%async_computation.6 | async-start | bytes 131072 | tf_op jit(solution)/shard_map/all_to_all | solution.py:512
  163.4 15.8 %all-to-all-start.7 = ((bf16[16,8,128]{2,1,0:T(8,128)(2,1)}), bf16[16,8,128]{2,1,0:T(8,128)(2,1)S(1)}, u32[]{:S(2)}, u32[]{:S(2)}) async-start(bf16[16,8,128]{2,1,0:T(8,128)(2,1)} %bitcast.12), calls=%async_computation.7 | async-start | bytes 65536 | tf_op jit(solution)/shard_map/all_to_all | solution.py:519
  167.5 0.7 copy-start.2
Sparse Core Ops, SparseCore 0:
  10.7 85.5 all-gather.4
  101.1 69.6 all-gather.6

commit v5 on v4

--- a/solution.py
+++ b/solution.py
@@ -227,15 +227,17 @@
     ).astype(bf16)
 
 
-def back_kernel(w_ref, hid_ref, extra_ref, sent_ref, w_vmem, sems):
+def back_kernel(w_ref, hid_ref, extra_ref, mine_ref, other_ref, w_vmem, sems):
     arrivals = load_weights(w_ref, w_vmem, sems)
     tokens = hid_ref.shape[2]
-    cores, _, chans = sent_ref.shape
+    chans = mine_ref.shape[1]
     n_ctx, _, hidden, rows = w_ref.shape
     per = rows // chans
+    cores = 2
     terms = n_ctx * per // cores * tokens
-    for core in range(cores):
-        sent_ref[core, terms:] = extra_ref[...]
+    mine_ref[terms:] = extra_ref[...]
+    other_ref[terms:] = extra_ref[...]
+    first = lax.axis_index("ch") % cores == 0
     rest = jnp.zeros((-hidden % 128, tokens), f32)
     d_gate, d_up = (
         jnp.concatenate([hid_ref[half].astype(f32), rest]).T.astype(bf16)[:, :hidden]
@@ -246,22 +248,23 @@
         if i % step == 0:
             for arrival in arrivals[i : i + step]:
                 arrival.wait()
-        term = (dot(d_gate, w_vmem[i, 0]) + dot(d_up, w_vmem[i, 1])).astype(bf16)
-        for k in range(per):
-            pair_at, core = divmod(i * per + k, cores)
-            sent_ref[core, pair_at * tokens : (pair_at + 1) * tokens] = term[
-                :, k * chans : (k + 1) * chans
-            ]
-
-
-def add_kernel(tokens, met_ref, piece_ref, sent_ref):
-    cores, _, chans = met_ref.shape
+        term = dot(d_gate, w_vmem[i, 0]) + dot(d_up, w_vmem[i, 1])
+        for k in range(0, per, cores):
+            even = term[:, k * chans : (k + 1) * chans]
+            odd = term[:, (k + 1) * chans : (k + 2) * chans]
+            start = (i * per + k) // cores * tokens
+            mine_ref[start : start + tokens] = jnp.where(first, even, odd).astype(bf16)
+            other_ref[start : start + tokens] = jnp.where(first, odd, even).astype(bf16)
+
+
+def add_kernel(tokens, mine_ref, theirs_ref, piece_ref, sent_ref):
+    chans = mine_ref.shape[1]
     pairs = sent_ref.shape[0]
     terms = pairs * tokens
     piece = piece_ref[...]
     inner, peak = None, None
-    for core in range(cores):
-        extra = met_ref[core, terms : terms + EXTRA].astype(f32)[:8]
+    for met_ref in (mine_ref, theirs_ref):
+        extra = met_ref[terms : terms + EXTRA].astype(f32)[:8]
         part = extra[0:1] + extra[1:2] + extra[2:3]
         top = extra[3:4] + extra[4:5] + extra[5:6]
         inner = part if inner is None else inner + part
@@ -270,9 +273,8 @@
         split_rows(inner) + split_rows(peak) + [jnp.zeros((EXTRA - 6, chans), f32)]
     ).astype(bf16)
     for q in range(pairs):
-        total = met_ref[0, q * tokens : (q + 1) * tokens].astype(f32)
-        for core in range(1, cores):
-            total = total + met_ref[core, q * tokens : (q + 1) * tokens].astype(f32)
+        rows = slice(q * tokens, (q + 1) * tokens)
+        total = mine_ref[rows].astype(f32) + theirs_ref[rows].astype(f32)
         sent_ref[q, :tokens] = total.astype(bf16)
         sent_ref[q, tokens : tokens + EXTRA] = extra
         sent_ref[q, tokens + EXTRA :] = piece
@@ -464,24 +466,24 @@
     cores = 2
     pairs = n_ch // cores
     piece_rows = n_ctx * share
-    (sent,) = call(
+    mine, theirs = call(
         back_kernel,
-        [((cores, pairs * tokens + EXTRA, chans), bf16)],
+        [((pairs * tokens + EXTRA, chans), bf16)] * 2,
         3,
         in_specs=[HBM, VMEM, VMEM],
         scratch=[pltpu.VMEM(weights, bf16), pltpu.SemaphoreType.DMA((n_ctx,))],
         flops=1e9,
         limit=20,
     )(w_all, d_hid, extra)
-    chip = [[q * cores + core for core in range(cores)] for q in range(pairs)]
+    swap = [(j, j + 1 - 2 * (j % cores)) for j in range(n_ch)]
     plane = [[q * cores + core for q in range(pairs)] for core in range(cores)]
-    met = lax.all_to_all(sent, "ch", 0, 0, tiled=True, axis_index_groups=chip)
+    theirs = lax.ppermute(theirs, "ch", swap)
     (sent,) = call(
         functools.partial(add_kernel, tokens),
         [((pairs, tokens + EXTRA + piece_rows, chans), bf16)],
-        2,
+        3,
         limit=16,
-    )(met, piece)
+    )(mine, theirs, piece)
     back = lax.all_to_all(sent, "ch", 0, 0, tiled=True, axis_index_groups=plane)
     dx, dq, sent, mark = call(
         functools.partial(norm_kernel, chans * n_ch),
@@ -506,7 +508,7 @@
 
     mine, mark = lax.optimization_barrier((back[:, tokens + EXTRA :], mark))
     kept = reload(mark, [fre_far, fim_far, *tables])
-    theirs = lax.ppermute(mine, "ch", [(j, j + 1 - 2 * (j % 2)) for j in range(n_ch)])
+    theirs = lax.ppermute(mine, "ch", swap)
     (row_acts,) = call(rows_kernel, [((length, rows), bf16)], 2)(mine, theirs)
     kept[0], row_acts = lax.optimization_barrier((kept[0], row_acts))
     back = lax.all_to_all(sent, "ctx", 0, 0, tiled=True)

time: 191 us -> 191 us (level)
  blocking collectives: 46.9 us -> 37.6 us
  starting transfers between devices: 44.6 us -> 52.6 us
    all_to_all x1 -> x0, blocking collectives: 9.39 us -> none  [on_device(): met = lax.all_to_all(sent, 'ch', 0, 0, tiled=True, axis_index_groups=chip)]
    ppermute x1 -> x2, starting transfers between devices: 3.71 us -> 10.8 us  [the longest x1 7.12 us: on_device(): theirs = lax.ppermute(theirs, 'ch', swap)]
  transfers between devices with their start and end apart: 8 -> 9, of which waited for: 5 -> 6; matrix products, arithmetic and copies ran while one was open for 0% -> 0% of each run, Pallas kernels for 9% -> 9%
where the time goes in v5:
time: 191 us; the launch traced here: 190 us
  waiting for transfers between devices  57.2 us (30%)
  starting transfers between devices  52.6 us (28%)
  blocking collectives  37.6 us (20%)
  Pallas kernels  27.2 us (14%)
  between operations  14.2 us (7%)
    all_to_all x1, blocking collectives, on_device(): back = lax.all_to_all(sent, 'ch', 0, 0, tiled=True, axis_index_groups=plane)  23.6 us
    all_to_all x1, waiting for transfers between devices, on_device(): met = lax.all_to_all(sent, 'ch', 0, 0, tiled=True)  17.6 us
    all_to_all x1, starting transfers between devices, on_device(): lax.all_to_all(mixed.reshape(n_ctx, own, tokens), 'ctx', 0, 0, tiled=True)  15.8 us
    all_to_all x1, blocking collectives, on_device(): lax.all_to_all(piece, 'ctx', 0, 0, tiled=True)  14 us
    all_to_all x1, waiting for transfers between devices, on_device(): lax.all_to_all(conv.reshape(n_ctx, own, tokens), 'ctx', 0, 0, tiled=True)  11.4 us
    all_to_all x1, starting transfers between devices, on_device(): met = lax.all_to_all(sent, 'ch', 0, 0, tiled=True)  10.6 us
    all_to_all x1, waiting for transfers between devices, on_device(): back = lax.all_to_all(sent, 'ctx', 0, 0, tiled=True)  10 us
    all_to_all x1, waiting for transfers between devices, on_device(): lax.all_to_all(mixed.reshape(n_ctx, own, tokens), 'ctx', 0, 0, tiled=True)  8.92 us
  transfers between devices with their start and end apart: 9, of which 6 were waited for; matrix products, arithmetic and copies ran while one was open for 0% of the time, Pallas kernels for 9%

profile of v5, /device:TPU:1, one launch (start us, length us, event | category | flops | bytes accessed | tf_op | source)
XLA Modules:
  0.0 189.5 jit_solution(1465407560102278413)
XLA Ops:
  7.2 1.8 shard_map.232
  9.1 15.8 %all-to-all-start = ((bf16[16,8,128]{2,1,0:T(8,128)(2,1)}), bf16[16,8,128]{2,1,0:T(8,128)(2,1)S(1)}, u32[]{:S(2)}, u32[]{:S(2)}) async-start(bf16[16,8,128]{2,1,0:T(8,128)(2,1)} %bitcast.33), calls=%async_computation | async-start | bytes 65536 | tf_op jit(solution)/shard_map/all_to_all | solution.py:413
  24.8 2.5 %shard_map.233 = (f32[136,128]{1,0:T(8,128)S(1)}, f32[136,128]{1,0:T(8,128)S(1)}, f32[136,128]{1,0:T(8,128)}, f32[136,128]{1,0:T(8,128)}, bf16[272,128]{1,0:T(8,...) custom-call(f32[8,2048]{1,0:T(8,128)} %filt_ref.1, ...), custom_call_target="tpu_custom_call" | custom-call | flops 1000 | bytes 1 | tf_op jit(solution)/shard_map/pallas_call | solution.py:415
  27.4 8.9 %all-to-all-done = bf16[16,8,128]{2,1,0:T(8,128)(2,1)S(1)} async-done(((bf16[16,8,128]{2,1,0:T(8,128)(2,1)}), bf16[16,8,128]{2,1,0:T(8,128)(2,1)S(1)}, u32[]{:S(2)}, u32[]{:S(2)}) %all-to-all-start) | async-done | bytes 32800 | tf_op jit(solution)/shard_map/all_to_all | solution.py:413
  36.3 1.8 shard_map.234
  38.1 3.5 %all-to-all-start.1 = ((bf16[16,8,128]{2,1,0:T(8,128)(2,1)}), bf16[16,8,128]{2,1,0:T(8,128)(2,1)S(1)}, u32[]{:S(2)}, u32[]{:S(2)}) async-start(bf16[16,8,128]{2,1,0:T(8,128)(2,1)} %bitcast.5), calls=%async_computation.1 | async-start | bytes 65536 | tf_op jit(solution)/shard_map/all_to_all | solution.py:425
  41.6 0.1 copy.29.gain_ref
  41.7 11.4 %all-to-all-done.1 = bf16[16,8,128]{2,1,0:T(8,128)(2,1)S(1)} async-done(((bf16[16,8,128]{2,1,0:T(8,128)(2,1)}), bf16[16,8,128]{2,1,0:T(8,128)(2,1)S(1)}, u32[]{:S(2)}, u32[]{:S(2)}) %all-to-all-start.1) | async-done | bytes 32800 | tf_op jit(solution)/shard_map/all_to_all | solution.py:425
  53.2 1.2 shard_map.235
  54.4 10.6 %all-to-all-start.2 = ((bf16[32,144,128]{2,1,0:T(8,128)(2,1)}), bf16[32,144,128]{2,1,0:T(8,128)(2,1)S(1)}, u32[]{:S(2)}, u32[]{:S(2)}) async-start(bf16[32,144,128]{2,1,0:T(8,128)(2,1)} %get-tuple-element.79), calls=%async_computation.2 | async-start | bytes 2359296 | tf_op jit(solution)/shard_map/all_to_all | solution.py:433
  65.0 17.6 %all-to-all-done.2.met_ref = bf16[32,144,128]{2,1,0:T(8,128)(2,1)S(1)} async-done(((bf16[32,144,128]{2,1,0:T(8,128)(2,1)}), bf16[32,144,128]{2,1,0:T(8,128)(2,1)S(1)}, u32[]{:S(2)}, u32[]{:S(2)}) %all-to-all-start.2) | async-done | bytes 1179680 | tf_op jit(solution)/shard_map/all_to_all | solution.py:433
  82.6 14.0 %all_to_all.35 = bf16[16,8,128]{2,1,0:T(8,128)(2,1)S(1)} all-to-all(bf16[16,8,128]{2,1,0:T(8,128)(2,1)S(1)} %dynamic-slice_bitcast_fusion), channel_id=1, replica_groups=mesh['ctx'=16,'ch'=32] {'ctx'}, dimensions={0} | all-to-all | bytes 65536 | tf_op jit(solution)/shard_map/all_to_all | solution.py:442
  96.6 4.3 %shard_map.236 = (bf16[2,344,128]{2,1,0:T(8,128)(2,1)}, bf16[2,344,128]{2,1,0:T(8,128)(2,1)S(1)}, f32[1,128]{1,0:T(1,128)S(1)}, bf16[16,128]{1,0:T(8,128)(2,1)S(1)}) custom-call(bf16[32,144,128]{2,1,0:T(8,128)(2,1)S(1)} %all-to-all-done.2.met_ref, bf16[16,2,344,256]{3,2,1,0:T(8,128)(2,1)} %bitcast.27, bf16[344,128]{1,0:T(8,128)(2,1)} %bitcast.32, ...), custom_call_target="tpu_custom_call" | custom-call | flops 1000000000 | bytes 1000000 | tf_op jit(solution)/shard_map/pallas_call | solution.py:445
  101.0 3.2 %shard_map.237 = (bf16[2064,128]{1,0:T(8,128)(2,1)S(1)}, bf16[2064,128]{1,0:T(8,128)(2,1)S(1)}) custom-call(bf16[16,2,344,256]{3,2,1,0:T(8,128)(2,1)} %bitcast.28, bf16[2,344,128]{2,1,0:T(8,128)(2,1)S(1)} %get-tuple-element.82.hid_ref, bf16[16,128]{1,0:T(8,128)(2,1)S(1)} %get-tuple-element.83.extra_ref), custom_call_target="tpu_custom_call" | custom-call | flops 1000000000 | bytes 1000000 | tf_op jit(solution)/shard_map/pallas_call | solution.py:469
  104.2 7.1 %collective-permute-start = (bf16[2064,128]{1,0:T(8,128)(2,1)S(1)}, bf16[2064,128]{1,0:T(8,128)(2,1)S(1)}, u32[]{:S(2)}, u32[]{:S(2)}) collective-permute-start(bf16[2064,128]{1,0:T(8,128)(2,1)S(1)} %get-tuple-element.85), channel_id=1, source_target_pairs={{0,1},{1,0},{2,3},{3,2},{4,5},{5,4},{6,7},{7,6},{8,9},{9,8},{10,11... | collective-permute-start | bytes 1585160 | tf_op jit(solution)/shard_map/ppermute | solution.py:480
  111.3 1.5 collective-permute-done.theirs_ref
  112.9 0.2 shard_map.238
  113.1 23.6 %all_to_all.36.back_ref = bf16[16,272,128]{2,1,0:T(8,128)(2,1)S(1)} all-to-all(bf16[16,272,128]{2,1,0:T(8,128)(2,1)S(1)} %shard_map.238), channel_id=1, replica_groups={{0,2,4,6,8,10,12,14,16,18,20,22,24,26,28,30},{1,3,5,7,9,11,13,15,17,19,..., dimensions={0} | all-to-all | bytes 2228224 | tf_op jit(solution)/shard_map/all_to_all | solution.py:487
  136.7 0.9 shard_map.239
  137.6 3.7 %collective-permute-start.1 = (bf16[16,128,128]{2,1,0:T(8,128)(2,1)S(1)}, bf16[16,128,128]{2,1,0:T(8,128)(2,1)S(1)}, u32[]{:S(2)}, u32[]{:S(2)}) collective-permute-start(bf16[16,128,128]{2,1,0:T(8,128)(2,1)S(1)} %slice.4.own_ref), channel_id=1, source_target_pairs={{0,1},{1,0},{2,3},{3,2},{4,5},{5,4},{6,7},{7,6},{8,9},{9,8},{10,11... | collective-permute-start | bytes 1572872 | tf_op jit(solution)/shard_map/ppermute | solution.py:511
  141.3 7.0 %all-to-all-start.5 = ((bf16[16,16,128]{2,1,0:T(8,128)(2,1)}), bf16[16,16,128]{2,1,0:T(8,128)(2,1)S(1)}, u32[]{:S(2)}, u32[]{:S(2)}) async-start(bf16[16,16,128]{2,1,0:T(8,128)(2,1)} %get-tuple-element.90), calls=%async_computation.5 | async-start | bytes 131072 | tf_op jit(solution)/shard_map/all_to_all | solution.py:514
  148.3 1.3 shard_map.240
  149.6 0.4 shard_map.241.rows_ref
  150.0 10.0 %all-to-all-done.5.back_ref = bf16[16,16,128]{2,1,0:T(8,128)(2,1)S(1)} async-done(((bf16[16,16,128]{2,1,0:T(8,128)(2,1)}), bf16[16,16,128]{2,1,0:T(8,128)(2,1)S(1)}, u32[]{:S(2)}, u32[]{:S(2)}) %all-to-all-start.5) | async-done | bytes 65568 | tf_op jit(solution)/shard_map/all_to_all | solution.py:514
  160.0 1.8 shard_map.242
  161.8 4.9 %all-to-all-start.6 = ((bf16[16,8,128]{2,1,0:T(8,128)(2,1)}), bf16[16,8,128]{2,1,0:T(8,128)(2,1)S(1)}, u32[]{:S(2)}, u32[]{:S(2)}) async-start(bf16[16,8,128]{2,1,0:T(8,128)(2,1)} %bitcast.12), calls=%async_computation.6 | async-start | bytes 65536 | tf_op jit(solution)/shard_map/all_to_all | solution.py:521
  166.7 0.6 copy-done.2
  167.3 0.8 shard_map.243
  168.1 2.5 %shard_map.245 = f32[8,2048]{1,0:T(8,128)} custom-call(f32[136,128]{1,0:T(8,128)} %get-tuple-element.112.gre_ref, f32[136,128]{1,0:T(8,128)} %get-tuple-element.113.gim_ref, f32[136,128]{1,0:T(8,128)} %get-tuple-element.114.sre_ref, f32[136,128]{1,0:T(8,128)} %get-tuple-element.115.sim_ref, bf16[272,128]{1,0:T(8,128)(2,1)} %constant.51.clone.refs_0_.refs_2_, ...), custom_call_target="tpu_custom_call" | custom-call | flops 1000 | bytes 1 | tf_op jit(solution)/shard_map/pallas_call | solution.py:522
  170.6 7.6 %all-to-all-done.6 = bf16[16,8,128]{2,1,0:T(8,128)(2,1)S(1)} async-done(((bf16[16,8,128]{2,1,0:T(8,128)(2,1)}), bf16[16,8,128]{2,1,0:T(8,128)(2,1)S(1)}, u32[]{:S(2)}, u32[]{:S(2)}) %all-to-all-start.6) | async-done | bytes 32800 | tf_op jit(solution)/shard_map/all_to_all | solution.py:521
  178.2 0.7 shard_map.244
  178.9 3.7 %shard_map.246 = (f32[344,256]{1,0:T(8,128)}, f32[344,256]{1,0:T(8,128)}) custom-call(bf16[16,2,344,128]{3,2,1,0:T(8,128)(2,1)} %bitcast.29, bf16[2048,256]{1,0:T(8,128)(2,1)S(1)} %shard_map.241.rows_ref), custom_call_target="tpu_custom_call" | custom-call | flops 1000000000 | bytes 1000000 | tf_op jit(solution)/shard_map/pallas_call | solution.py:529
  (16 shorter events, 0.2 us)
Async XLA Ops:
  7.2 89.5 %all-gather.5.cloned.1.call-start = ((), (), s32[]{:S(2)}) async-start(), calls=%async_computation.7 | async-start | bytes 5988352 | tf_op jit(solution)/shard_map/all_gather | solution.py:412
  7.2 34.4 %copy-start.3 = (f32[128]{0:T(128)S(1)}, f32[128]{0:T(128)}, u32[]{:S(2)}) copy-start(f32[128]{0:T(128)} %param.22) | copy-start | bytes 1540
  9.1 27.2 %all-to-all-start = ((bf16[16,8,128]{2,1,0:T(8,128)(2,1)}), bf16[16,8,128]{2,1,0:T(8,128)(2,1)S(1)}, u32[]{:S(2)}, u32[]{:S(2)}) async-start(bf16[16,8,128]{2,1,0:T(8,128)(2,1)} %bitcast.33), calls=%async_computation | async-start | bytes 65536 | tf_op jit(solution)/shard_map/all_to_all | solution.py:413
  38.1 15.1 %all-to-all-start.1 = ((bf16[16,8,128]{2,1,0:T(8,128)(2,1)}), bf16[16,8,128]{2,1,0:T(8,128)(2,1)S(1)}, u32[]{:S(2)}, u32[]{:S(2)}) async-start(bf16[16,8,128]{2,1,0:T(8,128)(2,1)} %bitcast.5), calls=%async_computation.1 | async-start | bytes 65536 | tf_op jit(solution)/shard_map/all_to_all | solution.py:425
  54.4 28.3 %all-to-all-start.2 = ((bf16[32,144,128]{2,1,0:T(8,128)(2,1)}), bf16[32,144,128]{2,1,0:T(8,128)(2,1)S(1)}, u32[]{:S(2)}, u32[]{:S(2)}) async-start(bf16[32,144,128]{2,1,0:T(8,128)(2,1)} %get-tuple-element.79), calls=%async_computation.2 | async-start | bytes 2359296 | tf_op jit(solution)/shard_map/all_to_all | solution.py:433
  65.0 114.0 %all-gather.7.cloned.1.call-start = ((), (), s32[]{:S(2)}) async-start(), calls=%async_computation.8 | async-start | bytes 2994176 | tf_op jit(solution)/shard_map/all_gather | solution.py:465
  104.2 8.6 %collective-permute-start = (bf16[2064,128]{1,0:T(8,128)(2,1)S(1)}, bf16[2064,128]{1,0:T(8,128)(2,1)S(1)}, u32[]{:S(2)}, u32[]{:S(2)}) collective-permute-start(bf16[2064,128]{1,0:T(8,128)(2,1)S(1)} %get-tuple-element.85), channel_id=1, source_target_pairs={{0,1},{1,0},{2,3},{3,2},{4,5},{5,4},{6,7},{7,6},{8,9},{9,8},{10,11... | collective-permute-start | bytes 1585160 | tf_op jit(solution)/shard_map/ppermute | solution.py:480
  113.1 23.6 %copy-start = (bf16[128,128]{1,0:T(8,128)(2,1)S(1)}, bf16[128,128]{1,0:T(8,128)(2,1)}, u32[]{:S(2)}) copy-start(bf16[128,128]{1,0:T(8,128)(2,1)} %query_ref.1) | copy-start | bytes 98308
  113.1 23.6 %copy-start.1 = (bf16[128,128]{1,0:T(8,128)(2,1)S(1)}, bf16[128,128]{1,0:T(8,128)(2,1)}, u32[]{:S(2)}) copy-start(bf16[128,128]{1,0:T(8,128)(2,1)} %gres_ref.1) | copy-start | bytes 98308
  137.6 12.0 %collective-permute-start.1 = (bf16[16,128,128]{2,1,0:T(8,128)(2,1)S(1)}, bf16[16,128,128]{2,1,0:T(8,128)(2,1)S(1)}, u32[]{:S(2)}, u32[]{:S(2)}) collective-permute-start(bf16[16,128,128]{2,1,0:T(8,128)(2,1)S(1)} %slice.4.own_ref), channel_id=1, source_target_pairs={{0,1},{1,0},{2,3},{3,2},{4,5},{5,4},{6,7},{7,6},{8,9},{9,8},{10,11... | collective-permute-start | bytes 1572872 | tf_op jit(solution)/shard_map/ppermute | solution.py:511
  141.3 18.7 %all-to-all-start.5 = ((bf16[16,16,128]{2,1,0:T(8,128)(2,1)}), bf16[16,16,128]{2,1,0:T(8,128)(2,1)S(1)}, u32[]{:S(2)}, u32[]{:S(2)}) async-start(bf16[16,16,128]{2,1,0:T(8,128)(2,1)} %get-tuple-element.90), calls=%async_computation.5 | async-start | bytes 131072 | tf_op jit(solution)/shard_map/all_to_all | solution.py:514
  161.8 16.4 %all-to-all-start.6 = ((bf16[16,8,128]{2,1,0:T(8,128)(2,1)}), bf16[16,8,128]{2,1,0:T(8,128)(2,1)S(1)}, u32[]{:S(2)}, u32[]{:S(2)}) async-start(bf16[16,8,128]{2,1,0:T(8,128)(2,1)} %bitcast.12), calls=%async_computation.6 | async-start | bytes 65536 | tf_op jit(solution)/shard_map/all_to_all | solution.py:521
  166.7 0.7 copy-start.2
Sparse Core Ops, SparseCore 0:
  10.7 85.5 all-gather.4
  101.1 69.7 all-gather.6

commit v6 on v5

--- a/solution.py
+++ b/solution.py
@@ -363,15 +363,15 @@
         out_ref[:, a * lanes : (a + 1) * lanes] = grad[a * own : (a + 1) * own]
 
 
-def products_kernel(ds_ref, key_ref, value_ref, dk_ref, dv_ref):
+def weight_kernel(
+    d_ref, rows_ref, ds_ref, key_ref, value_ref, first_ref, second_ref, dk_ref, dv_ref, d_vmem, out_vmem, sems, out_sems
+):
+    n_ctx, _, _, tokens = d_ref.shape
+    copies = load_weights(d_ref, d_vmem, sems)
     grad = ds_ref[...].astype(f32).T
     dk_ref[...] = (grad * value_ref[...].astype(f32)).astype(bf16)
     dv_ref[...] = (grad * key_ref[...].astype(f32)).astype(bf16)
-
-
-def weight_kernel(d_ref, rows_ref, first_ref, second_ref, d_vmem, out_vmem, sems, out_sems):
-    n_ctx, _, _, tokens = d_ref.shape
-    for copy in load_weights(d_ref, d_vmem, sems):
+    for copy in copies:
         copy.wait()
     stores = []
     for half, out_ref in enumerate((first_ref, second_ref)):
@@ -523,15 +523,12 @@
         *(in_hbm(array) for array in (gre, gim, sre, sim)), *tables
     )
     key_near, value_near = reload(dgain, [key_in, value_in])
-    dk, dv = call(products_kernel, [((tokens, chans), bf16)] * 2, 3)(
-        ds.reshape(chans, tokens), key_near, value_near
-    )
-    first, second = call(
+    first, second, dk, dv = call(
         weight_kernel,
-        [((hidden, rows), f32)] * 2,
-        2,
-        in_specs=[HBM, VMEM],
-        out_specs=[HBM, HBM],
+        [((hidden, rows), f32)] * 2 + [((tokens, chans), bf16)] * 2,
+        5,
+        in_specs=[HBM] + [VMEM] * 4,
+        out_specs=[HBM, HBM, VMEM, VMEM],
         scratch=[
             pltpu.VMEM((n_ctx, 2, hidden, tokens), bf16),
             pltpu.VMEM((2, hidden, rows), f32),
@@ -541,7 +538,7 @@
         hbm=(0, 1),
         flops=1e9,
         limit=16,
-    )(d_all, row_acts)
+    )(d_all, row_acts, ds.reshape(chans, tokens), key_near, value_near)
     return (dx, dq, dk, dv, dfilt, dgain[0], first.T, second.T, amax[0, 0])
 
 

time: 191 us -> 192 us (level)
    pallas_call x2 -> x1, Pallas kernels: 4.45 us -> 4.36 us  [on_device(): call(weight_kernel, [((hidden, rows), f32)] * 2 + [((tokens, chans), bf16...]
where the time goes in v6:
time: 192 us; the launch traced here: 189 us
  waiting for transfers between devices  57.2 us (30%)
  starting transfers between devices  52.6 us (27%)
  blocking collectives  37.6 us (20%)
  Pallas kernels  27.1 us (14%)
  between operations  14.2 us (7%)
    all_to_all x1, blocking collectives, on_device(): back = lax.all_to_all(sent, 'ch', 0, 0, tiled=True, axis_index_groups=plane)  23.6 us
    all_to_all x1, waiting for transfers between devices, on_device(): met = lax.all_to_all(sent, 'ch', 0, 0, tiled=True)  17.6 us
    all_to_all x1, starting transfers between devices, on_device(): lax.all_to_all(mixed.reshape(n_ctx, own, tokens), 'ctx', 0, 0, tiled=True)  15.8 us
    all_to_all x1, blocking collectives, on_device(): lax.all_to_all(piece, 'ctx', 0, 0, tiled=True)  14 us
    all_to_all x1, waiting for transfers between devices, on_device(): lax.all_to_all(conv.reshape(n_ctx, own, tokens), 'ctx', 0, 0, tiled=True)  11.4 us
    all_to_all x1, starting transfers between devices, on_device(): met = lax.all_to_all(sent, 'ch', 0, 0, tiled=True)  10.6 us
    all_to_all x1, waiting for transfers between devices, on_device(): back = lax.all_to_all(sent, 'ctx', 0, 0, tiled=True)  10 us
    all_to_all x1, waiting for transfers between devices, on_device(): lax.all_to_all(mixed.reshape(n_ctx, own, tokens), 'ctx', 0, 0, tiled=True)  8.92 us
  transfers between devices with their start and end apart: 9, of which 6 were waited for; matrix products, arithmetic and copies ran while one was open for 0% of the time, Pallas kernels for 9%

profile of v6, /device:TPU:1, one launch (start us, length us, event | category | flops | bytes accessed | tf_op | source)
XLA Modules:
  0.0 189.4 jit_solution(1748634470406801335)
XLA Ops:
  7.2 1.8 shard_map.232
  9.1 15.8 %all-to-all-start = ((bf16[16,8,128]{2,1,0:T(8,128)(2,1)}), bf16[16,8,128]{2,1,0:T(8,128)(2,1)S(1)}, u32[]{:S(2)}, u32[]{:S(2)}) async-start(bf16[16,8,128]{2,1,0:T(8,128)(2,1)} %bitcast.33), calls=%async_computation | async-start | bytes 65536 | tf_op jit(solution)/shard_map/all_to_all | solution.py:413
  24.8 2.5 %shard_map.233 = (f32[136,128]{1,0:T(8,128)S(1)}, f32[136,128]{1,0:T(8,128)S(1)}, f32[136,128]{1,0:T(8,128)}, f32[136,128]{1,0:T(8,128)}, bf16[272,128]{1,0:T(8,...) custom-call(f32[8,2048]{1,0:T(8,128)} %filt_ref.1, ...), custom_call_target="tpu_custom_call" | custom-call | flops 1000 | bytes 1 | tf_op jit(solution)/shard_map/pallas_call | solution.py:415
  27.4 8.9 %all-to-all-done = bf16[16,8,128]{2,1,0:T(8,128)(2,1)S(1)} async-done(((bf16[16,8,128]{2,1,0:T(8,128)(2,1)}), bf16[16,8,128]{2,1,0:T(8,128)(2,1)S(1)}, u32[]{:S(2)}, u32[]{:S(2)}) %all-to-all-start) | async-done | bytes 32800 | tf_op jit(solution)/shard_map/all_to_all | solution.py:413
  36.3 1.8 shard_map.234
  38.1 3.5 %all-to-all-start.1 = ((bf16[16,8,128]{2,1,0:T(8,128)(2,1)}), bf16[16,8,128]{2,1,0:T(8,128)(2,1)S(1)}, u32[]{:S(2)}, u32[]{:S(2)}) async-start(bf16[16,8,128]{2,1,0:T(8,128)(2,1)} %bitcast.5), calls=%async_computation.1 | async-start | bytes 65536 | tf_op jit(solution)/shard_map/all_to_all | solution.py:425
  41.6 0.1 copy.29.gain_ref
  41.7 11.4 %all-to-all-done.1 = bf16[16,8,128]{2,1,0:T(8,128)(2,1)S(1)} async-done(((bf16[16,8,128]{2,1,0:T(8,128)(2,1)}), bf16[16,8,128]{2,1,0:T(8,128)(2,1)S(1)}, u32[]{:S(2)}, u32[]{:S(2)}) %all-to-all-start.1) | async-done | bytes 32800 | tf_op jit(solution)/shard_map/all_to_all | solution.py:425
  53.2 1.2 shard_map.235
  54.4 10.6 %all-to-all-start.2 = ((bf16[32,144,128]{2,1,0:T(8,128)(2,1)}), bf16[32,144,128]{2,1,0:T(8,128)(2,1)S(1)}, u32[]{:S(2)}, u32[]{:S(2)}) async-start(bf16[32,144,128]{2,1,0:T(8,128)(2,1)} %get-tuple-element.79), calls=%async_computation.2 | async-start | bytes 2359296 | tf_op jit(solution)/shard_map/all_to_all | solution.py:433
  65.0 0.0 all-gather.7.cloned.1.call-start
  65.0 17.6 %all-to-all-done.2.met_ref = bf16[32,144,128]{2,1,0:T(8,128)(2,1)S(1)} async-done(((bf16[32,144,128]{2,1,0:T(8,128)(2,1)}), bf16[32,144,128]{2,1,0:T(8,128)(2,1)S(1)}, u32[]{:S(2)}, u32[]{:S(2)}) %all-to-all-start.2) | async-done | bytes 1179680 | tf_op jit(solution)/shard_map/all_to_all | solution.py:433
  82.6 14.0 %all_to_all.35 = bf16[16,8,128]{2,1,0:T(8,128)(2,1)S(1)} all-to-all(bf16[16,8,128]{2,1,0:T(8,128)(2,1)S(1)} %dynamic-slice_bitcast_fusion), channel_id=1, replica_groups=mesh['ctx'=16,'ch'=32] {'ctx'}, dimensions={0} | all-to-all | bytes 65536 | tf_op jit(solution)/shard_map/all_to_all | solution.py:442
  96.6 4.3 %shard_map.236 = (bf16[2,344,128]{2,1,0:T(8,128)(2,1)}, bf16[2,344,128]{2,1,0:T(8,128)(2,1)S(1)}, f32[1,128]{1,0:T(1,128)S(1)}, bf16[16,128]{1,0:T(8,128)(2,1)S(1)}) custom-call(bf16[32,144,128]{2,1,0:T(8,128)(2,1)S(1)} %all-to-all-done.2.met_ref, bf16[16,2,344,256]{3,2,1,0:T(8,128)(2,1)} %bitcast.27, bf16[344,128]{1,0:T(8,128)(2,1)} %bitcast.32, ...), custom_call_target="tpu_custom_call" | custom-call | flops 1000000000 | bytes 1000000 | tf_op jit(solution)/shard_map/pallas_call | solution.py:445
  101.0 3.2 %shard_map.237 = (bf16[2064,128]{1,0:T(8,128)(2,1)S(1)}, bf16[2064,128]{1,0:T(8,128)(2,1)S(1)}) custom-call(bf16[16,2,344,256]{3,2,1,0:T(8,128)(2,1)} %bitcast.28, bf16[2,344,128]{2,1,0:T(8,128)(2,1)S(1)} %get-tuple-element.82.hid_ref, bf16[16,128]{1,0:T(8,128)(2,1)S(1)} %get-tuple-element.83.extra_ref), custom_call_target="tpu_custom_call" | custom-call | flops 1000000000 | bytes 1000000 | tf_op jit(solution)/shard_map/pallas_call | solution.py:469
  104.2 7.1 %collective-permute-start = (bf16[2064,128]{1,0:T(8,128)(2,1)S(1)}, bf16[2064,128]{1,0:T(8,128)(2,1)S(1)}, u32[]{:S(2)}, u32[]{:S(2)}) collective-permute-start(bf16[2064,128]{1,0:T(8,128)(2,1)S(1)} %get-tuple-element.85), channel_id=1, source_target_pairs={{0,1},{1,0},{2,3},{3,2},{4,5},{5,4},{6,7},{7,6},{8,9},{9,8},{10,11... | collective-permute-start | bytes 1585160 | tf_op jit(solution)/shard_map/ppermute | solution.py:480
  111.3 1.5 collective-permute-done.theirs_ref
  112.9 0.2 shard_map.238
  113.1 23.6 %all_to_all.36.back_ref = bf16[16,272,128]{2,1,0:T(8,128)(2,1)S(1)} all-to-all(bf16[16,272,128]{2,1,0:T(8,128)(2,1)S(1)} %shard_map.238), channel_id=1, replica_groups={{0,2,4,6,8,10,12,14,16,18,20,22,24,26,28,30},{1,3,5,7,9,11,13,15,17,19,..., dimensions={0} | all-to-all | bytes 2228224 | tf_op jit(solution)/shard_map/all_to_all | solution.py:487
  136.7 0.9 shard_map.239
  137.6 3.7 %collective-permute-start.1 = (bf16[16,128,128]{2,1,0:T(8,128)(2,1)S(1)}, bf16[16,128,128]{2,1,0:T(8,128)(2,1)S(1)}, u32[]{:S(2)}, u32[]{:S(2)}) collective-permute-start(bf16[16,128,128]{2,1,0:T(8,128)(2,1)S(1)} %slice.4.own_ref), channel_id=1, source_target_pairs={{0,1},{1,0},{2,3},{3,2},{4,5},{5,4},{6,7},{7,6},{8,9},{9,8},{10,11... | collective-permute-start | bytes 1572872 | tf_op jit(solution)/shard_map/ppermute | solution.py:511
  141.3 7.0 %all-to-all-start.5 = ((bf16[16,16,128]{2,1,0:T(8,128)(2,1)}), bf16[16,16,128]{2,1,0:T(8,128)(2,1)S(1)}, u32[]{:S(2)}, u32[]{:S(2)}) async-start(bf16[16,16,128]{2,1,0:T(8,128)(2,1)} %get-tuple-element.98), calls=%async_computation.5 | async-start | bytes 131072 | tf_op jit(solution)/shard_map/all_to_all | solution.py:514
  148.3 1.3 shard_map.240
  149.6 0.4 shard_map.241.rows_ref
  150.0 10.0 %all-to-all-done.5.back_ref = bf16[16,16,128]{2,1,0:T(8,128)(2,1)S(1)} async-done(((bf16[16,16,128]{2,1,0:T(8,128)(2,1)}), bf16[16,16,128]{2,1,0:T(8,128)(2,1)S(1)}, u32[]{:S(2)}, u32[]{:S(2)}) %all-to-all-start.5) | async-done | bytes 65568 | tf_op jit(solution)/shard_map/all_to_all | solution.py:514
  160.0 1.8 shard_map.242
  161.8 4.9 %all-to-all-start.6 = ((bf16[16,8,128]{2,1,0:T(8,128)(2,1)}), bf16[16,8,128]{2,1,0:T(8,128)(2,1)S(1)}, u32[]{:S(2)}, u32[]{:S(2)}) async-start(bf16[16,8,128]{2,1,0:T(8,128)(2,1)} %bitcast.13), calls=%async_computation.6 | async-start | bytes 65536 | tf_op jit(solution)/shard_map/all_to_all | solution.py:521
  166.7 0.6 copy-done.2
  167.3 0.8 shard_map.243
  168.1 2.5 %shard_map.245 = f32[8,2048]{1,0:T(8,128)} custom-call(f32[136,128]{1,0:T(8,128)} %get-tuple-element.114.gre_ref, f32[136,128]{1,0:T(8,128)} %get-tuple-element.115.gim_ref, f32[136,128]{1,0:T(8,128)} %get-tuple-element.116.sre_ref, f32[136,128]{1,0:T(8,128)} %get-tuple-element.117.sim_ref, bf16[272,128]{1,0:T(8,128)(2,1)} %constant.51.clone.refs_0_.refs_2_, ...), custom_call_target="tpu_custom_call" | custom-call | flops 1000 | bytes 1 | tf_op jit(solution)/shard_map/pallas_call | solution.py:522
  170.6 7.6 %all-to-all-done.6 = bf16[16,8,128]{2,1,0:T(8,128)(2,1)S(1)} async-done(((bf16[16,8,128]{2,1,0:T(8,128)(2,1)}), bf16[16,8,128]{2,1,0:T(8,128)(2,1)S(1)}, u32[]{:S(2)}, u32[]{:S(2)}) %all-to-all-start.6) | async-done | bytes 32800 | tf_op jit(solution)/shard_map/all_to_all | solution.py:521
  178.2 4.4 %shard_map.244 = (f32[344,256]{1,0:T(8,128)}, f32[344,256]{1,0:T(8,128)}, bf16[128,128]{1,0:T(8,128)(2,1)}, bf16[128,128]{1,0:T(8,128)(2,1)}) custom-call(bf16[16,2,344,128]{3,2,1,0:T(8,128)(2,1)} %bitcast.29, bf16[2048,256]{1,0:T(8,128)(2,1)S(1)} %shard_map.241.rows_ref, bf16[128,128]{1,0:T(8,128)(2,1)S(1)} %bitcast.23, ...), custom_call_target="tpu_custom_call" | custom-call | flops 1000000000 | bytes 1000000 | tf_op jit(solution)/shard_map/pallas_call | solution.py:526
  (15 shorter events, 0.1 us)
Async XLA Ops:
  7.2 89.5 %all-gather.5.cloned.1.call-start = ((), (), s32[]{:S(2)}) async-start(), calls=%async_computation.7 | async-start | bytes 5988352 | tf_op jit(solution)/shard_map/all_gather | solution.py:412
  7.2 34.4 %copy-start.3 = (f32[128]{0:T(128)S(1)}, f32[128]{0:T(128)}, u32[]{:S(2)}) copy-start(f32[128]{0:T(128)} %param.22) | copy-start | bytes 1540
  9.1 27.2 %all-to-all-start = ((bf16[16,8,128]{2,1,0:T(8,128)(2,1)}), bf16[16,8,128]{2,1,0:T(8,128)(2,1)S(1)}, u32[]{:S(2)}, u32[]{:S(2)}) async-start(bf16[16,8,128]{2,1,0:T(8,128)(2,1)} %bitcast.33), calls=%async_computation | async-start | bytes 65536 | tf_op jit(solution)/shard_map/all_to_all | solution.py:413
  38.1 15.1 %all-to-all-start.1 = ((bf16[16,8,128]{2,1,0:T(8,128)(2,1)}), bf16[16,8,128]{2,1,0:T(8,128)(2,1)S(1)}, u32[]{:S(2)}, u32[]{:S(2)}) async-start(bf16[16,8,128]{2,1,0:T(8,128)(2,1)} %bitcast.5), calls=%async_computation.1 | async-start | bytes 65536 | tf_op jit(solution)/shard_map/all_to_all | solution.py:425
  54.4 28.3 %all-to-all-start.2 = ((bf16[32,144,128]{2,1,0:T(8,128)(2,1)}), bf16[32,144,128]{2,1,0:T(8,128)(2,1)S(1)}, u32[]{:S(2)}, u32[]{:S(2)}) async-start(bf16[32,144,128]{2,1,0:T(8,128)(2,1)} %get-tuple-element.79), calls=%async_computation.2 | async-start | bytes 2359296 | tf_op jit(solution)/shard_map/all_to_all | solution.py:433
  65.0 113.2 %all-gather.7.cloned.1.call-start = ((), (), s32[]{:S(2)}) async-start(), calls=%async_computation.8 | async-start | bytes 2994176 | tf_op jit(solution)/shard_map/all_gather | solution.py:465
  104.2 8.6 %collective-permute-start = (bf16[2064,128]{1,0:T(8,128)(2,1)S(1)}, bf16[2064,128]{1,0:T(8,128)(2,1)S(1)}, u32[]{:S(2)}, u32[]{:S(2)}) collective-permute-start(bf16[2064,128]{1,0:T(8,128)(2,1)S(1)} %get-tuple-element.85), channel_id=1, source_target_pairs={{0,1},{1,0},{2,3},{3,2},{4,5},{5,4},{6,7},{7,6},{8,9},{9,8},{10,11... | collective-permute-start | bytes 1585160 | tf_op jit(solution)/shard_map/ppermute | solution.py:480
  113.1 23.6 %copy-start = (bf16[128,128]{1,0:T(8,128)(2,1)S(1)}, bf16[128,128]{1,0:T(8,128)(2,1)}, u32[]{:S(2)}) copy-start(bf16[128,128]{1,0:T(8,128)(2,1)} %query_ref.1) | copy-start | bytes 98308
  113.1 23.6 %copy-start.1 = (bf16[128,128]{1,0:T(8,128)(2,1)S(1)}, bf16[128,128]{1,0:T(8,128)(2,1)}, u32[]{:S(2)}) copy-start(bf16[128,128]{1,0:T(8,128)(2,1)} %gres_ref.1) | copy-start | bytes 98308
  137.6 12.0 %collective-permute-start.1 = (bf16[16,128,128]{2,1,0:T(8,128)(2,1)S(1)}, bf16[16,128,128]{2,1,0:T(8,128)(2,1)S(1)}, u32[]{:S(2)}, u32[]{:S(2)}) collective-permute-start(bf16[16,128,128]{2,1,0:T(8,128)(2,1)S(1)} %slice.4.own_ref), channel_id=1, source_target_pairs={{0,1},{1,0},{2,3},{3,2},{4,5},{5,4},{6,7},{7,6},{8,9},{9,8},{10,11... | collective-permute-start | bytes 1572872 | tf_op jit(solution)/shard_map/ppermute | solution.py:511
  141.3 18.7 %all-to-all-start.5 = ((bf16[16,16,128]{2,1,0:T(8,128)(2,1)}), bf16[16,16,128]{2,1,0:T(8,128)(2,1)S(1)}, u32[]{:S(2)}, u32[]{:S(2)}) async-start(bf16[16,16,128]{2,1,0:T(8,128)(2,1)} %get-tuple-element.98), calls=%async_computation.5 | async-start | bytes 131072 | tf_op jit(solution)/shard_map/all_to_all | solution.py:514
  161.8 16.4 %all-to-all-start.6 = ((bf16[16,8,128]{2,1,0:T(8,128)(2,1)}), bf16[16,8,128]{2,1,0:T(8,128)(2,1)S(1)}, u32[]{:S(2)}, u32[]{:S(2)}) async-start(bf16[16,8,128]{2,1,0:T(8,128)(2,1)} %bitcast.13), calls=%async_computation.6 | async-start | bytes 65536 | tf_op jit(solution)/shard_map/all_to_all | solution.py:521
  166.7 0.7 copy-start.2
Sparse Core Ops, SparseCore 0:
  10.7 85.5 all-gather.4
  101.1 69.7 all-gather.6
